TPU v7x, 128 devices: a whole 4x4x4 slice. The times are simulated.
128 devices in a mesh: leaf: 16 (over z, y), blk: 8 (over x, core).
Axes of the slice: x: 4, y: 4, z: 4, core: 2. Of those that a mesh axis runs over, the one named last changes fastest.
Arguments:
- loads: float32 [3, 16384, 128], P(None, ('leaf', 'blk')), may hold values from -6 to 6
- inverse_root: bfloat16 [16, 8, 2048, 1024], P('leaf', 'blk'), as said below
- inverse_middle: bfloat16 [16, 8, 1024, 1024], P('leaf', 'blk'), as said below
- inverse_lower: bfloat16 [16, 8, 512, 1024], P('leaf', 'blk'), as said below
- couple_middle: bfloat16 [16384, 8192], P(('leaf', 'blk')), may hold values from -0.0625 to 0.0625
- couple_lower: bfloat16 [16384, 4096], P(('leaf', 'blk')), may hold values from -0.09375 to 0.09375
- couple_between: bfloat16 [16384, 4096], P(('leaf', 'blk')), may hold values from -0.09375 to 0.09375
- pattern_middle: int32 [2, 64], replicated, may hold values from 0 to 127, as said below
- pattern_lower: int32 [4, 32], replicated, may hold values from 0 to 127, as said below
- pattern_between: int32 [4, 32], replicated, may hold values from 0 to 63, as said below
- node_blocks: int32 [7], replicated, may hold values from 16 to 128, as said below
Outputs:
- forward: bfloat16 [3, 16384, 128], P(None, ('leaf', 'blk'))
- solution: bfloat16 [3, 16384, 128], P(None, ('leaf', 'blk'))
Inputs may be any that keep to these rules, and one draw needn't show every extreme that they name: `inverse_root`: each M_(k,n) is lower triangular, with diagonal entries between 1 and 4. `inverse_middle`: each M_(k,n) is lower triangular, with diagonal entries between 1 and 4. `inverse_lower`: each M_(k,n) is lower triangular, with diagonal entries between 1 and 4. `pattern_middle`: each row holds distinct block numbers of the ancestor node, among them its first and its last block. `pattern_lower`: each row holds distinct block numbers of the ancestor node, among them its first and its last block. `pattern_between`: each row holds distinct block numbers of the ancestor node, among them its first and its last block. `node_blocks`: entry 2**k - 1 + n counts the live blocks of node n of level k: between half and all of its (16 >> k) * 8 blocks. The root's blocks are all live; on levels 1 and 2 some node has all its blocks live and some node exactly half.
All inputs are finite; a program needn't handle non-finite values.
Results may differ from a plain program's by a relative error of at most 0.029.
Values may be sent and summed in bfloat16 or wider, within the bound.
No kernel may reach another device: no remote copies, remote signals or barrier semaphores. Data moves between devices by JAX's collectives and lax.ppermute only.
A program may use at most 128 MiB of HBM per device.

v0:
```python
import jax
import jax.numpy as jnp
from jax import lax
from jax.sharding import PartitionSpec as P


def swapped(x, axis, stride):
    return lax.ppermute(x, axis, [(i, i ^ 1 << stride) for i in range(lax.axis_size(axis))])


def shards(
    loads,
    inverse_root,
    inverse_middle,
    inverse_lower,
    couple_middle,
    couple_lower,
    couple_between,
    pattern_middle,
    pattern_lower,
    pattern_between,
    node_blocks,
):
    leaf_count = lax.axis_size("leaf")
    block_count = lax.axis_size("blk")
    tree_depth = leaf_count.bit_length() - 1
    leaf_index = lax.axis_index("leaf")
    block_index = lax.axis_index("blk")
    block_rows = loads.shape[1]
    load_count = loads.shape[2]
    root_total = leaf_count * block_count

    def level_bits(tree_level):
        return tree_depth - tree_level

    def node_of(tree_level):
        return leaf_index >> level_bits(tree_level)

    def live_of(tree_level):
        group_size = leaf_count >> tree_level
        position = (leaf_index & group_size - 1) * block_count + block_index
        limit = node_blocks[2**tree_level - 1 + node_of(tree_level)]
        return (position < limit).astype(jnp.float32)

    def halve(partial_value, bit_total):
        for bit_level in reversed(range(bit_total)):
            paired = partial_value.reshape(
                (2, partial_value.shape[0] // 2) + partial_value.shape[1:]
            )
            upper_half = leaf_index >> bit_level & 1 == 1
            retained = jnp.where(upper_half, paired[1], paired[0])
            outgoing = jnp.where(upper_half, paired[0], paired[1])
            partial_value = retained + swapped(
                outgoing.astype(jnp.bfloat16), "leaf", bit_level
            ).astype(outgoing.dtype)
        return partial_value[0]

    def double(segment, bit_total):
        for bit_level in range(bit_total):
            partner = swapped(segment, "leaf", bit_level)
            upper_half = leaf_index >> bit_level & 1 == 1
            segment = jnp.where(
                upper_half,
                jnp.concatenate([partner, segment], 0),
                jnp.concatenate([segment, partner], 0),
            )
        return segment

    def columns_of(block_values):
        return lax.all_gather(block_values, "blk", axis=0, tiled=True)

    def block_total(partial_rows):
        return lax.psum_scatter(
            partial_rows.astype(jnp.bfloat16), "blk", scatter_dimension=0, tiled=True
        ).astype(jnp.float32)[0]

    def reduce_updates(ancestor_sums, tree_level):
        group_size = leaf_count >> tree_level
        grid_sums = ancestor_sums.reshape(group_size, block_count, block_rows, load_count)
        return block_total(halve(grid_sums, level_bits(tree_level)))

    def solve_forward(inverse_tile, residual, tree_level):
        group_size = leaf_count >> tree_level
        columns = columns_of(residual)
        partial_value = jnp.dot(inverse_tile[0, 0], columns, preferred_element_type=jnp.float32)
        solved = halve(
            partial_value.reshape(group_size, block_rows, load_count), level_bits(tree_level)
        )
        return (solved * live_of(tree_level)).astype(jnp.bfloat16)

    def solve_backward(inverse_tile, reduced, tree_level):
        gathered = double(reduced, level_bits(tree_level))
        partial_value = lax.dot_general(
            inverse_tile[0, 0],
            gathered,
            (((0,), (0,)), ((), ())),
            preferred_element_type=jnp.float32,
        )
        solved = block_total(partial_value.reshape(block_count, block_rows, load_count))
        return (solved * live_of(tree_level)).astype(jnp.bfloat16)

    def lift(coupling, pattern, solved, lower_level):
        block_ids = pattern[node_of(lower_level)]
        update = lax.dot_general(
            coupling, solved, (((0,), (0,)), ((), ())), preferred_element_type=jnp.float32
        )
        return (block_ids, update.reshape(-1, block_rows, load_count))

    def node_vector(block_values, tree_level):
        return double(columns_of(block_values), level_bits(tree_level)).reshape(
            -1, block_rows, load_count
        )

    def pull(coupling, pattern, vector_blocks, lower_level):
        block_ids = pattern[node_of(lower_level)]
        chosen = vector_blocks[block_ids].reshape(-1, load_count)
        return jnp.dot(coupling, chosen, preferred_element_type=jnp.float32)

    lower_solved = solve_forward(inverse_lower, loads[2].astype(jnp.bfloat16), 2)
    between_ids, between_update = lift(couple_between, pattern_between, lower_solved, 2)
    middle_sums = jnp.zeros(((leaf_count >> 1) * block_count, block_rows, load_count), jnp.float32)
    middle_sums = middle_sums.at[between_ids].add(between_update)
    middle_residual = (loads[1] - reduce_updates(middle_sums, 1)).astype(jnp.bfloat16)
    middle_solved = solve_forward(inverse_middle, middle_residual, 1)
    middle_ids, middle_update = lift(couple_middle, pattern_middle, middle_solved, 1)
    lower_ids, lower_update = lift(couple_lower, pattern_lower, lower_solved, 2)
    root_sums = jnp.zeros((root_total, block_rows, load_count), jnp.float32)
    root_sums = root_sums.at[middle_ids].add(middle_update).at[lower_ids].add(lower_update)
    root_update = reduce_updates(root_sums, 0)
    root_residual = (loads[0] - root_update).astype(jnp.bfloat16)
    root_solved = solve_forward(inverse_root, root_residual, 0)
    root_answer = solve_backward(inverse_root, root_solved, 0)
    root_blocks = node_vector(root_answer, 0)
    middle_pull = pull(couple_middle, pattern_middle, root_blocks, 1)
    middle_reduced = (middle_solved.astype(jnp.float32) - middle_pull).astype(jnp.bfloat16)
    middle_answer = solve_backward(inverse_middle, middle_reduced, 1)
    middle_blocks = node_vector(middle_answer, 1)
    lower_pull = pull(couple_lower, pattern_lower, root_blocks, 2) + pull(
        couple_between, pattern_between, middle_blocks, 2
    )
    lower_reduced = (lower_solved.astype(jnp.float32) - lower_pull).astype(jnp.bfloat16)
    lower_answer = solve_backward(inverse_lower, lower_reduced, 2)
    forward = jnp.stack([root_solved, middle_solved, lower_solved])
    solution = jnp.stack([root_answer, middle_answer, lower_answer])
    return (forward, solution)


def solution(mesh):
    in_specs = (
        P(None, ("leaf", "blk"), None),
        P("leaf", "blk", None, None),
        P("leaf", "blk", None, None),
        P("leaf", "blk", None, None),
        P(("leaf", "blk"), None),
        P(("leaf", "blk"), None),
        P(("leaf", "blk"), None),
        P(),
        P(),
        P(),
        P(),
    )
    out_specs = (P(None, ("leaf", "blk"), None), P(None, ("leaf", "blk"), None))
    return jax.shard_map(shards, mesh=mesh, in_specs=in_specs, out_specs=out_specs, check_vma=False)
```

profile of v0, /device:TPU:0, one launch (start us, length us, event | category | flops | bytes accessed | tf_op | source)
XLA Modules:
  0.0 725.8 jit_solution(14835056462105034316)
XLA Ops:
  8.3 13.3 %all-gather = bf16[1,1024,128]{2,1,0:T(8,128)(2,1)S(1)} all-gather(bf16[1,128,128]{2,1,0:T(8,128)(2,1)S(1)} %slice.319), channel_id=2, replica_groups=mesh['leaf'=16,'blk'=8] {'blk'}, dimensions={1}, use_global_device_ids=true | all-gather | bytes 294912 | tf_op jit(solution)/shard_map/all_gather | solution.py:70
  40.4 7.1 scatter_fusion
  54.5 19.7 %collective-permute-done.2 = bf16[4,8,128,128]{3,2,1,0:T(8,128)(2,1)S(1)} collective-permute-done((bf16[4,8,128,128]{3,2,1,0:T(8,128)(2,1)S(1)}, bf16[4,8,128,128]{3,2,1,0:T(8,128)(2,1)S(1)}, u32[]{:S(2)}, u32[]{:S(2)}) %collective-permute-start.2) | collective-permute-done | bytes 1048608 | tf_op jit(solution)/shard_map/ppermute | solution.py:8
  77.7 10.6 %collective-permute-done.3 = bf16[2,8,128,128]{3,2,1,0:T(8,128)(2,1)S(1)} collective-permute-done((bf16[2,8,128,128]{3,2,1,0:T(8,128)(2,1)S(1)}, bf16[2,8,128,128]{3,2,1,0:T(8,128)(2,1)S(1)}, u32[]{:S(2)}, u32[]{:S(2)}) %collective-permute-start.3) | collective-permute-done | bytes 524320 | tf_op jit(solution)/shard_map/ppermute | solution.py:8
  89.2 5.8 collective-permute-done.4
  96.5 31.5 %reduce-scatter.6.cloned.1.call-done = bf16[1,128,128]{2,1,0:T(8,128)(2,1)} async-done(((bf16[8,128,128]{2,1,0:T(8,128)(2,1)}), bf16[1,128,128]{2,1,0:T(8,128)(2,1)}) %reduce-scatter.6.cloned.1.call-update) | async-done | bytes 32784 | tf_op jit(solution)/shard_map/reduce_scatter | solution.py:73
  128.8 12.8 %all-gather.1 = bf16[1,1024,128]{2,1,0:T(8,128)(2,1)S(1)} all-gather(bf16[1,128,128]{2,1,0:T(8,128)(2,1)S(1)} %subtract_convert_fusion.1), channel_id=3, replica_groups=mesh['leaf'=16,'blk'=8] {'blk'}, dimensions={1}, use_global_device_ids=true | all-gather | bytes 294912 | tf_op jit(solution)/shard_map/all_gather | solution.py:70
  167.6 5.6 copy.33
  177.5 13.7 %scatter_fusion.1 = f32[128,128,128]{2,1,0:T(8,128)} fusion(f32[128,128,128]{2,1,0:T(8,128)} %broadcast_in_dim.4, s32[64]{0:T(128)S(1)} %fusion.64, f32[64,128,128]{2,1,0:T(8,128)} %bitcast.139), kind=kCustom, calls=%fused_computation.4 | custom fusion | flops 1048576 | bytes 12583168 | tf_op jit(solution)/shard_map/scatter-add | solution.py:128
  191.2 7.2 scatter_fusion.2
  209.9 39.8 %collective-permute-done.8 = bf16[8,8,128,128]{3,2,1,0:T(8,128)(2,1)S(1)} collective-permute-done((bf16[8,8,128,128]{3,2,1,0:T(8,128)(2,1)S(1)}, bf16[8,8,128,128]{3,2,1,0:T(8,128)(2,1)S(1)}, u32[]{:S(2)}, u32[]{:S(2)}) %collective-permute-start.8) | collective-permute-done | bytes 2097184 | tf_op jit(solution)/shard_map/ppermute | solution.py:8
  252.3 20.7 %collective-permute-done.9 = bf16[4,8,128,128]{3,2,1,0:T(8,128)(2,1)S(1)} collective-permute-done((bf16[4,8,128,128]{3,2,1,0:T(8,128)(2,1)S(1)}, bf16[4,8,128,128]{3,2,1,0:T(8,128)(2,1)S(1)}, u32[]{:S(2)}, u32[]{:S(2)}) %collective-permute-start.9) | collective-permute-done | bytes 1048608 | tf_op jit(solution)/shard_map/ppermute | solution.py:8
  276.5 9.9 %collective-permute-done.10 = bf16[2,8,128,128]{3,2,1,0:T(8,128)(2,1)S(1)} collective-permute-done((bf16[2,8,128,128]{3,2,1,0:T(8,128)(2,1)S(1)}, bf16[2,8,128,128]{3,2,1,0:T(8,128)(2,1)S(1)}, u32[]{:S(2)}, u32[]{:S(2)}) %collective-permute-start.10) | collective-permute-done | bytes 524320 | tf_op jit(solution)/shard_map/ppermute | solution.py:8
  286.7 6.4 collective-permute-done.11
  294.0 31.3 %reduce-scatter.8.cloned.1.call-done = bf16[1,128,128]{2,1,0:T(8,128)(2,1)} async-done(((bf16[8,128,128]{2,1,0:T(8,128)(2,1)}), bf16[1,128,128]{2,1,0:T(8,128)(2,1)}) %reduce-scatter.8.cloned.1.call-update) | async-done | bytes 32784 | tf_op jit(solution)/shard_map/reduce_scatter | solution.py:73
  326.1 12.8 %all-gather.2 = bf16[1,1024,128]{2,1,0:T(8,128)(2,1)S(1)} all-gather(bf16[1,128,128]{2,1,0:T(8,128)(2,1)S(1)} %subtract_convert_fusion), channel_id=4, replica_groups=mesh['leaf'=16,'blk'=8] {'blk'}, dimensions={1}, use_global_device_ids=true | all-gather | bytes 294912 | tf_op jit(solution)/shard_map/all_gather | solution.py:70
  348.8 5.1 collective-permute-done.12
  380.9 4.6 collective-permute-done.18
  387.6 5.9 collective-permute-done.19
  397.3 29.3 %reduce-scatter.10.cloned.1.call-done = bf16[1,128,128]{2,1,0:T(8,128)(2,1)} async-done(((bf16[8,128,128]{2,1,0:T(8,128)(2,1)}), bf16[1,128,128]{2,1,0:T(8,128)(2,1)}) %reduce-scatter.10.cloned.1.call-update) | async-done | bytes 32784 | tf_op jit(solution)/shard_map/reduce_scatter | solution.py:73
  427.4 12.8 %all-gather.3 = bf16[1,1024,128]{2,1,0:T(8,128)(2,1)S(1)} all-gather(bf16[1,128,128]{2,1,0:T(8,128)(2,1)S(1)} %multiply_convert_fusion.2), channel_id=5, replica_groups=mesh['leaf'=16,'blk'=8] {'blk'}, dimensions={1}, use_global_device_ids=true | all-gather | bytes 294912 | tf_op jit(solution)/shard_map/all_gather | solution.py:70
  441.8 7.0 collective-permute-done.20
  452.1 11.8 %collective-permute-done.21 = bf16[2048,128]{1,0:T(8,128)(2,1)S(1)} collective-permute-done((bf16[2048,128]{1,0:T(8,128)(2,1)S(1)}, bf16[2048,128]{1,0:T(8,128)(2,1)S(1)}, u32[]{:S(2)}, u32[]{:S(2)}) %collective-permute-start.21) | collective-permute-done | bytes 524320 | tf_op jit(solution)/shard_map/ppermute | solution.py:8
  465.9 22.1 %collective-permute-done.22 = bf16[4096,128]{1,0:T(8,128)(2,1)S(1)} collective-permute-done((bf16[4096,128]{1,0:T(8,128)(2,1)S(1)}, bf16[4096,128]{1,0:T(8,128)(2,1)S(1)}, u32[]{:S(2)}, u32[]{:S(2)}) %collective-permute-start.22) | collective-permute-done | bytes 1048608 | tf_op jit(solution)/shard_map/ppermute | solution.py:8
  492.0 43.5 %collective-permute-done.23 = bf16[8192,128]{1,0:T(8,128)(2,1)S(1)} collective-permute-done((bf16[8192,128]{1,0:T(8,128)(2,1)S(1)}, bf16[8192,128]{1,0:T(8,128)(2,1)S(1)}, u32[]{:S(2)}, u32[]{:S(2)}) %collective-permute-start.23) | collective-permute-done | bytes 2097184 | tf_op jit(solution)/shard_map/ppermute | solution.py:8
  535.5 15.9 %maximum_select_fusion = bf16[16384,128]{1,0:T(8,128)(2,1)} fusion(bf16[8192,128]{1,0:T(8,128)(2,1)S(1)} %maximum_select_fusion.1, bf16[8192,128]{1,0:T(8,128)(2,1)S(1)} %collective-permute-done.23, pred[]{:T(512)S(6)} %eq.11), kind=kLoop, calls=%fused_computation.9 | loop fusion | flops 18874368 | bytes 8388609 | tf_op jit(solution)/shard_map/jit(_where)/select_n | solution.py:62
  574.7 30.3 %reduce-scatter.12.cloned.1.call-done = bf16[1,128,128]{2,1,0:T(8,128)(2,1)} async-done(((bf16[8,128,128]{2,1,0:T(8,128)(2,1)}), bf16[1,128,128]{2,1,0:T(8,128)(2,1)}) %reduce-scatter.12.cloned.1.call-update) | async-done | bytes 32784 | tf_op jit(solution)/shard_map/reduce_scatter | solution.py:73
  605.8 12.8 %all-gather.4 = bf16[1,1024,128]{2,1,0:T(8,128)(2,1)S(1)} all-gather(bf16[1,128,128]{2,1,0:T(8,128)(2,1)S(1)} %multiply_convert_fusion.1), channel_id=6, replica_groups=mesh['leaf'=16,'blk'=8] {'blk'}, dimensions={1}, use_global_device_ids=true | all-gather | bytes 294912 | tf_op jit(solution)/shard_map/all_gather | solution.py:70
  620.1 7.1 collective-permute-done.27
  630.4 11.9 %collective-permute-done.28 = bf16[2048,128]{1,0:T(8,128)(2,1)S(1)} collective-permute-done((bf16[2048,128]{1,0:T(8,128)(2,1)S(1)}, bf16[2048,128]{1,0:T(8,128)(2,1)S(1)}, u32[]{:S(2)}, u32[]{:S(2)}) %collective-permute-start.28) | collective-permute-done | bytes 524320 | tf_op jit(solution)/shard_map/ppermute | solution.py:8
  648.4 18.3 %collective-permute-done.29 = bf16[4096,128]{1,0:T(8,128)(2,1)} collective-permute-done((bf16[4096,128]{1,0:T(8,128)(2,1)S(1)}, bf16[4096,128]{1,0:T(8,128)(2,1)}, u32[]{:S(2)}, u32[]{:S(2)}) %collective-permute-start.29) | collective-permute-done | bytes 1048608 | tf_op jit(solution)/shard_map/ppermute | solution.py:8
  687.5 29.9 %reduce-scatter.14.cloned.1.call-done = bf16[1,128,128]{2,1,0:T(8,128)(2,1)} async-done(((bf16[8,128,128]{2,1,0:T(8,128)(2,1)}), bf16[1,128,128]{2,1,0:T(8,128)(2,1)}) %reduce-scatter.14.cloned.1.call-update) | async-done | bytes 32784 | tf_op jit(solution)/shard_map/reduce_scatter | solution.py:73
  (168 shorter events, 192.8 us)
Async XLA Ops:
  7.2 120.8 %reduce-scatter.6.cloned.1.call-start = ((), (), s32[]{:S(2)}) async-start(), calls=%async_computation.5 | async-start | bytes 294912 | tf_op jit(solution)/shard_map/reduce_scatter | solution.py:73
  23.2 5.9 collective-permute-start
  50.0 24.2 %collective-permute-start.2 = (bf16[4,8,128,128]{3,2,1,0:T(8,128)(2,1)S(1)}, bf16[4,8,128,128]{3,2,1,0:T(8,128)(2,1)S(1)}, u32[]{:S(2)}, u32[]{:S(2)}) collective-permute-start(bf16[4,8,128,128]{3,2,1,0:T(8,128)(2,1)S(1)} %bitcast.151), channel_id=1, source_target_pairs={{0,32},{8,40},{16,48},{24,56},{32,0},{40,8},{48,16},{56,24},{64,96... | collective-permute-start | bytes 3145736 | tf_op jit(solution)/shard_map/ppermute | solution.py:8
  74.7 13.6 %collective-permute-start.3 = (bf16[2,8,128,128]{3,2,1,0:T(8,128)(2,1)S(1)}, bf16[2,8,128,128]{3,2,1,0:T(8,128)(2,1)S(1)}, u32[]{:S(2)}, u32[]{:S(2)}) collective-permute-start(bf16[2,8,128,128]{3,2,1,0:T(8,128)(2,1)S(1)} %select_convert_fusion.4), channel_id=1, source_target_pairs={{0,16},{8,24},{16,0},{24,8},{32,48},{40,56},{48,32},{56,40},{64,80... | collective-permute-start | bytes 1572872 | tf_op jit(solution)/shard_map/ppermute | solution.py:8
  88.5 6.5 collective-permute-start.4
  95.8 229.5 %reduce-scatter.8.cloned.1.call-start = ((), (), s32[]{:S(2)}) async-start(), calls=%async_computation.6 | async-start | bytes 294912 | tf_op jit(solution)/shard_map/reduce_scatter | solution.py:73
  145.7 6.1 collective-permute-start.5
  152.7 5.8 collective-permute-start.6
  158.6 6.2 collective-permute-start.7
  202.2 47.4 %collective-permute-start.8 = (bf16[8,8,128,128]{3,2,1,0:T(8,128)(2,1)S(1)}, bf16[8,8,128,128]{3,2,1,0:T(8,128)(2,1)S(1)}, u32[]{:S(2)}, u32[]{:S(2)}) collective-permute-start(bf16[8,8,128,128]{3,2,1,0:T(8,128)(2,1)S(1)} %bitcast.149), channel_id=1, source_target_pairs={{0,64},{8,72},{16,80},{24,88},{32,96},{40,104},{48,112},{56,120},{... | collective-permute-start | bytes 6291464 | tf_op jit(solution)/shard_map/ppermute | solution.py:8
  250.7 22.3 %collective-permute-start.9 = (bf16[4,8,128,128]{3,2,1,0:T(8,128)(2,1)S(1)}, bf16[4,8,128,128]{3,2,1,0:T(8,128)(2,1)S(1)}, u32[]{:S(2)}, u32[]{:S(2)}) collective-permute-start(bf16[4,8,128,128]{3,2,1,0:T(8,128)(2,1)S(1)} %select_convert_fusion.1), channel_id=1, source_target_pairs={{0,32},{8,40},{16,48},{24,56},{32,0},{40,8},{48,16},{56,24},{64,96... | collective-permute-start | bytes 3145736 | tf_op jit(solution)/shard_map/ppermute | solution.py:8
  273.7 12.7 %collective-permute-start.10 = (bf16[2,8,128,128]{3,2,1,0:T(8,128)(2,1)S(1)}, bf16[2,8,128,128]{3,2,1,0:T(8,128)(2,1)S(1)}, u32[]{:S(2)}, u32[]{:S(2)}) collective-permute-start(bf16[2,8,128,128]{3,2,1,0:T(8,128)(2,1)S(1)} %select_convert_fusion.3), channel_id=1, source_target_pairs={{0,16},{8,24},{16,0},{24,8},{32,48},{40,56},{48,32},{56,40},{64,80... | collective-permute-start | bytes 1572872 | tf_op jit(solution)/shard_map/ppermute | solution.py:8
  286.7 6.5 collective-permute-start.11
  293.9 132.7 %reduce-scatter.10.cloned.1.call-start = ((), (), s32[]{:S(2)}) async-start(), calls=%async_computation.7 | async-start | bytes 294912 | tf_op jit(solution)/shard_map/reduce_scatter | solution.py:73
  343.6 10.3 %collective-permute-start.12 = (bf16[8,128,128]{2,1,0:T(8,128)(2,1)}, bf16[8,128,128]{2,1,0:T(8,128)(2,1)S(1)}, u32[]{:S(2)}, u32[]{:S(2)}) collective-permute-start(bf16[8,128,128]{2,1,0:T(8,128)(2,1)} %bitcast.163), channel_id=1, source_target_pairs={{0,64},{8,72},{16,80},{24,88},{32,96},{40,104},{48,112},{56,120},{... | collective-permute-start | bytes 786440 | tf_op jit(solution)/shard_map/ppermute | solution.py:8
  353.9 5.0 collective-permute-start.13
  359.1 5.8 collective-permute-start.14
  373.1 5.8 collective-permute-start.17
  379.0 6.4 collective-permute-start.18
  385.5 8.0 %collective-permute-start.19 = (bf16[1024,128]{1,0:T(8,128)(2,1)S(1)}, bf16[1024,128]{1,0:T(8,128)(2,1)S(1)}, u32[]{:S(2)}, u32[]{:S(2)}) collective-permute-start(bf16[1024,128]{1,0:T(8,128)(2,1)S(1)} %maximum_select_fusion.9), channel_id=1, source_target_pairs={{0,64},{8,72},{16,80},{24,88},{32,96},{40,104},{48,112},{56,120},{... | collective-permute-start | bytes 786440 | tf_op jit(solution)/shard_map/ppermute | solution.py:8
  397.3 207.7 %reduce-scatter.12.cloned.1.call-start = ((), (), s32[]{:S(2)}) async-start(), calls=%async_computation.8 | async-start | bytes 294912 | tf_op jit(solution)/shard_map/reduce_scatter | solution.py:73
  440.2 8.6 %collective-permute-start.20 = (bf16[1024,128]{1,0:T(8,128)(2,1)S(1)}, bf16[1024,128]{1,0:T(8,128)(2,1)S(1)}, u32[]{:S(2)}, u32[]{:S(2)}) collective-permute-start(bf16[1024,128]{1,0:T(8,128)(2,1)S(1)} %bitcast.156), channel_id=1, source_target_pairs={{0,8},{8,0},{16,24},{24,16},{32,40},{40,32},{48,56},{56,48},{64,72... | collective-permute-start | bytes 786440 | tf_op jit(solution)/shard_map/ppermute | solution.py:8
  448.9 15.0 %collective-permute-start.21 = (bf16[2048,128]{1,0:T(8,128)(2,1)S(1)}, bf16[2048,128]{1,0:T(8,128)(2,1)S(1)}, u32[]{:S(2)}, u32[]{:S(2)}) collective-permute-start(bf16[2048,128]{1,0:T(8,128)(2,1)S(1)} %maximum_select_fusion.7), channel_id=1, source_target_pairs={{0,16},{8,24},{16,0},{24,8},{32,48},{40,56},{48,32},{56,40},{64,80... | collective-permute-start | bytes 1572872 | tf_op jit(solution)/shard_map/ppermute | solution.py:8
  464.2 23.8 %collective-permute-start.22 = (bf16[4096,128]{1,0:T(8,128)(2,1)S(1)}, bf16[4096,128]{1,0:T(8,128)(2,1)S(1)}, u32[]{:S(2)}, u32[]{:S(2)}) collective-permute-start(bf16[4096,128]{1,0:T(8,128)(2,1)S(1)} %maximum_select_fusion.3), channel_id=1, source_target_pairs={{0,32},{8,40},{16,48},{24,56},{32,0},{40,8},{48,16},{56,24},{64,96... | collective-permute-start | bytes 3145736 | tf_op jit(solution)/shard_map/ppermute | solution.py:8
  488.5 47.0 %collective-permute-start.23 = (bf16[8192,128]{1,0:T(8,128)(2,1)S(1)}, bf16[8192,128]{1,0:T(8,128)(2,1)S(1)}, u32[]{:S(2)}, u32[]{:S(2)}) collective-permute-start(bf16[8192,128]{1,0:T(8,128)(2,1)S(1)} %maximum_select_fusion.1), channel_id=1, source_target_pairs={{0,64},{8,72},{16,80},{24,88},{32,96},{40,104},{48,112},{56,120},{... | collective-permute-start | bytes 6291464 | tf_op jit(solution)/shard_map/ppermute | solution.py:8
  562.4 5.8 collective-permute-start.25
  568.3 5.0 collective-permute-start.26
  574.7 142.7 %reduce-scatter.14.cloned.1.call-start = ((), (), s32[]{:S(2)}) async-start(), calls=%async_computation.9 | async-start | bytes 294912 | tf_op jit(solution)/shard_map/reduce_scatter | solution.py:73
  618.6 8.6 %collective-permute-start.27 = (bf16[1024,128]{1,0:T(8,128)(2,1)S(1)}, bf16[1024,128]{1,0:T(8,128)(2,1)S(1)}, u32[]{:S(2)}, u32[]{:S(2)}) collective-permute-start(bf16[1024,128]{1,0:T(8,128)(2,1)S(1)} %bitcast.158), channel_id=1, source_target_pairs={{0,8},{8,0},{16,24},{24,16},{32,40},{40,32},{48,56},{56,48},{64,72... | collective-permute-start | bytes 786440 | tf_op jit(solution)/shard_map/ppermute | solution.py:8
  627.3 15.0 %collective-permute-start.28 = (bf16[2048,128]{1,0:T(8,128)(2,1)S(1)}, bf16[2048,128]{1,0:T(8,128)(2,1)S(1)}, u32[]{:S(2)}, u32[]{:S(2)}) collective-permute-start(bf16[2048,128]{1,0:T(8,128)(2,1)S(1)} %maximum_select_fusion.8), channel_id=1, source_target_pairs={{0,16},{8,24},{16,0},{24,8},{32,48},{40,56},{48,32},{56,40},{64,80... | collective-permute-start | bytes 1572872 | tf_op jit(solution)/shard_map/ppermute | solution.py:8
  642.6 24.1 %collective-permute-start.29 = (bf16[4096,128]{1,0:T(8,128)(2,1)S(1)}, bf16[4096,128]{1,0:T(8,128)(2,1)}, u32[]{:S(2)}, u32[]{:S(2)}) collective-permute-start(bf16[4096,128]{1,0:T(8,128)(2,1)S(1)} %maximum_select_fusion.4), channel_id=1, source_target_pairs={{0,32},{8,40},{16,48},{24,56},{32,0},{40,8},{48,16},{56,24},{64,96... | collective-permute-start | bytes 3145736 | tf_op jit(solution)/shard_map/ppermute | solution.py:8
  679.8 5.8 collective-permute-start.31
  (16 other events, 291.9 us)
Sparse Core Ops, SparseCore 0:
  95.9 31.9 reduce-scatter.5
  294.0 31.1 reduce-scatter.7
  397.4 29.1 reduce-scatter.9
  574.8 30.1 reduce-scatter.11
  687.0 30.3 reduce-scatter.13
where the time goes:
time: 735 us; the launch traced here: 726 us
  waiting for transfers between devices  437 us (59%)
  other arithmetic  76.2 us (10%)
  starting transfers between devices  70.4 us (10%)
  blocking collectives  64.6 us (9%)
  local copies, waits for them, and re-layouts  38.8 us (5%)
  matrix products  22.5 us (3%)
  between operations  16.6 us (2%)
    ppermute x32, waiting for transfers between devices, swapped(): lax.ppermute(x, axis, [(i, i ^ 1 << stride) for i in range(lax.axis_size(...  284 us
    reduce_scatter x5, waiting for transfers between devices, block_total(): lax.psum_scatter(partial_rows.astype(jnp.bfloat16), 'blk', scatter_dimens...  152 us
    ppermute x32, starting transfers between devices, swapped(): lax.ppermute(x, axis, [(i, i ^ 1 << stride) for i in range(lax.axis_size(...  70.2 us
    all_gather x5, blocking collectives, columns_of(): return lax.all_gather(block_values, 'blk', axis=0, tiled=True)  64.6 us
    select_n x13, other arithmetic, double(): jnp.where(upper_half, jnp.concatenate([partner, segment], 0), jnp.concate...  20.9 us
    scatter-add x2, other arithmetic, shards(): root_sums.at[middle_ids].add(middle_update).at[lower_ids].add(lower_update)  20.9 us
  transfers between devices with their start and end apart: 37, of which 36 were waited for; matrix products, arithmetic and copies ran while one was open for 3% of the time, Pallas kernels for 0%

commit v1 on v0

v1 whole, which is shorter than its diff:
```python
import functools

import jax
import jax.numpy as jnp
from jax import lax
from jax.experimental import pallas as pl
from jax.experimental.pallas import tpu as pltpu
from jax.sharding import PartitionSpec as P

BF16 = jnp.bfloat16
F32 = jnp.float32
VMEM_LIMIT = 48 * 1024 * 1024


def lift_kernel(level_spans, info, *refs):
    total = len(level_spans)
    patterns, values, factors = refs[:total], refs[total : 2 * total], refs[2 * total : 3 * total]
    keep, send, sums = refs[3 * total :]
    core = info[0]
    sums[...] = jnp.zeros_like(sums)
    half = keep.shape[0]
    for index, span in enumerate(level_spans):
        node = info[1 + index]
        value = values[index][...]

        def chunk(step, carry, index=index, node=node, value=value):
            start = pl.multiple_of(step * 1024, 1024)
            product = jnp.dot(
                value, factors[index][:, pl.ds(start, 1024)], preferred_element_type=F32
            )
            for part in range(8):
                block = patterns[index][node, step * 8 + part]
                slot = ((block & 1) ^ core) * half + (block >> 1)
                sums[slot] += product[:, part * 128 : part * 128 + 128]
            return carry

        lax.fori_loop(0, span // 1024, chunk, 0)

    def emit(slot, carry):
        keep[slot] = sums[slot].astype(BF16)
        send[slot] = sums[half + slot].astype(BF16)
        return carry

    lax.fori_loop(0, half, emit, 0)


def lift(info, patterns, values, factors, half):
    spans = tuple(f.shape[1] for f in factors)
    smem = pl.BlockSpec(memory_space=pltpu.SMEM)
    vmem = pl.BlockSpec(memory_space=pltpu.VMEM)
    total = len(factors)
    shape = jax.ShapeDtypeStruct((half, 128, 128), BF16)
    return pl.pallas_call(
        functools.partial(lift_kernel, spans),
        out_shape=(shape, shape),
        in_specs=[smem] * (1 + total) + [vmem] * (2 * total),
        out_specs=(vmem, vmem),
        scratch_shapes=[pltpu.VMEM((2 * half, 128, 128), F32)],
        compiler_params=pltpu.CompilerParams(vmem_limit_bytes=VMEM_LIMIT),
        name="lift",
    )(info, *patterns, *values, *factors)


def pull_kernel(info, pattern, own, other, factor, out, chosen):
    core, node = info[0], info[1]
    count = factor.shape[1] // 128

    def pick(position, carry):
        block = pattern[node, position]
        mine = (block & 1) == core
        row = pl.multiple_of(position * 128, 128)
        chosen[pl.ds(row, 128), :] = jnp.where(mine, own[block >> 1], other[block >> 1])
        return carry

    lax.fori_loop(0, count, pick, 0)
    out[...] = jnp.dot(factor[...], chosen[...], preferred_element_type=F32)


def pull(info, pattern, own, other, factor):
    smem = pl.BlockSpec(memory_space=pltpu.SMEM)
    vmem = pl.BlockSpec(memory_space=pltpu.VMEM)
    return pl.pallas_call(
        pull_kernel,
        out_shape=jax.ShapeDtypeStruct((128, 128), F32),
        in_specs=[smem, smem, vmem, vmem, vmem],
        out_specs=vmem,
        scratch_shapes=[pltpu.VMEM((factor.shape[1], 128), BF16)],
        compiler_params=pltpu.CompilerParams(vmem_limit_bytes=VMEM_LIMIT),
        name="pull",
    )(info, pattern, own, other, factor)


def shards(
    loads,
    inverse_root,
    inverse_middle,
    inverse_lower,
    couple_middle,
    couple_lower,
    couple_between,
    pattern_middle,
    pattern_lower,
    pattern_between,
    node_blocks,
):
    leaf_count = lax.axis_size("leaf")
    block_count = lax.axis_size("blk")
    chip_count = block_count // 2
    leaf_index = lax.axis_index("leaf")
    block_index = lax.axis_index("blk")
    core = block_index & 1
    chip = block_index >> 1
    leaf_bits = leaf_count.bit_length() - 1

    def node_of(level):
        return leaf_index >> (leaf_bits - level)

    def leaf_groups(level):
        size = leaf_count >> level
        return [[g * size + j for j in range(size)] for g in range(1 << level)]

    chip_groups = [[2 * x + c for x in range(chip_count)] for c in range(2)]

    def limit_of(level):
        return node_blocks[2**level - 1 + node_of(level)]

    def live_own(level):
        position = (leaf_index & ((leaf_count >> level) - 1)) * block_count + block_index
        return (position < limit_of(level)).astype(F32)

    def live_chips(level):
        position = (leaf_index & ((leaf_count >> level) - 1)) * block_count + core
        position = position + 2 * jnp.arange(chip_count)
        return (position < limit_of(level)).astype(F32)[:, None, None]

    def swap_core(value):
        return lax.ppermute(value, "blk", [(i, i ^ 1) for i in range(block_count)])

    def swap_chip(value, first):
        pairs = []
        for i in range(block_count):
            near = (i & 1 == 0) == first
            pairs.append((i, i ^ (2 if near else 6)))
        return lax.ppermute(value, "blk", pairs)

    def exchange(value, level):
        groups = leaf_groups(level) if level else None
        return lax.all_to_all(value, "leaf", 0, 0, tiled=True, axis_index_groups=groups)

    def reduce_leaf(partial_value, level):
        return exchange(partial_value.astype(BF16), level).astype(F32).sum(0)

    def gather_leaf(value, level):
        size = leaf_count >> level
        return exchange(jnp.broadcast_to(value[None], (size,) + value.shape), level)

    def sum_chips(value):
        value = value + swap_chip(value.astype(BF16), True).astype(F32)
        return value + swap_chip(value.astype(BF16), False).astype(F32)

    def both_cores(value):
        other = swap_core(value)
        return jnp.where(
            core == 0, jnp.stack([value, other], 1), jnp.stack([other, value], 1)
        )

    def sum_cores(partial_value):
        mine = jnp.where(core == 0, partial_value[:, 0], partial_value[:, 1])
        theirs = jnp.where(core == 0, partial_value[:, 1], partial_value[:, 0])
        return mine + swap_core(theirs.astype(BF16)).astype(F32)

    def own_chip(blocks):
        return lax.dynamic_index_in_dim(blocks, chip, 0, keepdims=False)

    chip_mask = (jnp.arange(chip_count) == chip).astype(F32)[:, None, None]

    def info_of(*levels):
        return jnp.stack([core.astype(jnp.int32)] + [node_of(k).astype(jnp.int32) for k in levels])

    def residual(load, updates, level):
        keep, send = updates
        size = leaf_count >> level
        summed = (keep.astype(F32) + swap_core(send).astype(F32)).astype(BF16)
        partial_sum = reduce_leaf(summed.reshape(size, chip_count, 128, 128), level)
        partial_rest = chip_mask * load.T[None] - partial_sum
        rest = both_cores(sum_chips(partial_rest).astype(BF16))
        return rest.reshape(block_count, 128, 128)

    def forward_solve(tile, rest, level, transposed):
        size = leaf_count >> level
        columns = rest.swapaxes(1, 2) if transposed else rest
        partial_value = jnp.dot(
            tile[0, 0], columns.reshape(-1, 128), preferred_element_type=F32
        )
        return reduce_leaf(partial_value.reshape(size, 128, 128), level)

    def backward_partial(tile, value, level):
        gathered = gather_leaf(value, level).reshape(-1, 128)
        partial_value = lax.dot_general(
            tile[0, 0], gathered, (((0,), (0,)), ((), ())), preferred_element_type=F32
        )
        return sum_cores(partial_value.reshape(chip_count, 2, 128, 128))

    load_lower = loads[2].astype(BF16)
    near = lax.all_to_all(
        jnp.broadcast_to(load_lower[None], (chip_count, 128, 128)),
        "blk", 0, 0, tiled=True, axis_index_groups=chip_groups,
    )
    rest_lower = both_cores(near).reshape(block_count, 128, 128)
    y_lower = (forward_solve(inverse_lower, rest_lower, 2, False) * live_own(2)).astype(BF16)
    updates = lift(
        info_of(2), [pattern_between], [y_lower.T], [couple_between],
        (leaf_count >> 1) * chip_count,
    )
    rest_middle = residual(loads[1], updates, 1)
    y_middle = (forward_solve(inverse_middle, rest_middle, 1, True) * live_own(1)).astype(BF16)
    updates = lift(
        info_of(2, 1), [pattern_lower, pattern_middle], [y_lower.T, y_middle.T],
        [couple_lower, couple_middle], leaf_count * chip_count,
    )
    rest_root = residual(loads[0], updates, 0)
    y_root = (forward_solve(inverse_root, rest_root, 0, True) * live_own(0)).astype(BF16)
    x_root = sum_chips(backward_partial(inverse_root, y_root, 0))
    x_root = (x_root * live_chips(0)).astype(BF16)
    own_root = gather_leaf(x_root, 0).reshape(-1, 128, 128)
    other_root = swap_core(own_root)
    pull_middle = pull(info_of(1), pattern_middle, own_root, other_root, couple_middle)
    z_middle = (y_middle.astype(F32) - pull_middle).astype(BF16)
    x_middle = sum_chips(backward_partial(inverse_middle, z_middle, 1))
    x_middle = (x_middle * live_chips(1)).astype(BF16)
    own_middle = gather_leaf(x_middle, 1).reshape(-1, 128, 128)
    other_middle = swap_core(own_middle)
    pull_lower = pull(info_of(2), pattern_lower, own_root, other_root, couple_lower)
    pull_between = pull(info_of(2), pattern_between, own_middle, other_middle, couple_between)
    z_lower = (y_lower.astype(F32) - (pull_lower + pull_between)).astype(BF16)
    x_lower = backward_partial(inverse_lower, z_lower, 2)
    x_lower = lax.all_to_all(
        x_lower.astype(BF16), "blk", 0, 0, tiled=True, axis_index_groups=chip_groups
    )
    x_lower = (x_lower.astype(F32).sum(0) * live_own(2)).astype(BF16)

    forward = jnp.stack([y_root, y_middle, y_lower])
    answer = jnp.stack([own_chip(x_root), own_chip(x_middle), x_lower])
    return (forward, answer)


def solution(mesh):
    in_specs = (
        P(None, ("leaf", "blk"), None),
        P("leaf", "blk", None, None),
        P("leaf", "blk", None, None),
        P("leaf", "blk", None, None),
        P(("leaf", "blk"), None),
        P(("leaf", "blk"), None),
        P(("leaf", "blk"), None),
        P(),
        P(),
        P(),
        P(),
    )
    out_specs = (P(None, ("leaf", "blk"), None), P(None, ("leaf", "blk"), None))
    return jax.shard_map(shards, mesh=mesh, in_specs=in_specs, out_specs=out_specs, check_vma=False)
```

time: 735 us -> 333 us (0.45)
  waiting for transfers between devices: 437 us -> 138 us
  other arithmetic: 76.2 us -> 21.4 us
  starting transfers between devices: 70.4 us -> 35.4 us
  Pallas kernels: 0 us -> 16.6 us
  blocking collectives: 64.6 us -> 81.1 us
  local copies, waits for them, and re-layouts: 38.8 us -> 22.7 us
  between operations: 16.6 us -> 3.16 us
  matrix products: 22.5 us -> 12.3 us
    ppermute x32 -> x18, waiting for transfers between devices: 284 us -> 54.6 us  [the longest x8 38.3 us: swap_chip(): return lax.ppermute(value, 'blk', pairs)]
    reduce_scatter x5 -> x0, waiting for transfers between devices: 152 us -> none  [block_total(): lax.psum_scatter(partial_rows.astype(jnp.bfloat16), 'blk', scatter_dimens...]
    all_to_all x0 -> x7, waiting for transfers between devices: none -> 83.3 us  [the longest x6 77.9 us: exchange(): lax.all_to_all(value, 'leaf', 0, 0, tiled=True, axis_index_groups=groups)]
    all_to_all x0 -> x5, blocking collectives: none -> 81.1 us  [the longest x4 70.9 us: exchange(): lax.all_to_all(value, 'leaf', 0, 0, tiled=True, axis_index_groups=groups)]
    all_gather x5 -> x0, blocking collectives: 64.6 us -> none  [columns_of(): return lax.all_gather(block_values, 'blk', axis=0, tiled=True)]
    ppermute x32 -> x18, starting transfers between devices: 70.2 us -> 6.92 us  [the longest x8 6.31 us: swap_chip(): return lax.ppermute(value, 'blk', pairs)]
    select_n x20 -> x3, other arithmetic: 31 us -> 0.79 us  [both_cores(): jnp.where(core == 0, jnp.stack([value, other], 1), jnp.stack([other, valu...]
    all_to_all x0 -> x7, starting transfers between devices: none -> 28.5 us  [the longest x6 25.2 us: exchange(): lax.all_to_all(value, 'leaf', 0, 0, tiled=True, axis_index_groups=groups)]
  transfers between devices with their start and end apart: 37 -> 25, of which waited for: 36 -> 22; matrix products, arithmetic and copies ran while one was open for 3% -> 2% of each run, Pallas kernels for 0% -> 1%
where the time goes in v1:
time: 333 us; the launch traced here: 331 us
  waiting for transfers between devices  138 us (41%)
  blocking collectives  81.1 us (24%)
  starting transfers between devices  35.4 us (11%)
  local copies, waits for them, and re-layouts  22.7 us (7%)
  other arithmetic  21.4 us (6%)
  Pallas kernels  16.6 us (5%)
  matrix products  12.3 us (4%)
    all_to_all x6, waiting for transfers between devices, exchange(): lax.all_to_all(value, 'leaf', 0, 0, tiled=True, axis_index_groups=groups)  77.9 us
    all_to_all x4, blocking collectives, exchange(): lax.all_to_all(value, 'leaf', 0, 0, tiled=True, axis_index_groups=groups)  70.9 us
    ppermute x8, waiting for transfers between devices, swap_chip(): return lax.ppermute(value, 'blk', pairs)  38.3 us
    all_to_all x6, starting transfers between devices, exchange(): lax.all_to_all(value, 'leaf', 0, 0, tiled=True, axis_index_groups=groups)  25.2 us
    ppermute x10, waiting for transfers between devices, swap_core(): return lax.ppermute(value, 'blk', [(i, i ^ 1) for i in range(block_count)])  16.2 us
    all_to_all x1, blocking collectives, shards(): lax.all_to_all(jnp.broadcast_to(load_lower[None], (chip_count, 128, 128))...  10.2 us
    pallas_call x3, Pallas kernels, pull(): pl.pallas_call(pull_kernel, out_shape=jax.ShapeDtypeStruct((128, 128), F3...  8.76 us
    pallas_call x2, Pallas kernels, lift(): pl.pallas_call(functools.partial(lift_kernel, spans), out_shape=(shape, s...  7.82 us
  transfers between devices with their start and end apart: 25, of which 22 were waited for; matrix products, arithmetic and copies ran while one was open for 2% of the time, Pallas kernels for 1%

profile of v1, /device:TPU:0, one launch (start us, length us, event | category | flops | bytes accessed | tf_op | source)
XLA Modules:
  0.0 330.5 jit_solution(1882162993757978225)
XLA Ops:
  1.7 10.2 %all_to_all.60 = bf16[4,128,128]{2,1,0:T(8,128)(2,1)S(1)} all-to-all(bf16[4,128,128]{2,1,0:T(8,128)(2,1)S(1)} %broadcast_in_dim.15), channel_id=1, replica_groups={{0,2,4,6},{1,3,5,7},{8,10,12,14},{9,11,13,15},{16,18,20,22},{17,19,21,2..., dimensions={0} | all-to-all | bytes 262144 | tf_op jit(solution)/shard_map/all_to_all | solution.py:205
  16.3 4.5 %all-to-all-start.1 = ((bf16[4,128,128]{1,2,0:T(8,128)(2,1)}), bf16[4,128,128]{1,2,0:T(8,128)(2,1)S(1)}, u32[]{:S(2)}, u32[]{:S(2)}) async-start(bf16[4,128,128]{1,2,0:T(8,128)(2,1)} %bitcast.177), calls=%async_computation.1 | async-start | bytes 262144 | tf_op jit(solution)/shard_map/all_to_all | solution.py:148
  20.9 5.9 %all-to-all-done.1 = bf16[4,128,128]{1,2,0:T(8,128)(2,1)S(1)} async-done(((bf16[4,128,128]{1,2,0:T(8,128)(2,1)}), bf16[4,128,128]{1,2,0:T(8,128)(2,1)S(1)}, u32[]{:S(2)}, u32[]{:S(2)}) %all-to-all-start.1) | async-done | bytes 131104 | tf_op jit(solution)/shard_map/all_to_all | solution.py:148
  33.3 3.8 %all-to-all-start.2 = ((bf16[8,4,128,128]{3,2,1,0:T(8,128)(2,1)}), bf16[8,4,128,128]{3,2,1,0:T(8,128)(2,1)S(1)}, u32[]{:S(2)}, u32[]{:S(2)}) async-start(bf16[8,4,128,128]{3,2,1,0:T(8,128)(2,1)} %bitcast.15), calls=%async_computation.2 | async-start | bytes 2097152 | tf_op jit(solution)/shard_map/all_to_all | solution.py:148
  38.7 14.4 %all-to-all-done.2 = bf16[8,4,128,128]{3,2,1,0:T(8,128)(2,1)S(1)} async-done(((bf16[8,4,128,128]{3,2,1,0:T(8,128)(2,1)}), bf16[8,4,128,128]{3,2,1,0:T(8,128)(2,1)S(1)}, u32[]{:S(2)}, u32[]{:S(2)}) %all-to-all-start.2) | async-done | bytes 1048608 | tf_op jit(solution)/shard_map/all_to_all | solution.py:148
  54.0 4.4 %collective-permute-done.2 = bf16[4,128,128]{2,1,0:T(8,128)(2,1)S(1)} collective-permute-done((bf16[4,128,128]{2,1,0:T(8,128)(2,1)S(1)}, bf16[4,128,128]{2,1,0:T(8,128)(2,1)S(1)}, u32[]{:S(2)}, u32[]{:S(2)}) %collective-permute-start.2) | collective-permute-done | bytes 131104 | tf_op jit(solution)/shard_map/ppermute | solution.py:144
  59.7 5.0 %collective-permute-done.3 = bf16[4,128,128]{2,1,0:T(8,128)(2,1)S(1)} collective-permute-done((bf16[4,128,128]{2,1,0:T(8,128)(2,1)S(1)}, bf16[4,128,128]{2,1,0:T(8,128)(2,1)S(1)}, u32[]{:S(2)}, u32[]{:S(2)}) %collective-permute-start.3) | collective-permute-done | bytes 131104 | tf_op jit(solution)/shard_map/ppermute | solution.py:144
  68.2 3.4 %all-to-all-start.3 = ((bf16[8,128,128]{1,2,0:T(8,128)(2,1)}), bf16[8,128,128]{1,2,0:T(8,128)(2,1)S(1)}, u32[]{:S(2)}, u32[]{:S(2)}) async-start(bf16[8,128,128]{1,2,0:T(8,128)(2,1)} %bitcast.193), calls=%async_computation.3 | async-start | bytes 524288 | tf_op jit(solution)/shard_map/all_to_all | solution.py:148
  72.3 7.1 %all-to-all-done.3 = bf16[8,128,128]{1,2,0:T(8,128)(2,1)S(1)} async-done(((bf16[8,128,128]{1,2,0:T(8,128)(2,1)}), bf16[8,128,128]{1,2,0:T(8,128)(2,1)S(1)}, u32[]{:S(2)}, u32[]{:S(2)}) %all-to-all-start.3) | async-done | bytes 262176 | tf_op jit(solution)/shard_map/all_to_all | solution.py:148
  81.8 5.7 %lift.3 = (bf16[64,128,128]{2,1,0:T(8,128)(2,1)S(1)}, bf16[64,128,128]{2,1,0:T(8,128)(2,1)S(1)}) custom-call(s32[3]{0:T(128)S(1)} %pad_add_fusion.info, s32[4,32]{1,0:T(4,128)S(1)} %copy-done.8, s32[2,64]{1,0:T(2,128)S(1)} %copy-done.10, bf16[128,128]{1,0:T(8,128)(2,1)S(1)} %copy.65.refs_1_.refs_2_, bf16[128,128]{1,0:T(8,128)(2,1)S(1)} %copy.66.refs_3_, ...), custom_call_target="tpu_custom_call" | custom-call | tf_op jit(solution)/shard_map/lift/pallas_call | solution.py:53
  87.6 4.1 %collective-permute-done.5 = bf16[64,128,128]{2,1,0:T(8,128)(2,1)S(1)} collective-permute-done((bf16[64,128,128]{2,1,0:T(8,128)(2,1)S(1)}, bf16[64,128,128]{2,1,0:T(8,128)(2,1)S(1)}, u32[]{:S(2)}, u32[]{:S(2)}) %collective-permute-start.5) | collective-permute-done | bytes 2097184 | tf_op jit(solution)/shard_map/ppermute | solution.py:137
  94.2 6.0 %all-to-all-start.4 = ((bf16[16,4,128,128]{3,2,1,0:T(8,128)(2,1)}), bf16[16,4,128,128]{3,2,1,0:T(8,128)(2,1)}, u32[]{:S(2)}, u32[]{:S(2)}) async-start(bf16[16,4,128,128]{3,2,1,0:T(8,128)(2,1)} %bitcast.181), calls=%async_computation.4 | async-start | bytes 4194304 | tf_op jit(solution)/shard_map/all_to_all | solution.py:148
  100.3 32.8 %all-to-all-done.4 = bf16[16,4,128,128]{3,2,1,0:T(8,128)(2,1)} async-done(((bf16[16,4,128,128]{3,2,1,0:T(8,128)(2,1)}), bf16[16,4,128,128]{3,2,1,0:T(8,128)(2,1)}, u32[]{:S(2)}, u32[]{:S(2)}) %all-to-all-start.4) | async-done | bytes 2097184 | tf_op jit(solution)/shard_map/all_to_all | solution.py:148
  135.3 5.0 %collective-permute-done.6 = bf16[4,128,128]{2,1,0:T(8,128)(2,1)S(1)} collective-permute-done((bf16[4,128,128]{2,1,0:T(8,128)(2,1)S(1)}, bf16[4,128,128]{2,1,0:T(8,128)(2,1)S(1)}, u32[]{:S(2)}, u32[]{:S(2)}) %collective-permute-start.6) | collective-permute-done | bytes 131104 | tf_op jit(solution)/shard_map/ppermute | solution.py:144
  141.6 5.0 %collective-permute-done.7 = bf16[4,128,128]{2,1,0:T(8,128)(2,1)S(1)} collective-permute-done((bf16[4,128,128]{2,1,0:T(8,128)(2,1)S(1)}, bf16[4,128,128]{2,1,0:T(8,128)(2,1)S(1)}, u32[]{:S(2)}, u32[]{:S(2)}) %collective-permute-start.7) | collective-permute-done | bytes 131104 | tf_op jit(solution)/shard_map/ppermute | solution.py:144
  150.0 3.7 %fusion.14 = bf16[16,16,8,128]{3,2,1,0:T(8,128)(2,1)S(1)} fusion(bf16[1024,128]{1,0:T(8,128)(2,1)S(1)} %bitcast.191, bf16[1,1,2048,1024]{3,2,1,0:T(8,128)(2,1)} %param.12), kind=kOutput, calls=%fused_computation.14 | convolution fusion | flops 537133056 | bytes 4980736 | tf_op jit(solution)/shard_map/dot_general | solution.py:192
  154.7 4.2 %all-to-all-start.5 = ((bf16[16,128,128]{1,2,0:T(8,128)(2,1)}), bf16[16,128,128]{1,2,0:T(8,128)(2,1)}, u32[]{:S(2)}, u32[]{:S(2)}) async-start(bf16[16,128,128]{1,2,0:T(8,128)(2,1)} %bitcast.189), calls=%async_computation.5 | async-start | bytes 1048576 | tf_op jit(solution)/shard_map/all_to_all | solution.py:148
  159.5 11.6 %all-to-all-done.5 = bf16[16,128,128]{1,2,0:T(8,128)(2,1)} async-done(((bf16[16,128,128]{1,2,0:T(8,128)(2,1)}), bf16[16,128,128]{1,2,0:T(8,128)(2,1)}, u32[]{:S(2)}, u32[]{:S(2)}) %all-to-all-start.5) | async-done | bytes 524320 | tf_op jit(solution)/shard_map/all_to_all | solution.py:148
  172.4 14.0 %all_to_all.61 = bf16[16,128,128]{2,1,0:T(8,128)(2,1)S(1)} all-to-all(bf16[16,128,128]{2,1,0:T(8,128)(2,1)S(1)} %broadcast_in_dim.16), channel_id=1, replica_groups=mesh['leaf'=16,'blk'=8] {'leaf'}, dimensions={0} | all-to-all | bytes 1048576 | tf_op jit(solution)/shard_map/all_to_all | solution.py:148
  186.5 3.7 %fusion.17 = f32[1024,128]{0,1:T(8,128)} fusion(bf16[2048,128]{1,0:T(8,128)(2,1)S(1)} %bitcast.188, bf16[1,1,2048,1024]{3,2,1,0:T(8,128)(2,1)} %param.12), kind=kOutput, calls=%fused_computation.16 | convolution fusion | flops 536870912 | bytes 5242880 | tf_op jit(solution)/shard_map/dot_general | solution.py:199
  196.1 5.0 %collective-permute-done.10 = bf16[4,128,128]{2,1,0:T(8,128)(2,1)S(1)} collective-permute-done((bf16[4,128,128]{2,1,0:T(8,128)(2,1)S(1)}, bf16[4,128,128]{2,1,0:T(8,128)(2,1)S(1)}, u32[]{:S(2)}, u32[]{:S(2)}) %collective-permute-start.10) | collective-permute-done | bytes 131104 | tf_op jit(solution)/shard_map/ppermute | solution.py:144
  204.1 4.8 %collective-permute-done.11 = bf16[4,128,128]{2,1,0:T(8,128)(2,1)} collective-permute-done((bf16[4,128,128]{2,1,0:T(8,128)(2,1)}, bf16[4,128,128]{2,1,0:T(8,128)(2,1)}, u32[]{:S(2)}, u32[]{:S(2)}) %collective-permute-start.11) | collective-permute-done | bytes 131104 | tf_op jit(solution)/shard_map/ppermute | solution.py:144
  210.4 29.5 %all_to_all.62 = bf16[16,4,128,128]{3,2,1,0:T(8,128)(2,1)S(1)} all-to-all(bf16[16,4,128,128]{3,2,1,0:T(8,128)(2,1)S(1)} %broadcast_in_dim.17), channel_id=1, replica_groups=mesh['leaf'=16,'blk'=8] {'leaf'}, dimensions={0} | all-to-all | bytes 4194304 | tf_op jit(solution)/shard_map/all_to_all | solution.py:148
  240.1 4.1 %collective-permute-done.12.other = bf16[64,128,128]{2,1,0:T(8,128)(2,1)S(1)} collective-permute-done((bf16[64,128,128]{2,1,0:T(8,128)(2,1)S(1)}, bf16[64,128,128]{2,1,0:T(8,128)(2,1)S(1)}, u32[]{:S(2)}, u32[]{:S(2)}) %collective-permute-start.12) | collective-permute-done | bytes 2097184 | tf_op jit(solution)/shard_map/ppermute | solution.py:137
  244.1 4.4 %pull.3 = f32[128,128]{1,0:T(8,128)S(1)} custom-call(s32[2]{0:T(128)S(1)} %pad_add_fusion.2.info, s32[2,64]{1,0:T(2,128)S(1)} %copy-done.10, bf16[64,128,128]{2,1,0:T(8,128)(2,1)S(1)} %bitcast.179, bf16[64,128,128]{2,1,0:T(8,128)(2,1)S(1)} %collective-permute-done.12.other, bf16[128,8192]{1,0:T(8,128)(2,1)} %factor.3), custom_call_target="tpu_custom_call" | custom-call | tf_op jit(solution)/shard_map/pull/pallas_call | solution.py:82
  248.6 10.3 %all_to_all.63 = bf16[8,128,128]{2,1,0:T(8,128)(2,1)S(1)} all-to-all(bf16[8,128,128]{2,1,0:T(8,128)(2,1)S(1)} %broadcast_in_dim.18), channel_id=1, replica_groups={{0,8,16,24,32,40,48,56},{64,72,80,88,96,104,112,120},{1,9,17,25,33,41,4..., dimensions={0} | all-to-all | bytes 524288 | tf_op jit(solution)/shard_map/all_to_all | solution.py:148
  266.3 4.6 %collective-permute-done.14 = bf16[4,128,128]{2,1,0:T(8,128)(2,1)S(1)} collective-permute-done((bf16[4,128,128]{2,1,0:T(8,128)(2,1)S(1)}, bf16[4,128,128]{2,1,0:T(8,128)(2,1)S(1)}, u32[]{:S(2)}, u32[]{:S(2)}) %collective-permute-start.14) | collective-permute-done | bytes 131104 | tf_op jit(solution)/shard_map/ppermute | solution.py:144
  274.0 4.7 %collective-permute-done.15 = bf16[4,128,128]{2,1,0:T(8,128)(2,1)} collective-permute-done((bf16[4,128,128]{2,1,0:T(8,128)(2,1)}, bf16[4,128,128]{2,1,0:T(8,128)(2,1)}, u32[]{:S(2)}, u32[]{:S(2)}) %collective-permute-start.15) | collective-permute-done | bytes 131104 | tf_op jit(solution)/shard_map/ppermute | solution.py:144
  280.0 17.1 %all_to_all.64 = bf16[8,4,128,128]{3,2,1,0:T(8,128)(2,1)} all-to-all(bf16[8,4,128,128]{3,2,1,0:T(8,128)(2,1)S(1)} %broadcast_in_dim.19), channel_id=1, replica_groups={{0,8,16,24,32,40,48,56},{64,72,80,88,96,104,112,120},{1,9,17,25,33,41,4..., dimensions={0} | all-to-all | bytes 2097152 | tf_op jit(solution)/shard_map/all_to_all | solution.py:148
  309.6 6.1 %all-to-all-done.10 = bf16[4,128,128]{2,1,0:T(8,128)(2,1)S(1)} async-done(((bf16[4,128,128]{2,1,0:T(8,128)(2,1)}), bf16[4,128,128]{2,1,0:T(8,128)(2,1)S(1)}, u32[]{:S(2)}, u32[]{:S(2)}) %all-to-all-start.10) | async-done | bytes 131104 | tf_op jit(solution)/shard_map/all_to_all | solution.py:148
  320.3 3.3 %all-to-all-start.11 = ((bf16[4,128,128]{2,1,0:T(8,128)(2,1)}), bf16[4,128,128]{2,1,0:T(8,128)(2,1)S(1)}, u32[]{:S(2)}, u32[]{:S(2)}) async-start(bf16[4,128,128]{2,1,0:T(8,128)(2,1)} %fusion.29), calls=%async_computation.11 | async-start | bytes 262144 | tf_op jit(solution)/shard_map/all_to_all | solution.py:237
  324.4 5.4 %all-to-all-done.11 = bf16[4,128,128]{2,1,0:T(8,128)(2,1)S(1)} async-done(((bf16[4,128,128]{2,1,0:T(8,128)(2,1)}), bf16[4,128,128]{2,1,0:T(8,128)(2,1)S(1)}, u32[]{:S(2)}, u32[]{:S(2)}) %all-to-all-start.11) | async-done | bytes 131104 | tf_op jit(solution)/shard_map/all_to_all | solution.py:237
  (147 shorter events, 73.7 us)
Async XLA Ops:
  0.6 65.9 %copy-start = (bf16[1,1,1024,1024]{3,2,1,0:T(8,128)(2,1)S(1)}, bf16[1,1,1024,1024]{3,2,1,0:T(8,128)(2,1)}, u32[]{:S(2)}) copy-start(bf16[1,1,1024,1024]{3,2,1,0:T(8,128)(2,1)} %param.13) | copy-start | bytes 6291460
  0.6 26.4 %copy-start.9 = (s32[4,32]{1,0:T(4,128)S(1)}, s32[4,32]{1,0:T(4,128)}, u32[]{:S(2)}) copy-start(s32[4,32]{1,0:T(4,128)} %pattern.5) | copy-start | bytes 1540
  0.7 26.4 %copy-start.6 = (bf16[128,4096]{1,0:T(8,128)(2,1)S(1)}, bf16[128,4096]{1,0:T(8,128)(2,1)}, u32[]{:S(2)}) copy-start(bf16[128,4096]{1,0:T(8,128)(2,1)} %factor.5) | copy-start | bytes 3145732
  11.8 2.0 collective-permute-start
  16.3 10.4 %all-to-all-start.1 = ((bf16[4,128,128]{1,2,0:T(8,128)(2,1)}), bf16[4,128,128]{1,2,0:T(8,128)(2,1)S(1)}, u32[]{:S(2)}, u32[]{:S(2)}) async-start(bf16[4,128,128]{1,2,0:T(8,128)(2,1)} %bitcast.177), calls=%async_computation.1 | async-start | bytes 262144 | tf_op jit(solution)/shard_map/all_to_all | solution.py:148
  29.2 2.7 collective-permute-start.1
  33.3 19.8 %all-to-all-start.2 = ((bf16[8,4,128,128]{3,2,1,0:T(8,128)(2,1)}), bf16[8,4,128,128]{3,2,1,0:T(8,128)(2,1)S(1)}, u32[]{:S(2)}, u32[]{:S(2)}) async-start(bf16[8,4,128,128]{3,2,1,0:T(8,128)(2,1)} %bitcast.15), calls=%async_computation.2 | async-start | bytes 2097152 | tf_op jit(solution)/shard_map/all_to_all | solution.py:148
  53.3 5.0 %collective-permute-start.2 = (bf16[4,128,128]{2,1,0:T(8,128)(2,1)S(1)}, bf16[4,128,128]{2,1,0:T(8,128)(2,1)S(1)}, u32[]{:S(2)}, u32[]{:S(2)}) collective-permute-start(bf16[4,128,128]{2,1,0:T(8,128)(2,1)S(1)} %fusion.31), channel_id=1, source_target_pairs={{0,2},{1,7},{2,0},{3,5},{4,6},{5,3},{6,4},{7,1},{8,10},{9,15},{10,... | collective-permute-start | bytes 393224 | tf_op jit(solution)/shard_map/ppermute | solution.py:144
  58.5 6.3 %collective-permute-start.3 = (bf16[4,128,128]{2,1,0:T(8,128)(2,1)S(1)}, bf16[4,128,128]{2,1,0:T(8,128)(2,1)S(1)}, u32[]{:S(2)}, u32[]{:S(2)}) collective-permute-start(bf16[4,128,128]{2,1,0:T(8,128)(2,1)S(1)} %fusion.34), channel_id=1, source_target_pairs={{0,6},{1,3},{2,4},{3,1},{4,2},{5,7},{6,0},{7,5},{8,14},{9,11},{10,... | collective-permute-start | bytes 393224 | tf_op jit(solution)/shard_map/ppermute | solution.py:144
  64.9 1.4 collective-permute-start.4
  66.6 15.2 %copy-start.5 = (bf16[128,4096]{1,0:T(8,128)(2,1)S(1)}, bf16[128,4096]{1,0:T(8,128)(2,1)}, u32[]{:S(2)}) copy-start(bf16[128,4096]{1,0:T(8,128)(2,1)} %factor.4) | copy-start | bytes 3145732
  68.2 11.2 %all-to-all-start.3 = ((bf16[8,128,128]{1,2,0:T(8,128)(2,1)}), bf16[8,128,128]{1,2,0:T(8,128)(2,1)S(1)}, u32[]{:S(2)}, u32[]{:S(2)}) async-start(bf16[8,128,128]{1,2,0:T(8,128)(2,1)} %bitcast.193), calls=%async_computation.3 | async-start | bytes 524288 | tf_op jit(solution)/shard_map/all_to_all | solution.py:148
  87.5 4.2 %collective-permute-start.5 = (bf16[64,128,128]{2,1,0:T(8,128)(2,1)S(1)}, bf16[64,128,128]{2,1,0:T(8,128)(2,1)S(1)}, u32[]{:S(2)}, u32[]{:S(2)}) collective-permute-start(bf16[64,128,128]{2,1,0:T(8,128)(2,1)S(1)} %get-tuple-element.9), channel_id=1, source_target_pairs={{0,1},{1,0},{2,3},{3,2},{4,5},{5,4},{6,7},{7,6},{8,9},{9,8},{10,11... | collective-permute-start | bytes 6291464 | tf_op jit(solution)/shard_map/ppermute | solution.py:137
  94.2 38.9 %all-to-all-start.4 = ((bf16[16,4,128,128]{3,2,1,0:T(8,128)(2,1)}), bf16[16,4,128,128]{3,2,1,0:T(8,128)(2,1)}, u32[]{:S(2)}, u32[]{:S(2)}) async-start(bf16[16,4,128,128]{3,2,1,0:T(8,128)(2,1)} %bitcast.181), calls=%async_computation.4 | async-start | bytes 4194304 | tf_op jit(solution)/shard_map/all_to_all | solution.py:148
  135.2 5.0 %collective-permute-start.6 = (bf16[4,128,128]{2,1,0:T(8,128)(2,1)S(1)}, bf16[4,128,128]{2,1,0:T(8,128)(2,1)S(1)}, u32[]{:S(2)}, u32[]{:S(2)}) collective-permute-start(bf16[4,128,128]{2,1,0:T(8,128)(2,1)S(1)} %fusion.30), channel_id=1, source_target_pairs={{0,2},{1,7},{2,0},{3,5},{4,6},{5,3},{6,4},{7,1},{8,10},{9,15},{10,... | collective-permute-start | bytes 393224 | tf_op jit(solution)/shard_map/ppermute | solution.py:144
  140.3 6.3 %collective-permute-start.7 = (bf16[4,128,128]{2,1,0:T(8,128)(2,1)S(1)}, bf16[4,128,128]{2,1,0:T(8,128)(2,1)S(1)}, u32[]{:S(2)}, u32[]{:S(2)}) collective-permute-start(bf16[4,128,128]{2,1,0:T(8,128)(2,1)S(1)} %fusion.35), channel_id=1, source_target_pairs={{0,6},{1,3},{2,4},{3,1},{4,2},{5,7},{6,0},{7,5},{8,14},{9,11},{10,... | collective-permute-start | bytes 393224 | tf_op jit(solution)/shard_map/ppermute | solution.py:144
  146.7 1.4 collective-permute-start.8
  154.7 16.4 %all-to-all-start.5 = ((bf16[16,128,128]{1,2,0:T(8,128)(2,1)}), bf16[16,128,128]{1,2,0:T(8,128)(2,1)}, u32[]{:S(2)}, u32[]{:S(2)}) async-start(bf16[16,128,128]{1,2,0:T(8,128)(2,1)} %bitcast.189), calls=%async_computation.5 | async-start | bytes 1048576 | tf_op jit(solution)/shard_map/all_to_all | solution.py:148
  172.3 17.9 %copy-start.16 = (f32[128,128]{1,0:T(8,128)}, f32[128,128]{1,0:T(8,128)S(1)}, u32[]{:S(2)}) copy-start(f32[128,128]{1,0:T(8,128)S(1)} %copy.70) | copy-start | bytes 196612
  193.3 1.4 collective-permute-start.9
  195.8 5.2 %collective-permute-start.10 = (bf16[4,128,128]{2,1,0:T(8,128)(2,1)S(1)}, bf16[4,128,128]{2,1,0:T(8,128)(2,1)S(1)}, u32[]{:S(2)}, u32[]{:S(2)}) collective-permute-start(bf16[4,128,128]{2,1,0:T(8,128)(2,1)S(1)} %get-tuple-element.12), channel_id=1, source_target_pairs={{0,2},{1,7},{2,0},{3,5},{4,6},{5,3},{6,4},{7,1},{8,10},{9,15},{10,... | collective-permute-start | bytes 393224 | tf_op jit(solution)/shard_map/ppermute | solution.py:144
  202.4 6.5 %collective-permute-start.11 = (bf16[4,128,128]{2,1,0:T(8,128)(2,1)}, bf16[4,128,128]{2,1,0:T(8,128)(2,1)}, u32[]{:S(2)}, u32[]{:S(2)}) collective-permute-start(bf16[4,128,128]{2,1,0:T(8,128)(2,1)} %fusion.32), channel_id=1, source_target_pairs={{0,6},{1,3},{2,4},{3,1},{4,2},{5,7},{6,0},{7,5},{8,14},{9,11},{10,... | collective-permute-start | bytes 393224 | tf_op jit(solution)/shard_map/ppermute | solution.py:144
  209.9 30.0 %copy-start.14 = (bf16[4,128,128]{2,1,0:T(8,128)(2,1)}, bf16[4,128,128]{2,1,0:T(8,128)(2,1)S(1)}, u32[]{:S(2)}) copy-start(bf16[4,128,128]{2,1,0:T(8,128)(2,1)S(1)} %multiply_convert_fusion.1) | copy-start | bytes 393220
  240.0 4.2 %collective-permute-start.12 = (bf16[64,128,128]{2,1,0:T(8,128)(2,1)S(1)}, bf16[64,128,128]{2,1,0:T(8,128)(2,1)S(1)}, u32[]{:S(2)}, u32[]{:S(2)}) collective-permute-start(bf16[64,128,128]{2,1,0:T(8,128)(2,1)S(1)} %bitcast.178), channel_id=1, source_target_pairs={{0,1},{1,0},{2,3},{3,2},{4,5},{5,4},{6,7},{7,6},{8,9},{9,8},{10,11... | collective-permute-start | bytes 6291464 | tf_op jit(solution)/shard_map/ppermute | solution.py:137
  263.3 1.4 collective-permute-start.13
  265.8 5.0 %collective-permute-start.14 = (bf16[4,128,128]{2,1,0:T(8,128)(2,1)S(1)}, bf16[4,128,128]{2,1,0:T(8,128)(2,1)S(1)}, u32[]{:S(2)}, u32[]{:S(2)}) collective-permute-start(bf16[4,128,128]{2,1,0:T(8,128)(2,1)S(1)} %get-tuple-element.10), channel_id=1, source_target_pairs={{0,2},{1,7},{2,0},{3,5},{4,6},{5,3},{6,4},{7,1},{8,10},{9,15},{10,... | collective-permute-start | bytes 393224 | tf_op jit(solution)/shard_map/ppermute | solution.py:144
  272.2 6.5 %collective-permute-start.15 = (bf16[4,128,128]{2,1,0:T(8,128)(2,1)}, bf16[4,128,128]{2,1,0:T(8,128)(2,1)}, u32[]{:S(2)}, u32[]{:S(2)}) collective-permute-start(bf16[4,128,128]{2,1,0:T(8,128)(2,1)} %fusion.33), channel_id=1, source_target_pairs={{0,6},{1,3},{2,4},{3,1},{4,2},{5,7},{6,0},{7,5},{8,14},{9,11},{10,... | collective-permute-start | bytes 393224 | tf_op jit(solution)/shard_map/ppermute | solution.py:144
  279.7 17.4 %copy-start.15 = (bf16[4,128,128]{2,1,0:T(8,128)(2,1)}, bf16[4,128,128]{2,1,0:T(8,128)(2,1)S(1)}, u32[]{:S(2)}) copy-start(bf16[4,128,128]{2,1,0:T(8,128)(2,1)S(1)} %multiply_convert_fusion) | copy-start | bytes 393220
  297.1 5.7 %collective-permute-start.16 = (bf16[32,128,128]{2,1,0:T(8,128)(2,1)}, bf16[32,128,128]{2,1,0:T(8,128)(2,1)}, u32[]{:S(2)}, u32[]{:S(2)}) collective-permute-start(bf16[32,128,128]{2,1,0:T(8,128)(2,1)} %bitcast.48.own), channel_id=1, source_target_pairs={{0,1},{1,0},{2,3},{3,2},{4,5},{5,4},{6,7},{7,6},{8,9},{9,8},{10,11... | collective-permute-start | bytes 3145736 | tf_op jit(solution)/shard_map/ppermute | solution.py:137
  306.3 9.5 %all-to-all-start.10 = ((bf16[4,128,128]{2,1,0:T(8,128)(2,1)}), bf16[4,128,128]{2,1,0:T(8,128)(2,1)S(1)}, u32[]{:S(2)}, u32[]{:S(2)}) async-start(bf16[4,128,128]{2,1,0:T(8,128)(2,1)} %broadcast_in_dim.20), calls=%async_computation.10 | async-start | bytes 262144 | tf_op jit(solution)/shard_map/all_to_all | solution.py:148
  318.1 1.5 collective-permute-start.17
  320.3 9.5 %all-to-all-start.11 = ((bf16[4,128,128]{2,1,0:T(8,128)(2,1)}), bf16[4,128,128]{2,1,0:T(8,128)(2,1)S(1)}, u32[]{:S(2)}, u32[]{:S(2)}) async-start(bf16[4,128,128]{2,1,0:T(8,128)(2,1)} %fusion.29), calls=%async_computation.11 | async-start | bytes 262144 | tf_op jit(solution)/shard_map/all_to_all | solution.py:237
  (14 other events, 84.4 us)

commit v2 on v1

v2 whole, which is shorter than its diff:
```python
import functools

import jax
import jax.numpy as jnp
from jax import lax
from jax.experimental import pallas as pl
from jax.experimental.pallas import tpu as pltpu
from jax.sharding import PartitionSpec as P

BF16 = jnp.bfloat16
F32 = jnp.float32
MIB = 1024 * 1024
SMEM = pl.BlockSpec(memory_space=pltpu.SMEM)
VMEM = pl.BlockSpec(memory_space=pltpu.VMEM)
CORE, NODE_MIDDLE, NODE_LOWER, LIVE_MIDDLE, LIVE_LOWER = range(5)


def call(kernel, name, out_shape, smem, vmem, scratch=(), limit=24):
    return pl.pallas_call(
        kernel,
        out_shape=out_shape,
        in_specs=[SMEM] * len(smem) + [VMEM] * len(vmem),
        out_specs=jax.tree.map(lambda _: VMEM, out_shape),
        scratch_shapes=list(scratch),
        compiler_params=pltpu.CompilerParams(vmem_limit_bytes=limit * MIB),
        name=name,
    )(*smem, *vmem)


def blocks(count, dtype=BF16):
    return jax.ShapeDtypeStruct((count, 128, 128), dtype)


BLOCK = jax.ShapeDtypeStruct((128, 128), BF16)


def total_of(parts):
    total = parts[0].astype(F32)
    for index in range(1, parts.shape[0]):
        total = total + parts[index].astype(F32)
    return total


def multiply_kernel(transposed, info, own, other, tile, out, columns):
    first = info[CORE] == 0
    for chip in range(own.shape[0]):
        mine, theirs = own[chip], other[chip]
        for core in range(2):
            block = jnp.where(first == (core == 0), mine, theirs)
            row = (2 * chip + core) * 128
            columns[row : row + 128, :] = block.T if transposed else block
    for group in range(out.shape[0]):
        rows = tile[group * 128 : group * 128 + 128, :]
        out[group] = jnp.dot(rows, columns[...], preferred_element_type=F32).astype(BF16)


def multiply(info, own, other, tile, transposed):
    count = tile.shape[0] // 128
    return call(
        functools.partial(multiply_kernel, transposed),
        "multiply",
        blocks(count),
        [info],
        [own, other, tile],
        [pltpu.VMEM((tile.shape[1], 128), BF16)],
    )


def transposed_kernel(info, gathered, tile, mine, theirs):
    first = info[CORE] == 0
    rows = jnp.concatenate([gathered[a] for a in range(gathered.shape[0])], axis=1)
    for chip in range(mine.shape[0]):
        column = chip * 256
        product = jnp.dot(rows, tile[:, column : column + 256], preferred_element_type=F32)
        even, odd = product[:, :128].T, product[:, 128:].T
        mine[chip] = jnp.where(first, even, odd)
        theirs[chip] = jnp.where(first, odd, even).astype(BF16)


def multiply_transposed(info, gathered, tile):
    chips = tile.shape[1] // 256
    return call(
        transposed_kernel,
        "multiply_transposed",
        (blocks(chips, F32), blocks(chips)),
        [info],
        [gathered, tile],
    )


def lift_kernel(spans, nodes, live, info, *refs):
    total = len(spans)
    patterns, refs = refs[:total], refs[total:]
    parts, refs = refs[0], refs[1:]
    earlier, refs = refs[: total - 1], refs[total - 1 :]
    factors, (solved, keep, send, sums) = refs[:total], refs[total:]
    core = info[CORE]
    half = keep.shape[0]
    value = (total_of(parts) * info[live].astype(F32)).astype(BF16)
    solved[...] = value
    values = [value.T] + [e[...].T for e in earlier]
    sums[...] = jnp.zeros_like(sums)
    for index, span in enumerate(spans):
        node = info[nodes[index]]

        def chunk(step, carry, index=index, node=node):
            start = pl.multiple_of(step * 1024, 1024)
            product = jnp.dot(
                values[index], factors[index][:, pl.ds(start, 1024)], preferred_element_type=F32
            )
            for part in range(8):
                block = patterns[index][node, step * 8 + part]
                slot = ((block & 1) ^ core) * half + (block >> 1)
                sums[slot] += product[:, part * 128 : part * 128 + 128]
            return carry

        lax.fori_loop(0, span // 1024, chunk, 0)

    def emit(slot, carry):
        keep[slot] = sums[slot].astype(BF16)
        send[slot] = sums[half + slot].astype(BF16)
        return carry

    lax.fori_loop(0, half, emit, 0)


def lift(info, live, nodes, patterns, parts, earlier, factors, half):
    spans = tuple(f.shape[1] for f in factors)
    return call(
        functools.partial(lift_kernel, spans, nodes, live),
        "lift",
        (BLOCK, blocks(half), blocks(half)),
        [info, *patterns],
        [parts, *earlier, *factors],
        [pltpu.VMEM((2 * half, 128, 128), F32)],
    )


def root_kernel(parts, middle, lower, forward, copies):
    value = total_of(parts).astype(BF16)
    forward[0] = value
    forward[1] = middle[...]
    forward[2] = lower[...]
    turned = value.T
    for index in range(copies.shape[0]):
        copies[index] = turned


def pick_blocks(info, node, pattern, own, other, chosen):
    core, row_of = info[CORE], info[node]

    def pick(position, carry):
        block = pattern[row_of, position]
        mine = (block & 1) == core
        row = pl.multiple_of(position * 128, 128)
        chosen[pl.ds(row, 128), :] = jnp.where(mine, own[block >> 1], other[block >> 1])
        return carry

    lax.fori_loop(0, pattern.shape[1], pick, 0, unroll=4)


def pull_kernel(node, info, pattern, own, other, factor, out, chosen):
    pick_blocks(info, node, pattern, own, other, chosen)
    out[...] = jnp.dot(factor[...], chosen[...], preferred_element_type=F32)


def reduce_kernel(node, earlier, info, pattern, own, other, factor, solved, *refs):
    copies, chosen = refs[-2:]
    pick_blocks(info, node, pattern, own, other, chosen)
    pulled = jnp.dot(factor[...], chosen[...], preferred_element_type=F32)
    if earlier:
        pulled = pulled + refs[0][...]
    turned = (solved[...].astype(F32) - pulled).astype(BF16).T
    for index in range(copies.shape[0]):
        copies[index] = turned


def pull(info, node, pattern, own, other, factor):
    return call(
        functools.partial(pull_kernel, node),
        "pull",
        jax.ShapeDtypeStruct((128, 128), F32),
        [info, pattern],
        [own, other, factor],
        [pltpu.VMEM((factor.shape[1], 128), BF16)],
    )


def reduced(info, node, pattern, own, other, factor, solved, earlier, count):
    return call(
        functools.partial(reduce_kernel, node, bool(earlier)),
        "reduced",
        blocks(count),
        [info, pattern],
        [own, other, factor, solved, *earlier],
        [pltpu.VMEM((factor.shape[1], 128), BF16)],
    )


def last_kernel(info, parts, root, middle, out):
    out[0] = root[...]
    out[1] = middle[...]
    out[2] = (total_of(parts) * info[LIVE_LOWER].astype(F32)).astype(BF16)


def shards(
    loads,
    inverse_root,
    inverse_middle,
    inverse_lower,
    couple_middle,
    couple_lower,
    couple_between,
    pattern_middle,
    pattern_lower,
    pattern_between,
    node_blocks,
):
    leaf_count = lax.axis_size("leaf")
    block_count = lax.axis_size("blk")
    chip_count = block_count // 2
    leaf_index = lax.axis_index("leaf")
    block_index = lax.axis_index("blk")
    core = block_index & 1
    chip = block_index >> 1
    leaf_bits = leaf_count.bit_length() - 1

    def node_of(level):
        return leaf_index >> (leaf_bits - level)

    def leaf_groups(level):
        size = leaf_count >> level
        return [[g * size + j for j in range(size)] for g in range(1 << level)]

    chip_groups = [[2 * x + c for x in range(chip_count)] for c in range(2)]

    def live(level, lane):
        position = (leaf_index & ((leaf_count >> level) - 1)) * block_count + lane
        return position < node_blocks[2**level - 1 + node_of(level)]

    def swap_core(value):
        return lax.ppermute(value, "blk", [(i, i ^ 1) for i in range(block_count)])

    def swap_chip(value, first):
        pairs = []
        for i in range(block_count):
            near = (i & 1 == 0) == first
            pairs.append((i, i ^ (2 if near else 6)))
        return lax.ppermute(value, "blk", pairs)

    info = jnp.stack(
        [core, node_of(1), node_of(2), live(1, block_index), live(2, block_index)]
    ).astype(jnp.int32)
    chip_mask = (jnp.arange(chip_count) == chip).astype(F32)[:, None, None]
    live_middle = live(1, 2 * jnp.arange(chip_count) + core).astype(F32)[:, None, None]
    kept = {
        "info": info,
        "chip_mask": chip_mask,
        "live_middle": live_middle,
        "load_middle": loads[1].T,
        "load_root": loads[0].T,
    }

    def fence(value):
        tied, held = lax.optimization_barrier((value, dict(kept)))
        kept.update(held)
        return tied

    def exchange(value, axis, groups):
        value = fence(value)
        value = lax.all_to_all(value, axis, 0, 0, tiled=True, axis_index_groups=groups)
        return fence(value)

    def over_leaf(value, level):
        return exchange(value, "leaf", leaf_groups(level) if level else None)

    def sum_chips(value):
        for first in (True, False):
            value = (value.astype(F32) + swap_chip(value, first).astype(F32)).astype(BF16)
        return value

    def residual(load, level):
        size = leaf_count >> level
        keep, send = kept.pop("keep"), kept.pop("send")
        summed = (keep.astype(F32) + swap_core(send).astype(F32)).astype(BF16)
        partial_sum = over_leaf(summed.reshape(size, chip_count, 128, 128), level)
        partial_sum = partial_sum.astype(F32).sum(0)
        rest = sum_chips((kept["chip_mask"] * kept[load][None] - partial_sum).astype(BF16))
        return rest, swap_core(rest)

    def backward(gathered, tile):
        mine, theirs = multiply_transposed(kept["info"], gathered, tile)
        return (mine + swap_core(theirs).astype(F32)).astype(BF16)

    def own_chip(value):
        return lax.dynamic_index_in_dim(value, chip, 0, keepdims=False)

    tile_root, tile_middle, tile_lower = inverse_root[0, 0], inverse_middle[0, 0], inverse_lower[0, 0]

    load_lower = loads[2].astype(BF16)
    own = exchange(
        jnp.broadcast_to(load_lower[None], (chip_count, 128, 128)), "blk", chip_groups
    )
    parts = over_leaf(multiply(kept["info"], own, swap_core(own), tile_lower, False), 2)
    y_lower, kept["keep"], kept["send"] = lift(
        kept["info"], LIVE_LOWER, (NODE_LOWER,), [pattern_between], parts, [],
        [couple_between], (leaf_count >> 1) * chip_count,
    )
    kept["y_lower"] = y_lower
    own, other = residual("load_middle", 1)
    parts = over_leaf(multiply(kept["info"], own, other, tile_middle, True), 1)
    y_middle, kept["keep"], kept["send"] = lift(
        kept["info"], LIVE_MIDDLE, (NODE_MIDDLE, NODE_LOWER), [pattern_middle, pattern_lower],
        parts, [kept["y_lower"]], [couple_middle, couple_lower], leaf_count * chip_count,
    )
    kept["y_middle"] = y_middle
    own, other = residual("load_root", 0)
    parts = over_leaf(multiply(kept["info"], own, other, tile_root, True), 0)
    forward, copies = call(
        root_kernel, "root", (blocks(3), blocks(leaf_count)), [],
        [parts, kept["y_middle"], kept["y_lower"]],
    )
    kept["forward"] = forward
    x_root = sum_chips(backward(over_leaf(copies, 0), tile_root))
    kept["x_root"] = own_chip(x_root)
    own = over_leaf(jnp.broadcast_to(x_root[None], (leaf_count,) + x_root.shape), 0)
    own = own.reshape(-1, 128, 128)
    other = swap_core(own)
    copies = reduced(
        kept["info"], NODE_MIDDLE, pattern_middle, own, other, couple_middle,
        kept["y_middle"], [], leaf_count >> 1,
    )
    kept["own_root"], kept["other_root"] = own, other
    x_middle = sum_chips(backward(over_leaf(copies, 1), tile_middle))
    x_middle = (x_middle * kept["live_middle"]).astype(BF16)
    kept["x_middle"] = own_chip(x_middle)
    own = over_leaf(jnp.broadcast_to(x_middle[None], (leaf_count >> 1,) + x_middle.shape), 1)
    own = own.reshape(-1, 128, 128)
    other = swap_core(own)
    pulled = pull(
        kept["info"], NODE_LOWER, pattern_lower, kept.pop("own_root"), kept.pop("other_root"),
        couple_lower,
    )
    copies = reduced(
        kept["info"], NODE_LOWER, pattern_between, own, other, couple_between,
        kept["y_lower"], [pulled], leaf_count >> 2,
    )
    x_lower = backward(over_leaf(copies, 2), tile_lower)
    parts = exchange(x_lower, "blk", chip_groups)
    answer = call(
        last_kernel, "last", blocks(3), [kept["info"]],
        [parts, kept["x_root"], kept["x_middle"]],
    )
    return (kept["forward"], answer)


def solution(mesh):
    in_specs = (
        P(None, ("leaf", "blk"), None),
        P("leaf", "blk", None, None),
        P("leaf", "blk", None, None),
        P("leaf", "blk", None, None),
        P(("leaf", "blk"), None),
        P(("leaf", "blk"), None),
        P(("leaf", "blk"), None),
        P(),
        P(),
        P(),
        P(),
    )
    out_specs = (P(None, ("leaf", "blk"), None), P(None, ("leaf", "blk"), None))
    return jax.shard_map(shards, mesh=mesh, in_specs=in_specs, out_specs=out_specs, check_vma=False)
```

time: 333 us -> 292 us (0.88)
  blocking collectives: 81.1 us -> 186 us
  waiting for transfers between devices: 138 us -> 59.1 us
  starting transfers between devices: 35.4 us -> 7.07 us
  other arithmetic: 21.4 us -> 3.98 us
  matrix products: 12.3 us -> 0 us
  local copies, waits for them, and re-layouts: 22.7 us -> 11.4 us
  Pallas kernels: 16.6 us -> 21.4 us
    all_to_all x5 -> x12, blocking collectives: 81.1 us -> 186 us  [exchange(): lax.all_to_all(value, axis, 0, 0, tiled=True, axis_index_groups=groups)]
    all_to_all x7 -> x0, waiting for transfers between devices: 83.3 us -> none  [the longest x6 77.9 us: exchange(): lax.all_to_all(value, 'leaf', 0, 0, tiled=True, axis_index_groups=groups)]
    all_to_all x7 -> x0, starting transfers between devices: 28.5 us -> none  [the longest x6 25.2 us: exchange(): lax.all_to_all(value, 'leaf', 0, 0, tiled=True, axis_index_groups=groups)]
    dot_general x6 -> x0, matrix products: 12.3 us -> none  [the longest x3 6.25 us: forward_solve(): jnp.dot(tile[0, 0], columns.reshape(-1, 128), preferred_element_type=F32)]
    convert_element_type x28 -> x14, other arithmetic: 11.3 us -> 2.01 us  [the longest x1 1.21 us: shards(): live(1, 2 * jnp.arange(chip_count) + core).astype(F32)[:, None, None]]
    dot_general x3 -> x0, local copies, waits for them, and re-layouts: 5.36 us -> none  [backward_partial(): lax.dot_general(tile[0, 0], gathered, (((0,), (0,)), ((), ())), preferred...]
    pallas_call x5 -> x13, Pallas kernels: 16.6 us -> 21.4 us  [call(): pl.pallas_call(kernel, out_shape=out_shape, in_specs=[SMEM] * len(smem) +...]
    ppermute x10, waiting for transfers between devices: 16.2 us -> 20.2 us  [swap_core(): return lax.ppermute(value, 'blk', [(i, i ^ 1) for i in range(block_count)])]
  transfers between devices with their start and end apart: 25 -> 18, of which waited for: 22 -> 18; matrix products, arithmetic and copies ran while one was open for 2% -> 0% of each run, Pallas kernels for 1% -> 0%
where the time goes in v2:
time: 292 us; the launch traced here: 291 us
  blocking collectives  186 us (64%)
  waiting for transfers between devices  59.1 us (20%)
  Pallas kernels  21.4 us (7%)
  local copies, waits for them, and re-layouts  11.4 us (4%)
  starting transfers between devices  7.07 us (2%)
  other arithmetic  3.98 us (1%)
    all_to_all x12, blocking collectives, exchange(): lax.all_to_all(value, axis, 0, 0, tiled=True, axis_index_groups=groups)  186 us
    ppermute x8, waiting for transfers between devices, swap_chip(): return lax.ppermute(value, 'blk', pairs)  38.9 us
    pallas_call x13, Pallas kernels, call(): pl.pallas_call(kernel, out_shape=out_shape, in_specs=[SMEM] * len(smem) +...  21.4 us
    ppermute x10, waiting for transfers between devices, swap_core(): return lax.ppermute(value, 'blk', [(i, i ^ 1) for i in range(block_count)])  20.2 us
    ppermute x8, starting transfers between devices, swap_chip(): return lax.ppermute(value, 'blk', pairs)  6.47 us
  transfers between devices with their start and end apart: 18, of which 18 were waited for; matrix products, arithmetic and copies ran while one was open for 0% of the time, Pallas kernels for 0%

profile of v2, /device:TPU:0, one launch (start us, length us, event | category | flops | bytes accessed | tf_op | source)
XLA Modules:
  0.0 291.2 jit_solution(6489944896349743363)
XLA Ops:
  1.6 1.5 slice_bitcast_fusion
  7.0 10.2 %all_to_all.60.own = bf16[4,128,128]{2,1,0:T(8,128)(2,1)S(1)} all-to-all(bf16[4,128,128]{2,1,0:T(8,128)(2,1)S(1)} %broadcast_in_dim.9), channel_id=1, replica_groups={{0,2,4,6},{1,3,5,7},{8,10,12,14},{9,11,13,15},{16,18,20,22},{17,19,21,2..., dimensions={0} | all-to-all | bytes 262144 | tf_op jit(solution)/shard_map/all_to_all | solution.py:271
  20.7 10.2 %all_to_all.61.refs_1_ = bf16[4,128,128]{2,1,0:T(8,128)(2,1)S(1)} all-to-all(bf16[4,128,128]{2,1,0:T(8,128)(2,1)S(1)} %multiply.3), channel_id=1, replica_groups={{0,8,16,24},{32,40,48,56},{64,72,80,88},{96,104,112,120},{1,9,17,25},{3..., dimensions={0} | all-to-all | bytes 262144 | tf_op jit(solution)/shard_map/all_to_all | solution.py:271
  31.7 2.1 lift.2
  33.9 2.6 collective-permute-done.1
  36.9 19.6 %all_to_all.62 = bf16[8,4,128,128]{3,2,1,0:T(8,128)(2,1)S(1)} all-to-all(bf16[8,4,128,128]{3,2,1,0:T(8,128)(2,1)S(1)} %bitcast.43), channel_id=1, replica_groups={{0,8,16,24,32,40,48,56},{64,72,80,88,96,104,112,120},{1,9,17,25,33,41,4..., dimensions={0} | all-to-all | bytes 2097152 | tf_op jit(solution)/shard_map/all_to_all | solution.py:271
  57.6 4.4 %collective-permute-done.2 = bf16[4,128,128]{2,1,0:T(8,128)(2,1)S(1)} collective-permute-done((bf16[4,128,128]{2,1,0:T(8,128)(2,1)S(1)}, bf16[4,128,128]{2,1,0:T(8,128)(2,1)S(1)}, u32[]{:S(2)}, u32[]{:S(2)}) %collective-permute-start.2) | collective-permute-done | bytes 131104 | tf_op jit(solution)/shard_map/ppermute | solution.py:249
  63.3 5.0 %collective-permute-done.3 = bf16[4,128,128]{2,1,0:T(8,128)(2,1)S(1)} collective-permute-done((bf16[4,128,128]{2,1,0:T(8,128)(2,1)S(1)}, bf16[4,128,128]{2,1,0:T(8,128)(2,1)S(1)}, u32[]{:S(2)}, u32[]{:S(2)}) %collective-permute-start.3) | collective-permute-done | bytes 131104 | tf_op jit(solution)/shard_map/ppermute | solution.py:249
  69.8 1.6 copy-done.3
  72.8 10.3 %all_to_all.63.refs_2_ = bf16[8,128,128]{2,1,0:T(8,128)(2,1)S(1)} all-to-all(bf16[8,128,128]{2,1,0:T(8,128)(2,1)S(1)} %multiply.4), channel_id=1, replica_groups={{0,8,16,24,32,40,48,56},{64,72,80,88,96,104,112,120},{1,9,17,25,33,41,4..., dimensions={0} | all-to-all | bytes 524288 | tf_op jit(solution)/shard_map/all_to_all | solution.py:271
  83.1 4.7 %lift.3 = (bf16[128,128]{1,0:T(8,128)(2,1)S(1)}, bf16[64,128,128]{2,1,0:T(8,128)(2,1)S(1)}, bf16[64,128,128]{2,1,0:T(8,128)(2,1)S(1)}) custom-call(s32[5]{0:T(128)S(1)} %stack.31.info, s32[2,64]{1,0:T(2,128)S(1)} %copy-done.13, s32[4,32]{1,0:T(4,128)S(1)} %copy-done.10, bf16[8,128,128]{2,1,0:T(8,128)(2,1)S(1)} %all_to_all.63.refs_2_, ...), custom_call_target="tpu_custom_call" | custom-call | tf_op jit(solution)/shard_map/lift/pallas_call | solution.py:19
  87.8 4.1 %collective-permute-done.5 = bf16[64,128,128]{2,1,0:T(8,128)(2,1)S(1)} collective-permute-done((bf16[64,128,128]{2,1,0:T(8,128)(2,1)S(1)}, bf16[64,128,128]{2,1,0:T(8,128)(2,1)S(1)}, u32[]{:S(2)}, u32[]{:S(2)}) %collective-permute-start.5) | collective-permute-done | bytes 2097184 | tf_op jit(solution)/shard_map/ppermute | solution.py:242
  93.1 34.0 %all_to_all.64 = bf16[16,4,128,128]{3,2,1,0:T(8,128)(2,1)S(1)} all-to-all(bf16[16,4,128,128]{3,2,1,0:T(8,128)(2,1)S(1)} %bitcast.42), channel_id=1, replica_groups=mesh['leaf'=16,'blk'=8] {'leaf'}, dimensions={0} | all-to-all | bytes 4194304 | tf_op jit(solution)/shard_map/all_to_all | solution.py:271
  128.6 5.0 %collective-permute-done.6 = bf16[4,128,128]{2,1,0:T(8,128)(2,1)S(1)} collective-permute-done((bf16[4,128,128]{2,1,0:T(8,128)(2,1)S(1)}, bf16[4,128,128]{2,1,0:T(8,128)(2,1)S(1)}, u32[]{:S(2)}, u32[]{:S(2)}) %collective-permute-start.6) | collective-permute-done | bytes 131104 | tf_op jit(solution)/shard_map/ppermute | solution.py:249
  134.9 5.0 %collective-permute-done.7 = bf16[4,128,128]{2,1,0:T(8,128)(2,1)S(1)} collective-permute-done((bf16[4,128,128]{2,1,0:T(8,128)(2,1)S(1)}, bf16[4,128,128]{2,1,0:T(8,128)(2,1)S(1)}, u32[]{:S(2)}, u32[]{:S(2)}) %collective-permute-start.7) | collective-permute-done | bytes 131104 | tf_op jit(solution)/shard_map/ppermute | solution.py:249
  141.4 2.2 copy-done
  143.6 1.9 multiply.5
  145.5 14.8 %all_to_all.65.parts = bf16[16,128,128]{2,1,0:T(8,128)(2,1)S(1)} all-to-all(bf16[16,128,128]{2,1,0:T(8,128)(2,1)S(1)} %multiply.5), channel_id=1, replica_groups=mesh['leaf'=16,'blk'=8] {'leaf'}, dimensions={0} | all-to-all | bytes 1048576 | tf_op jit(solution)/shard_map/all_to_all | solution.py:271
  161.0 14.0 %all_to_all.66.gathered = bf16[16,128,128]{2,1,0:T(8,128)(2,1)S(1)} all-to-all(bf16[16,128,128]{2,1,0:T(8,128)(2,1)S(1)} %get-tuple-element.256), channel_id=1, replica_groups=mesh['leaf'=16,'blk'=8] {'leaf'}, dimensions={0} | all-to-all | bytes 1048576 | tf_op jit(solution)/shard_map/all_to_all | solution.py:271
  177.9 5.0 %collective-permute-done.10 = bf16[4,128,128]{2,1,0:T(8,128)(2,1)S(1)} collective-permute-done((bf16[4,128,128]{2,1,0:T(8,128)(2,1)S(1)}, bf16[4,128,128]{2,1,0:T(8,128)(2,1)S(1)}, u32[]{:S(2)}, u32[]{:S(2)}) %collective-permute-start.10) | collective-permute-done | bytes 131104 | tf_op jit(solution)/shard_map/ppermute | solution.py:249
  182.9 1.4 collective-permute-start.11
  184.4 5.0 %collective-permute-done.11 = bf16[4,128,128]{2,1,0:T(8,128)(2,1)S(1)} collective-permute-done((bf16[4,128,128]{2,1,0:T(8,128)(2,1)S(1)}, bf16[4,128,128]{2,1,0:T(8,128)(2,1)S(1)}, u32[]{:S(2)}, u32[]{:S(2)}) %collective-permute-start.11) | collective-permute-done | bytes 131104 | tf_op jit(solution)/shard_map/ppermute | solution.py:249
  189.9 29.5 %all_to_all.67 = bf16[16,4,128,128]{3,2,1,0:T(8,128)(2,1)S(1)} all-to-all(bf16[16,4,128,128]{3,2,1,0:T(8,128)(2,1)S(1)} %broadcast_in_dim.10), channel_id=1, replica_groups=mesh['leaf'=16,'blk'=8] {'leaf'}, dimensions={0} | all-to-all | bytes 4194304 | tf_op jit(solution)/shard_map/all_to_all | solution.py:271
  219.5 4.2 %collective-permute-done.12.other = bf16[64,128,128]{2,1,0:T(8,128)(2,1)S(1)} collective-permute-done((bf16[64,128,128]{2,1,0:T(8,128)(2,1)S(1)}, bf16[64,128,128]{2,1,0:T(8,128)(2,1)S(1)}, u32[]{:S(2)}, u32[]{:S(2)}) %collective-permute-start.12) | collective-permute-done | bytes 2097184 | tf_op jit(solution)/shard_map/ppermute | solution.py:242
  223.6 2.1 reduced.2
  225.8 10.3 %all_to_all.68.gathered = bf16[8,128,128]{2,1,0:T(8,128)(2,1)S(1)} all-to-all(bf16[8,128,128]{2,1,0:T(8,128)(2,1)S(1)} %reduced.2), channel_id=1, replica_groups={{0,8,16,24,32,40,48,56},{64,72,80,88,96,104,112,120},{1,9,17,25,33,41,4..., dimensions={0} | all-to-all | bytes 524288 | tf_op jit(solution)/shard_map/all_to_all | solution.py:271
  239.1 4.6 %collective-permute-done.14 = bf16[4,128,128]{2,1,0:T(8,128)(2,1)S(1)} collective-permute-done((bf16[4,128,128]{2,1,0:T(8,128)(2,1)S(1)}, bf16[4,128,128]{2,1,0:T(8,128)(2,1)S(1)}, u32[]{:S(2)}, u32[]{:S(2)}) %collective-permute-start.14) | collective-permute-done | bytes 131104 | tf_op jit(solution)/shard_map/ppermute | solution.py:249
  244.9 5.0 %collective-permute-done.15 = bf16[4,128,128]{2,1,0:T(8,128)(2,1)S(1)} collective-permute-done((bf16[4,128,128]{2,1,0:T(8,128)(2,1)S(1)}, bf16[4,128,128]{2,1,0:T(8,128)(2,1)S(1)}, u32[]{:S(2)}, u32[]{:S(2)}) %collective-permute-start.15) | collective-permute-done | bytes 131104 | tf_op jit(solution)/shard_map/ppermute | solution.py:249
  250.3 16.4 %all_to_all.69 = bf16[8,4,128,128]{3,2,1,0:T(8,128)(2,1)S(1)} all-to-all(bf16[8,4,128,128]{3,2,1,0:T(8,128)(2,1)S(1)} %broadcast_in_dim.11), channel_id=1, replica_groups={{0,8,16,24,32,40,48,56},{64,72,80,88,96,104,112,120},{1,9,17,25,33,41,4..., dimensions={0} | all-to-all | bytes 2097152 | tf_op jit(solution)/shard_map/all_to_all | solution.py:271
  269.4 1.5 reduced.3
  270.9 8.4 %all_to_all.70.gathered = bf16[4,128,128]{2,1,0:T(8,128)(2,1)S(1)} all-to-all(bf16[4,128,128]{2,1,0:T(8,128)(2,1)S(1)} %reduced.3), channel_id=1, replica_groups={{0,8,16,24},{32,40,48,56},{64,72,80,88},{96,104,112,120},{1,9,17,25},{3..., dimensions={0} | all-to-all | bytes 262144 | tf_op jit(solution)/shard_map/all_to_all | solution.py:271
  281.7 8.4 %all_to_all.71.parts = bf16[4,128,128]{2,1,0:T(8,128)(2,1)S(1)} all-to-all(bf16[4,128,128]{2,1,0:T(8,128)(2,1)S(1)} %add_convert_fusion.2), channel_id=1, replica_groups={{0,2,4,6},{1,3,5,7},{8,10,12,14},{9,11,13,15},{16,18,20,22},{17,19,21,2..., dimensions={0} | all-to-all | bytes 262144 | tf_op jit(solution)/shard_map/all_to_all | solution.py:271
  (88 shorter events, 34.1 us)
Async XLA Ops:
  0.6 30.4 %copy-start.6 = (bf16[128,4096]{1,0:T(8,128)(2,1)S(1)}, bf16[128,4096]{1,0:T(8,128)(2,1)}, u32[]{:S(2)}) copy-start(bf16[128,4096]{1,0:T(8,128)(2,1)} %factor.5) | copy-start | bytes 3145732
  17.2 1.3 collective-permute-start
  18.5 1.2 copy-start.8
  33.8 2.7 collective-permute-start.1
  56.5 26.5 %copy-start.5 = (bf16[128,4096]{1,0:T(8,128)(2,1)S(1)}, bf16[128,4096]{1,0:T(8,128)(2,1)}, u32[]{:S(2)}) copy-start(bf16[128,4096]{1,0:T(8,128)(2,1)} %factor.4) | copy-start | bytes 3145732
  56.8 26.3 %copy-start.10 = (s32[4,32]{1,0:T(4,128)S(1)}, s32[4,32]{1,0:T(4,128)}, u32[]{:S(2)}) copy-start(s32[4,32]{1,0:T(4,128)} %pattern.4) | copy-start | bytes 1540
  56.8 26.3 %copy-start.13 = (s32[2,64]{1,0:T(2,128)S(1)}, s32[2,64]{1,0:T(2,128)}, u32[]{:S(2)}) copy-start(s32[2,64]{1,0:T(2,128)} %pattern.3) | copy-start | bytes 1540
  56.9 26.1 %copy-start.2 = (bf16[128,8192]{1,0:T(8,128)(2,1)S(1)}, bf16[128,8192]{1,0:T(8,128)(2,1)}, u32[]{:S(2)}) copy-start(bf16[128,8192]{1,0:T(8,128)(2,1)} %factor.3) | copy-start | bytes 6291460
  56.9 5.0 %collective-permute-start.2 = (bf16[4,128,128]{2,1,0:T(8,128)(2,1)S(1)}, bf16[4,128,128]{2,1,0:T(8,128)(2,1)S(1)}, u32[]{:S(2)}, u32[]{:S(2)}) collective-permute-start(bf16[4,128,128]{2,1,0:T(8,128)(2,1)S(1)} %subtract_convert_fusion.1), channel_id=1, source_target_pairs={{0,2},{1,7},{2,0},{3,5},{4,6},{5,3},{6,4},{7,1},{8,10},{9,15},{10,... | collective-permute-start | bytes 393224 | tf_op jit(solution)/shard_map/ppermute | solution.py:249
  62.1 6.3 %collective-permute-start.3 = (bf16[4,128,128]{2,1,0:T(8,128)(2,1)S(1)}, bf16[4,128,128]{2,1,0:T(8,128)(2,1)S(1)}, u32[]{:S(2)}, u32[]{:S(2)}) collective-permute-start(bf16[4,128,128]{2,1,0:T(8,128)(2,1)S(1)} %add_convert_fusion.12), channel_id=1, source_target_pairs={{0,6},{1,3},{2,4},{3,1},{4,2},{5,7},{6,0},{7,5},{8,14},{9,11},{10,... | collective-permute-start | bytes 393224 | tf_op jit(solution)/shard_map/ppermute | solution.py:249
  68.4 1.4 collective-permute-start.4
  69.8 1.6 copy-start.3
  87.8 4.2 %collective-permute-start.5 = (bf16[64,128,128]{2,1,0:T(8,128)(2,1)S(1)}, bf16[64,128,128]{2,1,0:T(8,128)(2,1)S(1)}, u32[]{:S(2)}, u32[]{:S(2)}) collective-permute-start(bf16[64,128,128]{2,1,0:T(8,128)(2,1)S(1)} %get-tuple-element.223), channel_id=1, source_target_pairs={{0,1},{1,0},{2,3},{3,2},{4,5},{5,4},{6,7},{7,6},{8,9},{9,8},{10,11... | collective-permute-start | bytes 6291464 | tf_op jit(solution)/shard_map/ppermute | solution.py:242
  128.5 5.0 %collective-permute-start.6 = (bf16[4,128,128]{2,1,0:T(8,128)(2,1)S(1)}, bf16[4,128,128]{2,1,0:T(8,128)(2,1)S(1)}, u32[]{:S(2)}, u32[]{:S(2)}) collective-permute-start(bf16[4,128,128]{2,1,0:T(8,128)(2,1)S(1)} %subtract_convert_fusion), channel_id=1, source_target_pairs={{0,2},{1,7},{2,0},{3,5},{4,6},{5,3},{6,4},{7,1},{8,10},{9,15},{10,... | collective-permute-start | bytes 393224 | tf_op jit(solution)/shard_map/ppermute | solution.py:249
  133.7 6.3 %collective-permute-start.7 = (bf16[4,128,128]{2,1,0:T(8,128)(2,1)S(1)}, bf16[4,128,128]{2,1,0:T(8,128)(2,1)S(1)}, u32[]{:S(2)}, u32[]{:S(2)}) collective-permute-start(bf16[4,128,128]{2,1,0:T(8,128)(2,1)S(1)} %add_convert_fusion.10), channel_id=1, source_target_pairs={{0,6},{1,3},{2,4},{3,1},{4,2},{5,7},{6,0},{7,5},{8,14},{9,11},{10,... | collective-permute-start | bytes 393224 | tf_op jit(solution)/shard_map/ppermute | solution.py:249
  140.0 1.4 collective-permute-start.8
  141.4 2.2 copy-start
  143.6 31.4 %copy-start.1 = (bf16[1,1,2048,1024]{3,2,1,0:T(8,128)(2,1)S(1)}, bf16[1,1,2048,1024]{3,2,1,0:T(8,128)(2,1)}, u32[]{:S(2)}) copy-start(bf16[1,1,2048,1024]{3,2,1,0:T(8,128)(2,1)} %param.12) | copy-start | bytes 12582916
  176.4 1.4 collective-permute-start.9
  177.9 5.0 %collective-permute-start.10 = (bf16[4,128,128]{2,1,0:T(8,128)(2,1)S(1)}, bf16[4,128,128]{2,1,0:T(8,128)(2,1)S(1)}, u32[]{:S(2)}, u32[]{:S(2)}) collective-permute-start(bf16[4,128,128]{2,1,0:T(8,128)(2,1)S(1)} %add_convert_fusion.8), channel_id=1, source_target_pairs={{0,2},{1,7},{2,0},{3,5},{4,6},{5,3},{6,4},{7,1},{8,10},{9,15},{10,... | collective-permute-start | bytes 393224 | tf_op jit(solution)/shard_map/ppermute | solution.py:249
  182.9 6.4 %collective-permute-start.11 = (bf16[4,128,128]{2,1,0:T(8,128)(2,1)S(1)}, bf16[4,128,128]{2,1,0:T(8,128)(2,1)S(1)}, u32[]{:S(2)}, u32[]{:S(2)}) collective-permute-start(bf16[4,128,128]{2,1,0:T(8,128)(2,1)S(1)} %add_convert_fusion.7), channel_id=1, source_target_pairs={{0,6},{1,3},{2,4},{3,1},{4,2},{5,7},{6,0},{7,5},{8,14},{9,11},{10,... | collective-permute-start | bytes 393224 | tf_op jit(solution)/shard_map/ppermute | solution.py:249
  219.5 16.6 %copy-start.4 = (bf16[1,1,1024,1024]{3,2,1,0:T(8,128)(2,1)S(1)}, bf16[1,1,1024,1024]{3,2,1,0:T(8,128)(2,1)}, u32[]{:S(2)}) copy-start(bf16[1,1,1024,1024]{3,2,1,0:T(8,128)(2,1)} %param.13) | copy-start | bytes 6291460
  219.5 4.2 %collective-permute-start.12 = (bf16[64,128,128]{2,1,0:T(8,128)(2,1)S(1)}, bf16[64,128,128]{2,1,0:T(8,128)(2,1)S(1)}, u32[]{:S(2)}, u32[]{:S(2)}) collective-permute-start(bf16[64,128,128]{2,1,0:T(8,128)(2,1)S(1)} %bitcast.31), channel_id=1, source_target_pairs={{0,1},{1,0},{2,3},{3,2},{4,5},{5,4},{6,7},{7,6},{8,9},{9,8},{10,11... | collective-permute-start | bytes 6291464 | tf_op jit(solution)/shard_map/ppermute | solution.py:242
  225.8 24.2 %copy-start.14 = (f32[4,1,1]{0,2,1:T(1,128)S(1)}, f32[4,1,1]{0,2,1:T(1,128)}, u32[]{:S(2)}) copy-start(f32[4,1,1]{0,2,1:T(1,128)} %get-tuple-element.296) | copy-start | bytes 52
  237.1 1.4 collective-permute-start.13
  238.6 5.0 %collective-permute-start.14 = (bf16[4,128,128]{2,1,0:T(8,128)(2,1)S(1)}, bf16[4,128,128]{2,1,0:T(8,128)(2,1)S(1)}, u32[]{:S(2)}, u32[]{:S(2)}) collective-permute-start(bf16[4,128,128]{2,1,0:T(8,128)(2,1)S(1)} %add_convert_fusion.5), channel_id=1, source_target_pairs={{0,2},{1,7},{2,0},{3,5},{4,6},{5,3},{6,4},{7,1},{8,10},{9,15},{10,... | collective-permute-start | bytes 393224 | tf_op jit(solution)/shard_map/ppermute | solution.py:249
  243.7 6.3 %collective-permute-start.15 = (bf16[4,128,128]{2,1,0:T(8,128)(2,1)S(1)}, bf16[4,128,128]{2,1,0:T(8,128)(2,1)S(1)}, u32[]{:S(2)}, u32[]{:S(2)}) collective-permute-start(bf16[4,128,128]{2,1,0:T(8,128)(2,1)S(1)} %add_convert_fusion.4), channel_id=1, source_target_pairs={{0,6},{1,3},{2,4},{3,1},{4,2},{5,7},{6,0},{7,5},{8,14},{9,11},{10,... | collective-permute-start | bytes 393224 | tf_op jit(solution)/shard_map/ppermute | solution.py:249
  266.7 2.7 copy-start.7
  266.7 2.7 copy-start.12
  266.7 2.7 collective-permute-start.16
  268.1 11.1 %copy-start.9 = (bf16[1,1,512,1024]{3,2,1,0:T(8,128)(2,1)S(1)}, bf16[1,1,512,1024]{3,2,1,0:T(8,128)(2,1)}, u32[]{:S(2)}) copy-start(bf16[1,1,512,1024]{3,2,1,0:T(8,128)(2,1)} %param.14) | copy-start | bytes 3145732
  280.2 1.4 collective-permute-start.17
  (1 other events, 0.7 us)

commit v3 on v2

v3 whole, which is shorter than its diff:
```python
import functools

import jax
import jax.numpy as jnp
from jax import lax
from jax.experimental import pallas as pl
from jax.experimental.pallas import tpu as pltpu
from jax.sharding import PartitionSpec as P

BF16 = jnp.bfloat16
F32 = jnp.float32
MIB = 1024 * 1024
SMEM = pl.BlockSpec(memory_space=pltpu.SMEM)
VMEM = pl.BlockSpec(memory_space=pltpu.VMEM)


def near_of(lane):
    return lane ^ (2 + 4 * (lane & 1))


def core_of():
    return lax.axis_index("blk") & 1


def side_of():
    return lax.axis_index("blk") >> 1 & 1


def node_of(level):
    return lax.axis_index("leaf") // (lax.axis_size("leaf") >> level)


def live(node_blocks, level, lane):
    leaf = lax.axis_index("leaf") % (lax.axis_size("leaf") >> level)
    position = leaf * lax.axis_size("blk") + lane
    limit = node_blocks[2**level - 1 + node_of(level)]
    return jnp.where(position < limit, 1.0, 0.0).astype(F32)


def call(kernel, name, out_shape, smem, vmem, scratch=(), limit=24):
    return pl.pallas_call(
        kernel,
        out_shape=out_shape,
        in_specs=[SMEM] * len(smem) + [VMEM] * len(vmem),
        out_specs=jax.tree.map(lambda _: VMEM, out_shape),
        scratch_shapes=list(scratch),
        compiler_params=pltpu.CompilerParams(vmem_limit_bytes=limit * MIB),
        name=name,
    )(*smem, *vmem)


def array(*shape, dtype=BF16):
    return jax.ShapeDtypeStruct(shape, dtype)


def total_of(parts):
    total = parts[0].astype(F32)
    for part in parts[1:]:
        total = total + part.astype(F32)
    return total


def first_kernel(loads, out):
    lower = loads[2].astype(BF16)
    middle, root = loads[1].astype(BF16).T, loads[0].astype(BF16).T
    for chip in range(out.shape[0]):
        side = (chip & 1) * 64
        out[chip, :128, :] = lower
        out[chip, 128:192, :] = middle[side : side + 64]
        out[chip, 192:256, :] = root[side : side + 64]


def multiply_kernel(transposed, own, other, tile, out, columns):
    first = core_of() == 0
    for chip in range(own.shape[0]):
        mine, theirs = own[chip], other[chip]
        for core in range(2):
            block = jnp.where(first == (core == 0), mine, theirs)
            row = (2 * chip + core) * 128
            columns[row : row + 128, :] = block.T if transposed else block
    for group in range(out.shape[0]):
        rows = tile[group * 128 : group * 128 + 128, :]
        product = jnp.dot(rows, columns[...], preferred_element_type=F32)
        out[group] = product.astype(BF16).T


def multiply(own, other, tile, transposed):
    return call(
        functools.partial(multiply_kernel, transposed),
        "multiply",
        array(tile.shape[0] // 128, 128, 128),
        [],
        [own, other, tile],
        [pltpu.VMEM((tile.shape[1], 128), BF16)],
    )


def transposed_kernel(gathered, tile, mine, theirs):
    first = core_of() == 0
    rows = jnp.concatenate([gathered[a] for a in range(gathered.shape[0])], axis=1)
    for chip in range(mine.shape[0]):
        column = chip * 256
        product = jnp.dot(rows, tile[:, column : column + 256], preferred_element_type=F32)
        even, odd = product[:, :128], product[:, 128:]
        mine[chip] = jnp.where(first, even, odd)
        theirs[chip] = jnp.where(first, odd, even).astype(BF16)


def multiply_transposed(gathered, tile):
    chips = tile.shape[1] // 256
    return call(
        transposed_kernel,
        "multiply_transposed",
        (array(chips, 128, 128, dtype=F32), array(chips, 128, 128)),
        [],
        [gathered, tile],
    )


def lift_kernel(spans, levels, node_blocks, *refs):
    total = len(spans)
    patterns, refs = refs[:total], refs[total:]
    parts, refs = refs[0], refs[1:]
    earlier, refs = refs[: total - 1], refs[total - 1 :]
    factors, (solved, keep, send, sums) = refs[: 2 * total], refs[2 * total :]
    core, side = core_of(), side_of()
    lane = lax.axis_index("blk")
    half = keep.shape[0]
    for place in range(2):
        which = side if place == 0 else 1 - side
        summed = total_of([parts[g, which] for g in range(parts.shape[0])])
        factor = live(node_blocks, levels[0], near_of(lane) if place else lane)
        solved[place] = (summed * factor).astype(BF16)
    values = [jnp.concatenate([s[0], s[1]], axis=1) for s in (solved, *earlier)]
    sums[...] = jnp.zeros_like(sums)
    for index, span in enumerate(spans):
        node = node_of(levels[index])
        own, near = factors[2 * index], factors[2 * index + 1]

        def chunk(step, carry, index=index, node=node, own=own, near=near):
            columns = pl.ds(pl.multiple_of(step * 1024, 1024), 1024)
            factor = jnp.concatenate([own[:, columns], near[:, columns]], axis=0)
            product = jnp.dot(values[index], factor, preferred_element_type=F32)
            for part in range(8):
                block = patterns[index][node, step * 8 + part]
                slot = ((block & 1) ^ core) * half + (block >> 1)
                sums[slot] += product[:, part * 128 : part * 128 + 128]
            return carry

        lax.fori_loop(0, span // 1024, chunk, 0)

    def emit(slot, carry):
        keep[slot] = sums[slot].astype(BF16)
        send[slot] = sums[half + slot].astype(BF16)
        return carry

    lax.fori_loop(0, half, emit, 0, unroll=4)


def lift(node_blocks, levels, patterns, parts, earlier, factors, half):
    spans = tuple(f.shape[1] for f in factors[::2])
    return call(
        functools.partial(lift_kernel, spans, levels),
        "lift",
        (array(2, 64, 128), array(half, 64, 128), array(half, 64, 128)),
        [node_blocks, *patterns],
        [parts, *earlier, *factors],
        [pltpu.VMEM((2 * half, 64, 128), F32)],
    )


def rest_kernel(parts, load, copies):
    chip, near = lax.axis_index("blk") >> 1, near_of(lax.axis_index("blk")) >> 1
    for place in range(parts.shape[1]):
        total = total_of([parts[g, place] for g in range(parts.shape[0])])
        given = (chip == place) | (near == place)
        value = (jnp.where(given, load[place].astype(F32), 0.0) - total).astype(BF16)
        for index in range(copies.shape[0]):
            copies[index, place] = value


def join_kernel(parts, out):
    for place in range(out.shape[0]):
        for side in range(2):
            total = parts[side, place].astype(F32) + parts[2 + side, place].astype(F32)
            out[place, side * 64 : side * 64 + 64, :] = total.astype(BF16)


def split_kernel(mine, theirs, out):
    for place in range(mine.shape[0]):
        value = (mine[place] + theirs[place].astype(F32)).astype(BF16)
        for chip in range(out.shape[0]):
            side = (chip & 1) * 64
            out[chip, place] = value[side : side + 64]


def spread_kernel(level, node_blocks, parts, own, near, copies):
    lane = lax.axis_index("blk")
    for place in range(parts.shape[1]):
        value = total_of([parts[x, place] for x in range(parts.shape[0])])
        if level:
            value = value * live(node_blocks, level, 2 * place + (lane & 1))
        value = value.astype(BF16)

        @pl.when(lane >> 1 == place)
        def _():
            own[...] = value

        @pl.when(near_of(lane) >> 1 == place)
        def _():
            near[...] = value

        for index in range(copies.shape[0]):
            copies[index, place] = value


def root_kernel(parts, solved, copies):
    value = total_of([parts[g] for g in range(parts.shape[0])]).astype(BF16)
    solved[...] = value
    for index in range(copies.shape[0]):
        copies[index] = value


def pulled_of(level, pattern, own, other, factor, near, chosen):
    core, row_of = core_of(), node_of(level)

    def pick(position, carry):
        block = pattern[row_of, position]
        mine = (block & 1) == core
        column = pl.multiple_of(position * 128, 128)
        chosen[:, pl.ds(column, 128)] = jnp.where(mine, own[block >> 1], other[block >> 1])
        return carry

    lax.fori_loop(0, pattern.shape[1], pick, 0, unroll=4)
    result = []
    for rows in (factor, near):
        product = lax.dot_general(
            rows[...], chosen[...], (((1,), (1,)), ((), ())), preferred_element_type=F32
        )
        result.append(product.T)
    return result


def pull_kernel(level, pattern, own, other, factor, near, out, chosen):
    out[0], out[1] = pulled_of(level, pattern, own, other, factor, near, chosen)


def reduce_kernel(level, pattern, own, other, factor, near, solved, *refs):
    earlier, (copies, chosen) = refs[:-2], refs[-2:]
    side = side_of()
    pulled = pulled_of(level, pattern, own, other, factor, near, chosen)
    for place in range(2):
        value = pulled[place]
        for e in earlier:
            value = value + e[place]
        value = (solved[place].astype(F32) - value).astype(BF16)
        which = side if place == 0 else 1 - side
        for index in range(copies.shape[0]):
            copies[index, which] = value


def pull(level, pattern, own, other, factors):
    return call(
        functools.partial(pull_kernel, level),
        "pull",
        array(2, 64, 128, dtype=F32),
        [pattern],
        [own, other, *factors],
        [pltpu.VMEM((64, factors[0].shape[1]), BF16)],
    )


def reduced(level, pattern, own, other, factors, solved, earlier, count):
    return call(
        functools.partial(reduce_kernel, level),
        "reduced",
        array(count, 2, 64, 128),
        [pattern],
        [own, other, *factors, solved, *earlier],
        [pltpu.VMEM((64, factors[0].shape[1]), BF16)],
    )


def whole(mine, far):
    first = side_of() == 0
    low, high = jnp.where(first, mine, far), jnp.where(first, far, mine)
    return jnp.concatenate([low, high], axis=0).T


def stack_kernel(root, middle, lower, far, out):
    out[0] = root[...].T
    out[1] = whole(middle[0], far[2])
    out[2] = whole(lower[0], far[3])


def last_kernel(node_blocks, parts, root, middle, far, out):
    out[0] = whole(root[...], far[0])
    out[1] = whole(middle[...], far[1])
    total = total_of([parts[x] for x in range(parts.shape[0])])
    out[2] = (total * live(node_blocks, 2, lax.axis_index("blk"))).astype(BF16).T


def shards(
    loads,
    inverse_root,
    inverse_middle,
    inverse_lower,
    couple_middle,
    couple_lower,
    couple_between,
    pattern_middle,
    pattern_lower,
    pattern_between,
    node_blocks,
):
    leaf_count = lax.axis_size("leaf")
    block_count = lax.axis_size("blk")
    chip_count = block_count // 2
    chip_groups = [[2 * x + c for x in range(chip_count)] for c in range(2)]
    even_lanes = [i for i in range(block_count) if i >> 1 & 1 == 0]

    def leaf_groups(level):
        size = leaf_count >> level
        return [[g * size + j for j in range(size)] for g in range(1 << level)]

    def pair_groups(level):
        return [
            [leaf * block_count + i for leaf in group for i in (lane, near_of(lane))]
            for group in leaf_groups(level)
            for lane in even_lanes
        ]

    def swap_core(value):
        return lax.ppermute(value, "blk", [(i, i ^ 1) for i in range(block_count)])

    def swap_near(value):
        return lax.ppermute(value, "blk", [(i, near_of(i)) for i in range(block_count)])

    kept = {}

    def fence(value):
        tied, held = lax.optimization_barrier((value, dict(kept)))
        kept.update(held)
        return tied

    def exchange(value, axis, groups):
        value = fence(value)
        value = lax.all_to_all(value, axis, 0, 0, tiled=True, axis_index_groups=groups)
        return fence(value)

    def over_chips(value):
        return exchange(value, "blk", chip_groups)

    def over_leaf(value, level):
        return exchange(value, "leaf", leaf_groups(level) if level else None)

    def over_pair(value, level):
        size = leaf_count >> level
        value = exchange(value.reshape(2 * size, 64, 128), ("leaf", "blk"), pair_groups(level))
        return value.reshape(size, 2, 64, 128)

    halves = array(chip_count, chip_count, 64, 128)

    def residual(load, level, before_chips=lambda: None):
        size = leaf_count >> level
        keep, send = kept.pop("keep"), kept.pop("send")
        summed = (keep.astype(F32) + swap_core(send).astype(F32)).astype(BF16)
        parts = over_leaf(summed.reshape(size, chip_count, 64, 128), level)
        before_chips()
        parts = over_chips(call(rest_kernel, "rest", halves, [], [parts, kept.pop(load)]))
        rest = call(join_kernel, "join", array(chip_count, 128, 128), [], [parts])
        return rest, swap_core(rest)

    def backward(gathered, tile):
        mine, theirs = multiply_transposed(gathered, tile)
        return mine, swap_core(theirs)

    def spread(partial_sums, level):
        size = leaf_count >> level
        parts = over_chips(call(split_kernel, "split", halves, [], partial_sums))
        own, near, copies = call(
            functools.partial(spread_kernel, level), "spread",
            (array(64, 128), array(64, 128), array(size, chip_count, 64, 128)),
            [node_blocks], [parts],
        )
        kept[f"own{level}"], kept[f"near{level}"] = own, near
        blocks = over_leaf(copies, level).reshape(-1, 64, 128)
        return blocks, swap_core(blocks)

    tile_root, tile_middle, tile_lower = inverse_root[0, 0], inverse_middle[0, 0], inverse_lower[0, 0]
    kept["couples"] = [couple_between, couple_lower, couple_middle]

    loaded = over_chips(call(first_kernel, "first", array(chip_count, 256, 128), [], [loads]))
    between = [couple_between, swap_near(kept["couples"][0])]
    own = loaded[:, :128]
    kept["load_middle"], kept["load_root"] = loaded[:, 128:192], loaded[:, 192:]
    parts = over_pair(multiply(own, swap_core(own), tile_lower, False), 2)
    lower = [couple_lower, swap_near(kept["couples"][1])]
    kept["y_lower"], kept["keep"], kept["send"] = lift(
        node_blocks, (2,), [pattern_between], parts, [], between, (leaf_count >> 1) * chip_count
    )
    def before_chips():
        kept["lower"] = lower[1]

    own, other = residual("load_middle", 1, before_chips)
    middle = [couple_middle, swap_near(kept.pop("couples")[2])]
    lower[1] = kept.pop("lower")
    parts = over_pair(multiply(own, other, tile_middle, True), 1)
    kept["y_middle"], kept["keep"], kept["send"] = lift(
        node_blocks, (1, 2), [pattern_middle, pattern_lower], parts, [kept["y_lower"]],
        middle + lower, leaf_count * chip_count,
    )
    own, other = residual("load_root", 0)
    parts = over_leaf(multiply(own, other, tile_root, True), 0)
    kept["y_root"], copies = call(
        root_kernel, "root", (array(128, 128), array(leaf_count, 128, 128)), [], [parts]
    )
    own, other = spread(backward(over_leaf(copies, 0), tile_root), 0)
    copies = reduced(
        1, pattern_middle, own, other, middle, kept["y_middle"], [], leaf_count >> 1
    )
    kept["own_root"], kept["other_root"] = own, other
    gathered = over_pair(copies, 1).reshape(-1, 128, 128)
    own, other = spread(backward(gathered, tile_middle), 1)
    pulled = pull(2, pattern_lower, kept.pop("own_root"), kept.pop("other_root"), lower)
    copies = reduced(
        2, pattern_between, own, other, between, kept["y_lower"], [pulled], leaf_count >> 2
    )
    kept["far"] = swap_near(
        jnp.stack([kept.pop("near0"), kept.pop("near1"), kept["y_middle"][1], kept["y_lower"][1]])
    )
    gathered = over_pair(copies, 2).reshape(-1, 128, 128)
    mine, theirs = backward(gathered, tile_lower)
    kept["forward"] = call(
        stack_kernel, "stack", array(3, 128, 128), [],
        [kept.pop("y_root"), kept.pop("y_middle"), kept.pop("y_lower"), kept["far"]],
    )
    parts = over_chips((mine + theirs.astype(F32)).astype(BF16))
    answer = call(
        last_kernel, "last", array(3, 128, 128), [node_blocks],
        [parts, kept["own0"], kept["own1"], kept["far"]],
    )
    return (kept["forward"], answer)


def solution(mesh):
    in_specs = (
        P(None, ("leaf", "blk"), None),
        P("leaf", "blk", None, None),
        P("leaf", "blk", None, None),
        P("leaf", "blk", None, None),
        P(("leaf", "blk"), None),
        P(("leaf", "blk"), None),
        P(("leaf", "blk"), None),
        P(),
        P(),
        P(),
        P(),
    )
    out_specs = (P(None, ("leaf", "blk"), None), P(None, ("leaf", "blk"), None))
    return jax.shard_map(shards, mesh=mesh, in_specs=in_specs, out_specs=out_specs, check_vma=False)
```

time: 292 us -> 258 us (0.88)
  waiting for transfers between devices: 59.1 us -> 13.8 us
  blocking collectives: 186 us -> 216 us
  local copies, waits for them, and re-layouts: 11.4 us -> 2.31 us
  other arithmetic: 3.98 us -> 0.63 us
    ppermute x8 -> x4, waiting for transfers between devices: 38.9 us -> 0.5 us  [swap_near(): lax.ppermute(value, 'blk', [(i, near_of(i)) for i in range(block_count)])]
    all_to_all x12 -> x16, blocking collectives: 186 us -> 216 us  [exchange(): lax.all_to_all(value, axis, 0, 0, tiled=True, axis_index_groups=groups)]
    ppermute x10, waiting for transfers between devices: 20.2 us -> 13.3 us  [swap_core(): return lax.ppermute(value, 'blk', [(i, i ^ 1) for i in range(block_count)])]
    ppermute x8 -> x4, starting transfers between devices: 6.47 us -> 2.42 us  [swap_near(): lax.ppermute(value, 'blk', [(i, near_of(i)) for i in range(block_count)])]
    unnamed x30 -> x24, local copies, waits for them, and re-layouts: 5.74 us -> 2.28 us
    pallas_call x13 -> x23, Pallas kernels: 21.4 us -> 19.2 us  [call(): pl.pallas_call(kernel, out_shape=out_shape, in_specs=[SMEM] * len(smem) +...]
  transfers between devices with their start and end apart: 18 -> 14, of which waited for: 18 -> 10; matrix products, arithmetic and copies ran while one was open for 0% -> 0% of each run, Pallas kernels for 0% -> 2%
where the time goes in v3:
time: 258 us; the launch traced here: 257 us
  blocking collectives  216 us (84%)
  Pallas kernels  19.2 us (7%)
  waiting for transfers between devices  13.8 us (5%)
  starting transfers between devices  4.64 us (2%)
    all_to_all x16, blocking collectives, exchange(): lax.all_to_all(value, axis, 0, 0, tiled=True, axis_index_groups=groups)  216 us
    pallas_call x23, Pallas kernels, call(): pl.pallas_call(kernel, out_shape=out_shape, in_specs=[SMEM] * len(smem) +...  19.2 us
    ppermute x10, waiting for transfers between devices, swap_core(): return lax.ppermute(value, 'blk', [(i, i ^ 1) for i in range(block_count)])  13.3 us
  transfers between devices with their start and end apart: 14, of which 10 were waited for; matrix products, arithmetic and copies ran while one was open for 0% of the time, Pallas kernels for 2%

profile of v3, /device:TPU:0, one launch (start us, length us, event | category | flops | bytes accessed | tf_op | source)
XLA Modules:
  0.0 257.2 jit_solution(15071926705071695758)
XLA Ops:
  1.7 10.9 %all_to_all.80 = bf16[4,256,128]{2,1,0:T(8,128)(2,1)S(1)} all-to-all(bf16[4,256,128]{2,1,0:T(8,128)(2,1)S(1)} %first.1), channel_id=1, replica_groups={{0,2,4,6},{1,3,5,7},{8,10,12,14},{9,11,13,15},{16,18,20,22},{17,19,21,2..., dimensions={0} | all-to-all | bytes 524288 | tf_op jit(solution)/shard_map/all_to_all | solution.py:348
  13.3 1.3 collective-permute-done.other
  14.6 1.2 copy-done.4
  16.3 14.4 %all_to_all.81 = bf16[8,64,128]{2,1,0:T(8,128)(2,1)S(1)} all-to-all(bf16[8,64,128]{2,1,0:T(8,128)(2,1)S(1)} %bitcast.35), channel_id=1, replica_groups={{0,2,8,10,16,18,24,26},{1,7,9,15,17,23,25,31},{4,6,12,14,20,22,28,30},{..., dimensions={0} | all-to-all | bytes 262144 | tf_op jit(solution)/shard_map/all_to_all | solution.py:348
  30.8 1.7 lift.2
  33.3 1.2 collective-permute-done.2
  34.7 14.2 %all_to_all.82.parts = bf16[8,4,64,128]{3,2,1,0:T(8,128)(2,1)S(1)} all-to-all(bf16[8,4,64,128]{3,2,1,0:T(8,128)(2,1)S(1)} %bitcast.39), channel_id=1, replica_groups={{0,8,16,24,32,40,48,56},{64,72,80,88,96,104,112,120},{1,9,17,25,33,41,4..., dimensions={0} | all-to-all | bytes 1048576 | tf_op jit(solution)/shard_map/all_to_all | solution.py:348
  49.1 9.2 %all_to_all.83.parts = bf16[4,4,64,128]{3,2,1,0:T(8,128)(2,1)S(1)} all-to-all(bf16[4,4,64,128]{3,2,1,0:T(8,128)(2,1)S(1)} %rest.2), channel_id=1, replica_groups={{0,2,4,6},{1,3,5,7},{8,10,12,14},{9,11,13,15},{16,18,20,22},{17,19,21,2..., dimensions={0} | all-to-all | bytes 524288 | tf_op jit(solution)/shard_map/all_to_all | solution.py:348
  58.9 1.3 collective-permute-done.4.other
  61.1 25.0 %all_to_all.84 = bf16[16,64,128]{2,1,0:T(8,128)(2,1)S(1)} all-to-all(bf16[16,64,128]{2,1,0:T(8,128)(2,1)S(1)} %bitcast.29), channel_id=1, replica_groups={{0,2,8,10,16,18,24,26,32,34,40,42,48,50,56,58},{1,7,9,15,17,23,25,31,33..., dimensions={0} | all-to-all | bytes 524288 | tf_op jit(solution)/shard_map/all_to_all | solution.py:348
  86.1 3.8 %lift.3 = (bf16[2,64,128]{2,1,0:T(8,128)(2,1)S(1)}, bf16[64,64,128]{2,1,0:T(8,128)(2,1)S(1)}, bf16[64,64,128]{2,1,0:T(8,128)(2,1)S(1)}) custom-call(s32[7]{0:T(128)S(1)} %copy-done.8, s32[2,64]{1,0:T(2,128)S(1)} %copy-done.11, s32[4,32]{1,0:T(4,128)S(1)} %copy-done.9, bf16[8,2,64,128]{3,2,1,0:T(8,128)(2,1)S(1)} %bitcast.31, ...), custom_call_target="tpu_custom_call" | custom-call | tf_op jit(solution)/shard_map/lift/pallas_call | solution.py:41
  90.0 2.6 %collective-permute-done.6 = bf16[64,64,128]{2,1,0:T(8,128)(2,1)S(1)} collective-permute-done((bf16[64,64,128]{2,1,0:T(8,128)(2,1)S(1)}, bf16[64,64,128]{2,1,0:T(8,128)(2,1)S(1)}, u32[]{:S(2)}, u32[]{:S(2)}) %collective-permute-start.6) | collective-permute-done | bytes 1048608 | tf_op jit(solution)/shard_map/ppermute | solution.py:334
  93.1 24.7 %all_to_all.85.parts = bf16[16,4,64,128]{3,2,1,0:T(8,128)(2,1)S(1)} all-to-all(bf16[16,4,64,128]{3,2,1,0:T(8,128)(2,1)S(1)} %bitcast.38), channel_id=1, replica_groups=mesh['leaf'=16,'blk'=8] {'leaf'}, dimensions={0} | all-to-all | bytes 2097152 | tf_op jit(solution)/shard_map/all_to_all | solution.py:348
  117.9 9.1 %all_to_all.86.parts = bf16[4,4,64,128]{3,2,1,0:T(8,128)(2,1)S(1)} all-to-all(bf16[4,4,64,128]{3,2,1,0:T(8,128)(2,1)S(1)} %rest.3), channel_id=1, replica_groups={{0,2,4,6},{1,3,5,7},{8,10,12,14},{9,11,13,15},{16,18,20,22},{17,19,21,2..., dimensions={0} | all-to-all | bytes 524288 | tf_op jit(solution)/shard_map/all_to_all | solution.py:348
  127.2 1.3 collective-permute-done.7.other
  128.5 1.4 multiply.5
  129.9 14.8 %all_to_all.87.parts = bf16[16,128,128]{2,1,0:T(8,128)(2,1)S(1)} all-to-all(bf16[16,128,128]{2,1,0:T(8,128)(2,1)S(1)} %multiply.5), channel_id=1, replica_groups=mesh['leaf'=16,'blk'=8] {'leaf'}, dimensions={0} | all-to-all | bytes 1048576 | tf_op jit(solution)/shard_map/all_to_all | solution.py:348
  144.8 14.0 %all_to_all.88.gathered = bf16[16,128,128]{2,1,0:T(8,128)(2,1)S(1)} all-to-all(bf16[16,128,128]{2,1,0:T(8,128)(2,1)S(1)} %get-tuple-element.262), channel_id=1, replica_groups=mesh['leaf'=16,'blk'=8] {'leaf'}, dimensions={0} | all-to-all | bytes 1048576 | tf_op jit(solution)/shard_map/all_to_all | solution.py:348
  159.6 1.3 collective-permute-done.8.theirs
  161.0 9.6 %all_to_all.89.parts = bf16[4,4,64,128]{3,2,1,0:T(8,128)(2,1)S(1)} all-to-all(bf16[4,4,64,128]{3,2,1,0:T(8,128)(2,1)S(1)} %split.2), channel_id=1, replica_groups={{0,2,4,6},{1,3,5,7},{8,10,12,14},{9,11,13,15},{16,18,20,22},{17,19,21,2..., dimensions={0} | all-to-all | bytes 524288 | tf_op jit(solution)/shard_map/all_to_all | solution.py:348
  171.3 19.6 %all_to_all.90 = bf16[16,4,64,128]{3,2,1,0:T(8,128)(2,1)S(1)} all-to-all(bf16[16,4,64,128]{3,2,1,0:T(8,128)(2,1)S(1)} %get-tuple-element.283), channel_id=1, replica_groups=mesh['leaf'=16,'blk'=8] {'leaf'}, dimensions={0} | all-to-all | bytes 2097152 | tf_op jit(solution)/shard_map/all_to_all | solution.py:348
  190.9 2.7 %collective-permute-done.9.other = bf16[64,64,128]{2,1,0:T(8,128)(2,1)S(1)} collective-permute-done((bf16[64,64,128]{2,1,0:T(8,128)(2,1)S(1)}, bf16[64,64,128]{2,1,0:T(8,128)(2,1)S(1)}, u32[]{:S(2)}, u32[]{:S(2)}) %collective-permute-start.9) | collective-permute-done | bytes 1048608 | tf_op jit(solution)/shard_map/ppermute | solution.py:334
  193.5 2.4 reduced.2
  195.9 10.0 %all_to_all.91 = bf16[16,64,128]{2,1,0:T(8,128)(2,1)S(1)} all-to-all(bf16[16,64,128]{2,1,0:T(8,128)(2,1)S(1)} %bitcast.30), channel_id=1, replica_groups={{0,2,8,10,16,18,24,26,32,34,40,42,48,50,56,58},{1,7,9,15,17,23,25,31,33..., dimensions={0} | all-to-all | bytes 524288 | tf_op jit(solution)/shard_map/all_to_all | solution.py:348
  208.1 10.3 %all_to_all.92.parts = bf16[4,4,64,128]{3,2,1,0:T(8,128)(2,1)S(1)} all-to-all(bf16[4,4,64,128]{3,2,1,0:T(8,128)(2,1)S(1)} %split.3), channel_id=1, replica_groups={{0,2,4,6},{1,3,5,7},{8,10,12,14},{9,11,13,15},{16,18,20,22},{17,19,21,2..., dimensions={0} | all-to-all | bytes 524288 | tf_op jit(solution)/shard_map/all_to_all | solution.py:348
  219.0 12.2 %all_to_all.93 = bf16[8,4,64,128]{3,2,1,0:T(8,128)(2,1)S(1)} all-to-all(bf16[8,4,64,128]{3,2,1,0:T(8,128)(2,1)S(1)} %get-tuple-element.332), channel_id=1, replica_groups={{0,8,16,24,32,40,48,56},{64,72,80,88,96,104,112,120},{1,9,17,25,33,41,4..., dimensions={0} | all-to-all | bytes 1048576 | tf_op jit(solution)/shard_map/all_to_all | solution.py:348
  231.8 1.6 pull.1.refs_0_
  233.4 1.6 reduced.3
  235.5 9.3 %all_to_all.94 = bf16[8,64,128]{2,1,0:T(8,128)(2,1)S(1)} all-to-all(bf16[8,64,128]{2,1,0:T(8,128)(2,1)S(1)} %bitcast.32), channel_id=1, replica_groups={{0,2,8,10,16,18,24,26},{1,7,9,15,17,23,25,31},{4,6,12,14,20,22,28,30},{..., dimensions={0} | all-to-all | bytes 262144 | tf_op jit(solution)/shard_map/all_to_all | solution.py:348
  245.1 1.3 collective-permute-start.13
  247.4 8.5 %all_to_all.95.parts = bf16[4,128,128]{2,1,0:T(8,128)(2,1)S(1)} all-to-all(bf16[4,128,128]{2,1,0:T(8,128)(2,1)S(1)} %add_convert_fusion.2), channel_id=1, replica_groups={{0,2,4,6},{1,3,5,7},{8,10,12,14},{9,11,13,15},{16,18,20,22},{17,19,21,2..., dimensions={0} | all-to-all | bytes 262144 | tf_op jit(solution)/shard_map/all_to_all | solution.py:348
  255.9 1.3 last.1
  (67 shorter events, 12.4 us)
Async XLA Ops:
  0.6 30.1 %copy-start.3 = (bf16[128,4096]{1,0:T(8,128)(2,1)S(1)}, bf16[128,4096]{1,0:T(8,128)(2,1)}, u32[]{:S(2)}) copy-start(bf16[128,4096]{1,0:T(8,128)(2,1)} %factor.5) | copy-start | bytes 3145732
  0.6 1.0 copy-start.7
  1.7 29.1 %copy-start.8 = (s32[7]{0:T(128)S(1)}, s32[7]{0:T(128)}, u32[]{:S(2)}) copy-start(s32[7]{0:T(128)} %node_blocks.9) | copy-start | bytes 88
  1.7 29.1 %copy-start.10 = (s32[4,32]{1,0:T(4,128)S(1)}, s32[4,32]{1,0:T(4,128)}, u32[]{:S(2)}) copy-start(s32[4,32]{1,0:T(4,128)} %pattern.5) | copy-start | bytes 1540
  12.6 18.2 %collective-permute-start.1 = (bf16[128,4096]{1,0:T(8,128)(2,1)}, bf16[128,4096]{1,0:T(8,128)(2,1)S(1)}, u32[]{:S(2)}, u32[]{:S(2)}) collective-permute-start(bf16[128,4096]{1,0:T(8,128)(2,1)} %factor.5), channel_id=1, source_target_pairs={{0,2},{1,7},{2,0},{3,5},{4,6},{5,3},{6,4},{7,1},{8,10},{9,15},{10,... | collective-permute-start | bytes 3145736 | tf_op jit(solution)/shard_map/ppermute | solution.py:337
  13.2 1.4 collective-permute-start
  14.6 1.2 copy-start.4
  15.8 16.8 %copy-start.6 = (bf16[128,4096]{1,0:T(8,128)(2,1)S(1)}, bf16[128,4096]{1,0:T(8,128)(2,1)}, u32[]{:S(2)}) copy-start(bf16[128,4096]{1,0:T(8,128)(2,1)} %factor.4) | copy-start | bytes 3145732
  32.5 25.7 %copy-start.2 = (bf16[128,8192]{1,0:T(8,128)(2,1)S(1)}, bf16[128,8192]{1,0:T(8,128)(2,1)}, u32[]{:S(2)}) copy-start(bf16[128,8192]{1,0:T(8,128)(2,1)} %factor.3) | copy-start | bytes 6291460
  32.5 2.0 collective-permute-start.2
  32.6 16.4 %collective-permute-start.3 = (bf16[128,4096]{1,0:T(8,128)(2,1)S(1)}, bf16[128,4096]{1,0:T(8,128)(2,1)S(1)}, u32[]{:S(2)}, u32[]{:S(2)}) collective-permute-start(bf16[128,4096]{1,0:T(8,128)(2,1)S(1)} %copy-done.6), channel_id=1, source_target_pairs={{0,2},{1,7},{2,0},{3,5},{4,6},{5,3},{6,4},{7,1},{8,10},{9,15},{10,... | collective-permute-start | bytes 3145736 | tf_op jit(solution)/shard_map/ppermute | solution.py:337
  34.5 25.7 %copy-start.1 = (bf16[1,1,1024,1024]{3,2,1,0:T(8,128)(2,1)S(1)}, bf16[1,1,1024,1024]{3,2,1,0:T(8,128)(2,1)}, u32[]{:S(2)}) copy-start(bf16[1,1,1024,1024]{3,2,1,0:T(8,128)(2,1)} %param.13) | copy-start | bytes 6291460
  49.0 37.1 %copy-start.9 = (s32[4,32]{1,0:T(4,128)S(1)}, s32[4,32]{1,0:T(4,128)}, u32[]{:S(2)}) copy-start(s32[4,32]{1,0:T(4,128)} %pattern.4) | copy-start | bytes 1540
  49.0 37.1 %copy-start.11 = (s32[2,64]{1,0:T(2,128)S(1)}, s32[2,64]{1,0:T(2,128)}, u32[]{:S(2)}) copy-start(s32[2,64]{1,0:T(2,128)} %pattern.3) | copy-start | bytes 1540
  58.2 27.9 %collective-permute-start.5 = (bf16[128,8192]{1,0:T(8,128)(2,1)S(1)}, bf16[128,8192]{1,0:T(8,128)(2,1)S(1)}, u32[]{:S(2)}, u32[]{:S(2)}) collective-permute-start(bf16[128,8192]{1,0:T(8,128)(2,1)S(1)} %copy-done.2), channel_id=1, source_target_pairs={{0,2},{1,7},{2,0},{3,5},{4,6},{5,3},{6,4},{7,1},{8,10},{9,15},{10,... | collective-permute-start | bytes 6291464 | tf_op jit(solution)/shard_map/ppermute | solution.py:337
  58.8 1.4 collective-permute-start.4
  89.9 2.7 %collective-permute-start.6 = (bf16[64,64,128]{2,1,0:T(8,128)(2,1)S(1)}, bf16[64,64,128]{2,1,0:T(8,128)(2,1)S(1)}, u32[]{:S(2)}, u32[]{:S(2)}) collective-permute-start(bf16[64,64,128]{2,1,0:T(8,128)(2,1)S(1)} %get-tuple-element.237), channel_id=1, source_target_pairs={{0,1},{1,0},{2,3},{3,2},{4,5},{5,4},{6,7},{7,6},{8,9},{9,8},{10,11... | collective-permute-start | bytes 3145736 | tf_op jit(solution)/shard_map/ppermute | solution.py:334
  93.1 35.4 %copy-start = (bf16[1,1,2048,1024]{3,2,1,0:T(8,128)(2,1)S(1)}, bf16[1,1,2048,1024]{3,2,1,0:T(8,128)(2,1)}, u32[]{:S(2)}) copy-start(bf16[1,1,2048,1024]{3,2,1,0:T(8,128)(2,1)} %param.12) | copy-start | bytes 12582916
  127.1 1.4 collective-permute-start.7
  159.5 1.4 collective-permute-start.8
  190.9 2.7 %collective-permute-start.9 = (bf16[64,64,128]{2,1,0:T(8,128)(2,1)S(1)}, bf16[64,64,128]{2,1,0:T(8,128)(2,1)S(1)}, u32[]{:S(2)}, u32[]{:S(2)}) collective-permute-start(bf16[64,64,128]{2,1,0:T(8,128)(2,1)S(1)} %bitcast.19), channel_id=1, source_target_pairs={{0,1},{1,0},{2,3},{3,2},{4,5},{5,4},{6,7},{7,6},{8,9},{9,8},{10,11... | collective-permute-start | bytes 3145736 | tf_op jit(solution)/shard_map/ppermute | solution.py:334
  206.4 1.6 collective-permute-start.10
  231.1 2.3 collective-permute-start.11
  231.2 4.3 %collective-permute-start.12 = (bf16[4,64,128]{2,1,0:T(8,128)(2,1)S(1)}, bf16[4,64,128]{2,1,0:T(8,128)(2,1)S(1)}, u32[]{:S(2)}, u32[]{:S(2)}) collective-permute-start(bf16[4,64,128]{2,1,0:T(8,128)(2,1)S(1)} %pad_maximum_fusion), channel_id=1, source_target_pairs={{0,2},{1,7},{2,0},{3,5},{4,6},{5,3},{6,4},{7,1},{8,10},{9,15},{10,... | collective-permute-start | bytes 196616 | tf_op jit(solution)/shard_map/ppermute | solution.py:337
  233.4 11.4 %copy-start.5 = (bf16[1,1,512,1024]{3,2,1,0:T(8,128)(2,1)S(1)}, bf16[1,1,512,1024]{3,2,1,0:T(8,128)(2,1)}, u32[]{:S(2)}) copy-start(bf16[1,1,512,1024]{3,2,1,0:T(8,128)(2,1)} %param.14) | copy-start | bytes 3145732
  245.1 2.3 collective-permute-start.13

commit v4 on v3

--- a/solution.py
+++ b/solution.py
@@ -30,8 +30,13 @@
     return lax.axis_index("leaf") // (lax.axis_size("leaf") >> level)
 
 
-def live(node_blocks, level, lane):
-    leaf = lax.axis_index("leaf") % (lax.axis_size("leaf") >> level)
+def leaf_near_of(leaf, lane):
+    return leaf ^ (1 + 2 * (lane & 1))
+
+
+def live(node_blocks, level, lane, leaf=None):
+    leaf = lax.axis_index("leaf") if leaf is None else leaf
+    leaf = leaf % (lax.axis_size("leaf") >> level)
     position = leaf * lax.axis_size("blk") + lane
     limit = node_blocks[2**level - 1 + node_of(level)]
     return jnp.where(position < limit, 1.0, 0.0).astype(F32)
@@ -61,16 +66,14 @@
 
 
 def first_kernel(loads, out):
-    lower = loads[2].astype(BF16)
-    middle, root = loads[1].astype(BF16).T, loads[0].astype(BF16).T
+    lower, root = loads[2].astype(BF16), loads[0].astype(BF16).T
     for chip in range(out.shape[0]):
         side = (chip & 1) * 64
         out[chip, :128, :] = lower
-        out[chip, 128:192, :] = middle[side : side + 64]
-        out[chip, 192:256, :] = root[side : side + 64]
-
-
-def multiply_kernel(transposed, own, other, tile, out, columns):
+        out[chip, 128:192, :] = root[side : side + 64]
+
+
+def gather_columns(transposed, own, other, columns):
     first = core_of() == 0
     for chip in range(own.shape[0]):
         mine, theirs = own[chip], other[chip]
@@ -78,17 +81,35 @@
             block = jnp.where(first == (core == 0), mine, theirs)
             row = (2 * chip + core) * 128
             columns[row : row + 128, :] = block.T if transposed else block
+
+
+def partial_of(tile, columns, group):
+    rows = tile[group * 128 : group * 128 + 128, :]
+    return jnp.dot(rows, columns[...], preferred_element_type=F32).astype(BF16).T
+
+
+def multiply_kernel(own, other, tile, out, columns):
+    gather_columns(True, own, other, columns)
     for group in range(out.shape[0]):
-        rows = tile[group * 128 : group * 128 + 128, :]
-        product = jnp.dot(rows, columns[...], preferred_element_type=F32)
-        out[group] = product.astype(BF16).T
-
-
-def multiply(own, other, tile, transposed):
+        out[group] = partial_of(tile, columns, group)
+
+
+def multiply_lower_kernel(own, other, tile, out, columns):
+    gather_columns(False, own, other, columns)
+    partials = [partial_of(tile, columns, group) for group in range(out.shape[0])]
+    first = core_of() == 0
+    for group in range(out.shape[0]):
+        near = jnp.where(first, partials[group ^ 1], partials[group ^ 3])
+        side = (group & 1) * 64
+        out[group, :128, :] = partials[group]
+        out[group, 128:, :] = near[side : side + 64]
+
+
+def multiply(kernel, rows, own, other, tile):
     return call(
-        functools.partial(multiply_kernel, transposed),
+        kernel,
         "multiply",
-        array(tile.shape[0] // 128, 128, 128),
+        array(tile.shape[0] // 128, rows, 128),
         [],
         [own, other, tile],
         [pltpu.VMEM((tile.shape[1], 128), BF16)],
@@ -117,29 +138,16 @@
     )
 
 
-def lift_kernel(spans, levels, node_blocks, *refs):
-    total = len(spans)
-    patterns, refs = refs[:total], refs[total:]
-    parts, refs = refs[0], refs[1:]
-    earlier, refs = refs[: total - 1], refs[total - 1 :]
-    factors, (solved, keep, send, sums) = refs[: 2 * total], refs[2 * total :]
-    core, side = core_of(), side_of()
-    lane = lax.axis_index("blk")
+def place_updates(spans, levels, patterns, values, factors, keep, send, sums):
+    core = core_of()
     half = keep.shape[0]
-    for place in range(2):
-        which = side if place == 0 else 1 - side
-        summed = total_of([parts[g, which] for g in range(parts.shape[0])])
-        factor = live(node_blocks, levels[0], near_of(lane) if place else lane)
-        solved[place] = (summed * factor).astype(BF16)
-    values = [jnp.concatenate([s[0], s[1]], axis=1) for s in (solved, *earlier)]
     sums[...] = jnp.zeros_like(sums)
     for index, span in enumerate(spans):
         node = node_of(levels[index])
-        own, near = factors[2 * index], factors[2 * index + 1]
-
-        def chunk(step, carry, index=index, node=node, own=own, near=near):
+
+        def chunk(step, carry, index=index, node=node):
             columns = pl.ds(pl.multiple_of(step * 1024, 1024), 1024)
-            factor = jnp.concatenate([own[:, columns], near[:, columns]], axis=0)
+            factor = jnp.concatenate([f[:, columns] for f in factors[index]], axis=0)
             product = jnp.dot(values[index], factor, preferred_element_type=F32)
             for part in range(8):
                 block = patterns[index][node, step * 8 + part]
@@ -157,15 +165,38 @@
     lax.fori_loop(0, half, emit, 0, unroll=4)
 
 
-def lift(node_blocks, levels, patterns, parts, earlier, factors, half):
-    spans = tuple(f.shape[1] for f in factors[::2])
-    return call(
-        functools.partial(lift_kernel, spans, levels),
-        "lift",
-        (array(2, 64, 128), array(half, 64, 128), array(half, 64, 128)),
-        [node_blocks, *patterns],
-        [parts, *earlier, *factors],
-        [pltpu.VMEM((2 * half, 64, 128), F32)],
+def lower_kernel(node_blocks, pattern, parts, factor, near, solved, own, far, keep, send, sums):
+    leaf, lane = lax.axis_index("leaf"), lax.axis_index("blk")
+    total = total_of([parts[g, :128, :] for g in range(parts.shape[0])])
+    value = (total * live(node_blocks, 2, lane)).astype(BF16)
+    total = total_of([parts[g, 128:, :] for g in range(parts.shape[0])])
+    partner = (total * live(node_blocks, 2, lane, leaf_near_of(leaf, lane))).astype(BF16)
+    solved[...] = value
+    first = side_of() == 0
+    low, high = value[:64], value[64:]
+    own[...] = jnp.where(first, low, high)
+    far[...] = jnp.where(first, high, low)
+    values = jnp.concatenate([jnp.where(leaf & 1 == 0, low, high), partner], axis=1)
+    spans = (factor.shape[1],)
+    place_updates(spans, (2,), [pattern], [values], [[factor, near]], keep, send, sums)
+
+
+def pair_kernel(node_blocks, pattern, pattern_lower, parts, lower, lower_near, *refs):
+    factors, (solved, keep, send, sums) = refs[:4], refs[4:]
+    side, lane = side_of(), lax.axis_index("blk")
+    for place in range(2):
+        which = side if place == 0 else 1 - side
+        total = total_of([parts[g, which] for g in range(parts.shape[0])])
+        factor = live(node_blocks, 1, near_of(lane) if place else lane)
+        solved[place] = (total * factor).astype(BF16)
+    values = [
+        jnp.concatenate([solved[0], solved[1]], axis=1),
+        jnp.concatenate([lower[...], lower_near[...]], axis=1),
+    ]
+    spans = (factors[0].shape[1], factors[2].shape[1])
+    place_updates(
+        spans, (1, 2), [pattern, pattern_lower], values, [factors[:2], factors[2:]],
+        keep, send, sums,
     )
 
 
@@ -177,6 +208,26 @@
         value = (jnp.where(given, load[place].astype(F32), 0.0) - total).astype(BF16)
         for index in range(copies.shape[0]):
             copies[index, place] = value
+
+
+def rest_middle_kernel(parts, loads, far, copies):
+    chip = lax.axis_index("blk") >> 1
+    load = loads[1].T
+    for place in range(parts.shape[1]):
+        total = [total_of([parts[g, place] for g in range(y, parts.shape[0], 2)]) for y in range(2)]
+        total = jnp.concatenate(total, axis=0)
+        value = (jnp.where(chip == place, load, 0.0) - total).astype(BF16)
+        for index in range(copies.shape[0]):
+            copies[index, place * 128 : place * 128 + 128, :] = value
+    for index in range(copies.shape[0]):
+        copies[index, parts.shape[1] * 128 :, :] = far[...]
+
+
+def join_middle_kernel(parts, out, near):
+    for place in range(out.shape[0]):
+        rows = pl.ds(place * 128, 128)
+        out[place] = total_of([parts[x, rows, :] for x in range(parts.shape[0])]).astype(BF16)
+    near[...] = parts[near_of(lax.axis_index("blk")) >> 1, out.shape[0] * 128 :, :]
 
 
 def join_kernel(parts, out):
@@ -266,7 +317,7 @@
         array(2, 64, 128, dtype=F32),
         [pattern],
         [own, other, *factors],
-        [pltpu.VMEM((64, factors[0].shape[1]), BF16)],
+        [pltpu.VMEM((64, factors[0].shape[1]), BF16)], 12,
     )
 
 
@@ -277,7 +328,7 @@
         array(count, 2, 64, 128),
         [pattern],
         [own, other, *factors, solved, *earlier],
-        [pltpu.VMEM((64, factors[0].shape[1]), BF16)],
+        [pltpu.VMEM((64, factors[0].shape[1]), BF16)], 12,
     )
 
 
@@ -290,7 +341,7 @@
 def stack_kernel(root, middle, lower, far, out):
     out[0] = root[...].T
     out[1] = whole(middle[0], far[2])
-    out[2] = whole(lower[0], far[3])
+    out[2] = lower[...].T
 
 
 def last_kernel(node_blocks, parts, root, middle, far, out):
@@ -336,6 +387,13 @@
     def swap_near(value):
         return lax.ppermute(value, "blk", [(i, near_of(i)) for i in range(block_count)])
 
+    def swap_leaf_near(value):
+        pairs = []
+        for i in range(leaf_count * block_count):
+            leaf, lane = divmod(i, block_count)
+            pairs.append((i, leaf_near_of(leaf, lane) * block_count + lane))
+        return lax.ppermute(value, ("leaf", "blk"), pairs)
+
     kept = {}
 
     def fence(value):
@@ -361,15 +419,10 @@
 
     halves = array(chip_count, chip_count, 64, 128)
 
-    def residual(load, level, before_chips=lambda: None):
+    def updates(keep, send, level):
+        summed = (keep.astype(F32) + swap_core(send).astype(F32)).astype(BF16)
         size = leaf_count >> level
-        keep, send = kept.pop("keep"), kept.pop("send")
-        summed = (keep.astype(F32) + swap_core(send).astype(F32)).astype(BF16)
-        parts = over_leaf(summed.reshape(size, chip_count, 64, 128), level)
-        before_chips()
-        parts = over_chips(call(rest_kernel, "rest", halves, [], [parts, kept.pop(load)]))
-        rest = call(join_kernel, "join", array(chip_count, 128, 128), [], [parts])
-        return rest, swap_core(rest)
+        return over_leaf(summed.reshape((size, chip_count) + keep.shape[1:]), level)
 
     def backward(gathered, tile):
         mine, theirs = multiply_transposed(gathered, tile)
@@ -388,30 +441,52 @@
         return blocks, swap_core(blocks)
 
     tile_root, tile_middle, tile_lower = inverse_root[0, 0], inverse_middle[0, 0], inverse_lower[0, 0]
+    leaf_near_between = swap_leaf_near(couple_between)
     kept["couples"] = [couple_between, couple_lower, couple_middle]
 
-    loaded = over_chips(call(first_kernel, "first", array(chip_count, 256, 128), [], [loads]))
-    between = [couple_between, swap_near(kept["couples"][0])]
+    loaded = over_chips(call(first_kernel, "first", array(chip_count, 192, 128), [], [loads]))
+    lower = [couple_lower, swap_near(kept["couples"][1])]
+    middle = [couple_middle, swap_near(kept["couples"][2])]
     own = loaded[:, :128]
-    kept["load_middle"], kept["load_root"] = loaded[:, 128:192], loaded[:, 192:]
-    parts = over_pair(multiply(own, swap_core(own), tile_lower, False), 2)
-    lower = [couple_lower, swap_near(kept["couples"][1])]
-    kept["y_lower"], kept["keep"], kept["send"] = lift(
-        node_blocks, (2,), [pattern_between], parts, [], between, (leaf_count >> 1) * chip_count
-    )
-    def before_chips():
-        kept["lower"] = lower[1]
-
-    own, other = residual("load_middle", 1, before_chips)
-    middle = [couple_middle, swap_near(kept.pop("couples")[2])]
-    lower[1] = kept.pop("lower")
-    parts = over_pair(multiply(own, other, tile_middle, True), 1)
-    kept["y_middle"], kept["keep"], kept["send"] = lift(
-        node_blocks, (1, 2), [pattern_middle, pattern_lower], parts, [kept["y_lower"]],
-        middle + lower, leaf_count * chip_count,
-    )
-    own, other = residual("load_root", 0)
-    parts = over_leaf(multiply(own, other, tile_root, True), 0)
+    kept["load_root"] = loaded[:, 128:]
+    parts = over_leaf(multiply(multiply_lower_kernel, 192, own, swap_core(own), tile_lower), 2)
+    half = (leaf_count >> 1) * chip_count
+    parts, lower[1] = lax.optimization_barrier((parts, lower[1]))
+    y_lower, own, far, keep, send = call(
+        lower_kernel, "lift_lower",
+        (array(128, 128), array(64, 128), array(64, 128), array(half, 64, 128), array(half, 64, 128)),
+        [node_blocks, pattern_between], [parts, couple_between, leaf_near_between],
+        [pltpu.VMEM((2 * half, 64, 128), F32)],
+    )
+    kept["y_lower"], kept["y_lower_own"], kept["far"], kept["lower"] = y_lower, own, far, lower[1]
+    parts = updates(keep, send, 1)
+    kept["middle"] = middle[1]
+    rows = chip_count * 128 + 64
+    parts = over_chips(
+        call(
+            rest_middle_kernel, "rest", array(chip_count, rows, 128), [],
+            [parts, loads, kept.pop("far")],
+        )
+    )
+    own, kept["y_lower_near"] = call(
+        join_middle_kernel, "join", (array(chip_count, 128, 128), array(64, 128)), [], [parts]
+    )
+    parts = over_pair(multiply(multiply_kernel, 128, own, swap_core(own), tile_middle), 1)
+    lower[1], middle[1] = kept.pop("lower"), kept.pop("middle")
+    near_between = swap_near(kept.pop("couples")[0])
+    half = leaf_count * chip_count
+    kept["y_middle"], keep, send = call(
+        pair_kernel, "lift_pair",
+        (array(2, 64, 128), array(half, 64, 128), array(half, 64, 128)),
+        [node_blocks, pattern_middle, pattern_lower],
+        [parts, kept["y_lower_own"], kept["y_lower_near"], *middle, *lower],
+        [pltpu.VMEM((2 * half, 64, 128), F32)], 16,
+    )
+    parts = updates(keep, send, 0)
+    kept["near_between"] = near_between
+    parts = over_chips(call(rest_kernel, "rest", halves, [], [parts, kept.pop("load_root")]))
+    own = call(join_kernel, "join", array(chip_count, 128, 128), [], [parts])
+    parts = over_leaf(multiply(multiply_kernel, 128, own, swap_core(own), tile_root), 0)
     kept["y_root"], copies = call(
         root_kernel, "root", (array(128, 128), array(leaf_count, 128, 128)), [], [parts]
     )
@@ -423,11 +498,11 @@
     gathered = over_pair(copies, 1).reshape(-1, 128, 128)
     own, other = spread(backward(gathered, tile_middle), 1)
     pulled = pull(2, pattern_lower, kept.pop("own_root"), kept.pop("other_root"), lower)
-    copies = reduced(
-        2, pattern_between, own, other, between, kept["y_lower"], [pulled], leaf_count >> 2
-    )
+    between = [couple_between, kept.pop("near_between")]
+    solved = jnp.stack([kept.pop("y_lower_own"), kept.pop("y_lower_near")])
+    copies = reduced(2, pattern_between, own, other, between, solved, [pulled], leaf_count >> 2)
     kept["far"] = swap_near(
-        jnp.stack([kept.pop("near0"), kept.pop("near1"), kept["y_middle"][1], kept["y_lower"][1]])
+        jnp.stack([kept.pop("near0"), kept.pop("near1"), kept["y_middle"][1]])
     )
     gathered = over_pair(copies, 2).reshape(-1, 128, 128)
     mine, theirs = backward(gathered, tile_lower)

time: 258 us -> 249 us (0.965)
  blocking collectives: 216 us -> 204 us
  starting transfers between devices: 4.64 us -> 7.87 us
    all_to_all x16, blocking collectives: 216 us -> 204 us  [exchange(): lax.all_to_all(value, axis, 0, 0, tiled=True, axis_index_groups=groups)]
  transfers between devices with their start and end apart: 14 -> 15, of which waited for: 10 -> 10; matrix products, arithmetic and copies ran while one was open for 0% -> 0% of each run, Pallas kernels for 2% -> 3%
where the time goes in v4:
time: 249 us; the launch traced here: 248 us
  blocking collectives  204 us (82%)
  Pallas kernels  19.2 us (8%)
  waiting for transfers between devices  13.1 us (5%)
  starting transfers between devices  7.87 us (3%)
    all_to_all x16, blocking collectives, exchange(): lax.all_to_all(value, axis, 0, 0, tiled=True, axis_index_groups=groups)  204 us
    pallas_call x23, Pallas kernels, call(): pl.pallas_call(kernel, out_shape=out_shape, in_specs=[SMEM] * len(smem) +...  19.2 us
    ppermute x10, waiting for transfers between devices, swap_core(): return lax.ppermute(value, 'blk', [(i, i ^ 1) for i in range(block_count)])  12.8 us
  transfers between devices with their start and end apart: 15, of which 10 were waited for; matrix products, arithmetic and copies ran while one was open for 0% of the time, Pallas kernels for 3%

profile of v4, /device:TPU:0, one launch (start us, length us, event | category | flops | bytes accessed | tf_op | source)
XLA Modules:
  0.0 247.8 jit_solution(1671382335934109541)
XLA Ops:
  1.7 10.5 %all_to_all.80 = bf16[4,192,128]{2,1,0:T(8,128)(2,1)S(1)} all-to-all(bf16[4,192,128]{2,1,0:T(8,128)(2,1)S(1)} %first.1), channel_id=1, replica_groups={{0,2,4,6},{1,3,5,7},{8,10,12,14},{9,11,13,15},{16,18,20,22},{17,19,21,2..., dimensions={0} | all-to-all | bytes 393216 | tf_op jit(solution)/shard_map/all_to_all | solution.py:406
  12.8 1.6 collective-permute-start.2
  14.4 1.5 collective-permute-start.4
  19.0 13.4 %all_to_all.81.parts = bf16[4,192,128]{2,1,0:T(8,128)(2,1)S(1)} all-to-all(bf16[4,192,128]{2,1,0:T(8,128)(2,1)S(1)} %multiply.3), channel_id=1, replica_groups={{0,8,16,24},{32,40,48,56},{64,72,80,88},{96,104,112,120},{1,9,17,25},{3..., dimensions={0} | all-to-all | bytes 393216 | tf_op jit(solution)/shard_map/all_to_all | solution.py:406
  32.4 1.7 lift_lower.1
  34.3 1.9 collective-permute-done.3
  36.4 13.6 %all_to_all.82.parts = bf16[8,4,64,128]{3,2,1,0:T(8,128)(2,1)S(1)} all-to-all(bf16[8,4,64,128]{3,2,1,0:T(8,128)(2,1)S(1)} %bitcast.39), channel_id=1, replica_groups={{0,8,16,24,32,40,48,56},{64,72,80,88,96,104,112,120},{1,9,17,25,33,41,4..., dimensions={0} | all-to-all | bytes 1048576 | tf_op jit(solution)/shard_map/all_to_all | solution.py:406
  50.1 12.4 %all_to_all.83.parts = bf16[4,576,128]{2,1,0:T(8,128)(2,1)S(1)} all-to-all(bf16[4,576,128]{2,1,0:T(8,128)(2,1)S(1)} %rest.2), channel_id=1, replica_groups={{0,2,4,6},{1,3,5,7},{8,10,12,14},{9,11,13,15},{16,18,20,22},{17,19,21,2..., dimensions={0} | all-to-all | bytes 1179648 | tf_op jit(solution)/shard_map/all_to_all | solution.py:406
  62.7 1.3 collective-permute-done.5.other
  64.9 12.0 %all_to_all.84 = bf16[16,64,128]{2,1,0:T(8,128)(2,1)S(1)} all-to-all(bf16[16,64,128]{2,1,0:T(8,128)(2,1)S(1)} %bitcast.28), channel_id=1, replica_groups={{0,2,8,10,16,18,24,26,32,34,40,42,48,50,56,58},{1,7,9,15,17,23,25,31,33..., dimensions={0} | all-to-all | bytes 524288 | tf_op jit(solution)/shard_map/all_to_all | solution.py:406
  76.9 3.8 %lift_pair.1 = (bf16[2,64,128]{2,1,0:T(8,128)(2,1)S(1)}, bf16[64,64,128]{2,1,0:T(8,128)(2,1)S(1)}, bf16[64,64,128]{2,1,0:T(8,128)(2,1)S(1)}) custom-call(s32[7]{0:T(128)S(1)} %copy-done.9, s32[2,64]{1,0:T(2,128)S(1)} %copy-done.12, s32[4,32]{1,0:T(4,128)S(1)} %copy-done.10, bf16[8,2,64,128]{3,2,1,0:T(8,128)(2,1)S(1)} %bitcast.31, ...), custom_call_target="tpu_custom_call" | custom-call | tf_op jit(solution)/shard_map/lift_pair/pallas_call | solution.py:46
  82.1 1.7 collective-permute-done.6
  84.2 23.6 %all_to_all.85.parts = bf16[16,4,64,128]{3,2,1,0:T(8,128)(2,1)S(1)} all-to-all(bf16[16,4,64,128]{3,2,1,0:T(8,128)(2,1)S(1)} %bitcast.38), channel_id=1, replica_groups=mesh['leaf'=16,'blk'=8] {'leaf'}, dimensions={0} | all-to-all | bytes 2097152 | tf_op jit(solution)/shard_map/all_to_all | solution.py:406
  107.9 9.8 %all_to_all.86.parts = bf16[4,4,64,128]{3,2,1,0:T(8,128)(2,1)S(1)} all-to-all(bf16[4,4,64,128]{3,2,1,0:T(8,128)(2,1)S(1)} %rest.3), channel_id=1, replica_groups={{0,2,4,6},{1,3,5,7},{8,10,12,14},{9,11,13,15},{16,18,20,22},{17,19,21,2..., dimensions={0} | all-to-all | bytes 524288 | tf_op jit(solution)/shard_map/all_to_all | solution.py:406
  117.9 1.3 collective-permute-done.8.other
  119.3 1.4 multiply.5
  120.7 14.8 %all_to_all.87.parts = bf16[16,128,128]{2,1,0:T(8,128)(2,1)S(1)} all-to-all(bf16[16,128,128]{2,1,0:T(8,128)(2,1)S(1)} %multiply.5), channel_id=1, replica_groups=mesh['leaf'=16,'blk'=8] {'leaf'}, dimensions={0} | all-to-all | bytes 1048576 | tf_op jit(solution)/shard_map/all_to_all | solution.py:406
  135.6 14.0 %all_to_all.88.gathered = bf16[16,128,128]{2,1,0:T(8,128)(2,1)S(1)} all-to-all(bf16[16,128,128]{2,1,0:T(8,128)(2,1)S(1)} %get-tuple-element.370), channel_id=1, replica_groups=mesh['leaf'=16,'blk'=8] {'leaf'}, dimensions={0} | all-to-all | bytes 1048576 | tf_op jit(solution)/shard_map/all_to_all | solution.py:406
  150.4 1.3 collective-permute-done.9.theirs
  151.7 9.6 %all_to_all.89.parts = bf16[4,4,64,128]{3,2,1,0:T(8,128)(2,1)S(1)} all-to-all(bf16[4,4,64,128]{3,2,1,0:T(8,128)(2,1)S(1)} %split.2), channel_id=1, replica_groups={{0,2,4,6},{1,3,5,7},{8,10,12,14},{9,11,13,15},{16,18,20,22},{17,19,21,2..., dimensions={0} | all-to-all | bytes 524288 | tf_op jit(solution)/shard_map/all_to_all | solution.py:406
  162.0 19.6 %all_to_all.90 = bf16[16,4,64,128]{3,2,1,0:T(8,128)(2,1)S(1)} all-to-all(bf16[16,4,64,128]{3,2,1,0:T(8,128)(2,1)S(1)} %get-tuple-element.403), channel_id=1, replica_groups=mesh['leaf'=16,'blk'=8] {'leaf'}, dimensions={0} | all-to-all | bytes 2097152 | tf_op jit(solution)/shard_map/all_to_all | solution.py:406
  181.6 2.7 %collective-permute-done.10.other = bf16[64,64,128]{2,1,0:T(8,128)(2,1)S(1)} collective-permute-done((bf16[64,64,128]{2,1,0:T(8,128)(2,1)S(1)}, bf16[64,64,128]{2,1,0:T(8,128)(2,1)S(1)}, u32[]{:S(2)}, u32[]{:S(2)}) %collective-permute-start.10) | collective-permute-done | bytes 1048608 | tf_op jit(solution)/shard_map/ppermute | solution.py:385
  184.3 2.4 reduced.2
  186.7 10.0 %all_to_all.91 = bf16[16,64,128]{2,1,0:T(8,128)(2,1)S(1)} all-to-all(bf16[16,64,128]{2,1,0:T(8,128)(2,1)S(1)} %bitcast.30), channel_id=1, replica_groups={{0,2,8,10,16,18,24,26,32,34,40,42,48,50,56,58},{1,7,9,15,17,23,25,31,33..., dimensions={0} | all-to-all | bytes 524288 | tf_op jit(solution)/shard_map/all_to_all | solution.py:406
  198.6 10.3 %all_to_all.92.parts = bf16[4,4,64,128]{3,2,1,0:T(8,128)(2,1)S(1)} all-to-all(bf16[4,4,64,128]{3,2,1,0:T(8,128)(2,1)S(1)} %split.3), channel_id=1, replica_groups={{0,2,4,6},{1,3,5,7},{8,10,12,14},{9,11,13,15},{16,18,20,22},{17,19,21,2..., dimensions={0} | all-to-all | bytes 524288 | tf_op jit(solution)/shard_map/all_to_all | solution.py:406
  209.6 12.2 %all_to_all.93 = bf16[8,4,64,128]{3,2,1,0:T(8,128)(2,1)S(1)} all-to-all(bf16[8,4,64,128]{3,2,1,0:T(8,128)(2,1)S(1)} %get-tuple-element.470), channel_id=1, replica_groups={{0,8,16,24,32,40,48,56},{64,72,80,88,96,104,112,120},{1,9,17,25,33,41,4..., dimensions={0} | all-to-all | bytes 1048576 | tf_op jit(solution)/shard_map/all_to_all | solution.py:406
  222.4 1.6 pull.1.refs_0_
  224.0 1.6 reduced.3
  225.9 9.5 %all_to_all.94 = bf16[8,64,128]{2,1,0:T(8,128)(2,1)S(1)} all-to-all(bf16[8,64,128]{2,1,0:T(8,128)(2,1)S(1)} %bitcast.32), channel_id=1, replica_groups={{0,2,8,10,16,18,24,26},{1,7,9,15,17,23,25,31},{4,6,12,14,20,22,28,30},{..., dimensions={0} | all-to-all | bytes 262144 | tf_op jit(solution)/shard_map/all_to_all | solution.py:406
  235.7 1.3 collective-permute-start.14
  238.0 8.5 %all_to_all.95.parts = bf16[4,128,128]{2,1,0:T(8,128)(2,1)S(1)} all-to-all(bf16[4,128,128]{2,1,0:T(8,128)(2,1)S(1)} %add_convert_fusion.2), channel_id=1, replica_groups={{0,2,4,6},{1,3,5,7},{8,10,12,14},{9,11,13,15},{16,18,20,22},{17,19,21,2..., dimensions={0} | all-to-all | bytes 262144 | tf_op jit(solution)/shard_map/all_to_all | solution.py:406
  246.5 1.3 last.1
  (71 shorter events, 14.8 us)
Async XLA Ops:
  0.6 31.8 %copy-start.3 = (bf16[128,4096]{1,0:T(8,128)(2,1)S(1)}, bf16[128,4096]{1,0:T(8,128)(2,1)}, u32[]{:S(2)}) copy-start(bf16[128,4096]{1,0:T(8,128)(2,1)} %factor.7) | copy-start | bytes 3145732
  0.6 1.0 copy-start.7
  1.7 30.7 %copy-start.9 = (s32[7]{0:T(128)S(1)}, s32[7]{0:T(128)}, u32[]{:S(2)}) copy-start(s32[7]{0:T(128)} %node_blocks.9) | copy-start | bytes 88
  1.7 30.7 %copy-start.11 = (s32[4,32]{1,0:T(4,128)S(1)}, s32[4,32]{1,0:T(4,128)}, u32[]{:S(2)}) copy-start(s32[4,32]{1,0:T(4,128)} %pattern.9) | copy-start | bytes 1540
  12.2 20.1 %collective-permute-start.1 = (bf16[128,4096]{1,0:T(8,128)(2,1)}, bf16[128,4096]{1,0:T(8,128)(2,1)S(1)}, u32[]{:S(2)}, u32[]{:S(2)}) collective-permute-start(bf16[128,4096]{1,0:T(8,128)(2,1)} %factor.6), channel_id=1, source_target_pairs={{0,2},{1,7},{2,0},{3,5},{4,6},{5,3},{6,4},{7,1},{8,10},{9,15},{10,... | collective-permute-start | bytes 3145736 | tf_op jit(solution)/shard_map/ppermute | solution.py:388
  12.8 19.6 %collective-permute-start.2 = (bf16[128,4096]{1,0:T(8,128)(2,1)}, bf16[128,4096]{1,0:T(8,128)(2,1)S(1)}, u32[]{:S(2)}, u32[]{:S(2)}) collective-permute-start(bf16[128,4096]{1,0:T(8,128)(2,1)} %factor.7), channel_id=1, source_target_pairs={{0,8},{1,25},{2,10},{3,27},{4,12},{5,29},{6,14},{7,31},{8,0},{9,17... | collective-permute-start | bytes 3145736 | tf_op jit(solution)/shard_map/ppermute | solution.py:395
  14.4 35.7 %collective-permute-start.4 = (bf16[128,8192]{1,0:T(8,128)(2,1)}, bf16[128,8192]{1,0:T(8,128)(2,1)S(1)}, u32[]{:S(2)}, u32[]{:S(2)}) collective-permute-start(bf16[128,8192]{1,0:T(8,128)(2,1)} %factor.5), channel_id=1, source_target_pairs={{0,2},{1,7},{2,0},{3,5},{4,6},{5,3},{6,4},{7,1},{8,10},{9,15},{10,... | collective-permute-start | bytes 6291464 | tf_op jit(solution)/shard_map/ppermute | solution.py:388
  15.9 1.4 collective-permute-start
  17.3 1.2 copy-start.4
  32.4 17.6 %copy-start.8 = (f32[3,128,128]{2,1,0:T(8,128)S(1)}, f32[3,128,128]{2,1,0:T(8,128)}, u32[]{:S(2)}) copy-start(f32[3,128,128]{2,1,0:T(8,128)} %loads.3) | copy-start | bytes 589828
  34.2 2.0 collective-permute-start.3
  36.4 27.7 %copy-start.1 = (bf16[1,1,1024,1024]{3,2,1,0:T(8,128)(2,1)S(1)}, bf16[1,1,1024,1024]{3,2,1,0:T(8,128)(2,1)}, u32[]{:S(2)}) copy-start(bf16[1,1,1024,1024]{3,2,1,0:T(8,128)(2,1)} %param.13) | copy-start | bytes 6291460
  62.5 14.4 %copy-start.2 = (bf16[128,8192]{1,0:T(8,128)(2,1)S(1)}, bf16[128,8192]{1,0:T(8,128)(2,1)}, u32[]{:S(2)}) copy-start(bf16[128,8192]{1,0:T(8,128)(2,1)} %factor.5) | copy-start | bytes 6291460
  62.5 14.4 %copy-start.6 = (bf16[128,4096]{1,0:T(8,128)(2,1)S(1)}, bf16[128,4096]{1,0:T(8,128)(2,1)}, u32[]{:S(2)}) copy-start(bf16[128,4096]{1,0:T(8,128)(2,1)} %factor.6) | copy-start | bytes 3145732
  62.5 14.4 %copy-start.10 = (s32[4,32]{1,0:T(4,128)S(1)}, s32[4,32]{1,0:T(4,128)}, u32[]{:S(2)}) copy-start(s32[4,32]{1,0:T(4,128)} %pattern.8) | copy-start | bytes 1540
  62.5 14.4 %copy-start.12 = (s32[2,64]{1,0:T(2,128)S(1)}, s32[2,64]{1,0:T(2,128)}, u32[]{:S(2)}) copy-start(s32[2,64]{1,0:T(2,128)} %pattern.7) | copy-start | bytes 1540
  62.6 1.4 collective-permute-start.5
  80.7 3.1 %collective-permute-start.6 = (bf16[64,64,128]{2,1,0:T(8,128)(2,1)S(1)}, bf16[64,64,128]{2,1,0:T(8,128)(2,1)S(1)}, u32[]{:S(2)}, u32[]{:S(2)}) collective-permute-start(bf16[64,64,128]{2,1,0:T(8,128)(2,1)S(1)} %get-tuple-element.327), channel_id=1, source_target_pairs={{0,1},{1,0},{2,3},{3,2},{4,5},{5,4},{6,7},{7,6},{8,9},{9,8},{10,11... | collective-permute-start | bytes 3145736 | tf_op jit(solution)/shard_map/ppermute | solution.py:385
  81.5 26.4 %collective-permute-start.7 = (bf16[128,4096]{1,0:T(8,128)(2,1)S(1)}, bf16[128,4096]{1,0:T(8,128)(2,1)S(1)}, u32[]{:S(2)}, u32[]{:S(2)}) collective-permute-start(bf16[128,4096]{1,0:T(8,128)(2,1)S(1)} %copy-done.3), channel_id=1, source_target_pairs={{0,2},{1,7},{2,0},{3,5},{4,6},{5,3},{6,4},{7,1},{8,10},{9,15},{10,... | collective-permute-start | bytes 3145736 | tf_op jit(solution)/shard_map/ppermute | solution.py:388
  84.2 35.1 %copy-start = (bf16[1,1,2048,1024]{3,2,1,0:T(8,128)(2,1)S(1)}, bf16[1,1,2048,1024]{3,2,1,0:T(8,128)(2,1)}, u32[]{:S(2)}) copy-start(bf16[1,1,2048,1024]{3,2,1,0:T(8,128)(2,1)} %param.12) | copy-start | bytes 12582916
  117.8 1.4 collective-permute-start.8
  150.3 1.4 collective-permute-start.9
  181.6 2.7 %collective-permute-start.10 = (bf16[64,64,128]{2,1,0:T(8,128)(2,1)S(1)}, bf16[64,64,128]{2,1,0:T(8,128)(2,1)S(1)}, u32[]{:S(2)}, u32[]{:S(2)}) collective-permute-start(bf16[64,64,128]{2,1,0:T(8,128)(2,1)S(1)} %bitcast.19), channel_id=1, source_target_pairs={{0,1},{1,0},{2,3},{3,2},{4,5},{5,4},{6,7},{7,6},{8,9},{9,8},{10,11... | collective-permute-start | bytes 3145736 | tf_op jit(solution)/shard_map/ppermute | solution.py:385
  197.2 1.4 collective-permute-start.11
  221.7 2.3 collective-permute-start.12
  221.7 4.2 %collective-permute-start.13 = (bf16[3,64,128]{2,1,0:T(8,128)(2,1)S(1)}, bf16[3,64,128]{2,1,0:T(8,128)(2,1)S(1)}, u32[]{:S(2)}, u32[]{:S(2)}) collective-permute-start(bf16[3,64,128]{2,1,0:T(8,128)(2,1)S(1)} %pad_maximum_fusion), channel_id=1, source_target_pairs={{0,2},{1,7},{2,0},{3,5},{4,6},{5,3},{6,4},{7,1},{8,10},{9,15},{10,... | collective-permute-start | bytes 147464 | tf_op jit(solution)/shard_map/ppermute | solution.py:388
  224.0 11.4 %copy-start.5 = (bf16[1,1,512,1024]{3,2,1,0:T(8,128)(2,1)S(1)}, bf16[1,1,512,1024]{3,2,1,0:T(8,128)(2,1)}, u32[]{:S(2)}) copy-start(bf16[1,1,512,1024]{3,2,1,0:T(8,128)(2,1)} %param.14) | copy-start | bytes 3145732
  235.7 2.3 collective-permute-start.14

commit v5 on v4

--- a/solution.py
+++ b/solution.py
@@ -42,7 +42,7 @@
     return jnp.where(position < limit, 1.0, 0.0).astype(F32)
 
 
-def call(kernel, name, out_shape, smem, vmem, scratch=(), limit=24):
+def call(kernel, name, out_shape, smem, vmem, scratch=(), limit=24, cost=None):
     return pl.pallas_call(
         kernel,
         out_shape=out_shape,
@@ -50,6 +50,7 @@
         out_specs=jax.tree.map(lambda _: VMEM, out_shape),
         scratch_shapes=list(scratch),
         compiler_params=pltpu.CompilerParams(vmem_limit_bytes=limit * MIB),
+        cost_estimate=cost,
         name=name,
     )(*smem, *vmem)
 
@@ -105,7 +106,7 @@
         out[group, 128:, :] = near[side : side + 64]
 
 
-def multiply(kernel, rows, own, other, tile):
+def multiply(kernel, rows, own, other, tile, cost=None):
     return call(
         kernel,
         "multiply",
@@ -113,6 +114,7 @@
         [],
         [own, other, tile],
         [pltpu.VMEM((tile.shape[1], 128), BF16)],
+        cost=cost,
     )
 
 
@@ -136,6 +138,21 @@
         [],
         [gathered, tile],
     )
+
+
+def transposed_pair_kernel(gathered, tile, near, mine, theirs):
+    first = core_of() == 0
+    rows = [
+        jnp.concatenate([gathered[a, place] for a in range(gathered.shape[0])], axis=1)
+        for place in range(2)
+    ]
+    for chip in range(mine.shape[0]):
+        columns = pl.ds(chip * 256, 256)
+        product = jnp.dot(rows[0], tile[:, columns], preferred_element_type=F32)
+        product = product + jnp.dot(rows[1], near[:, columns], preferred_element_type=F32)
+        even, odd = product[:, :128], product[:, 128:]
+        mine[chip] = jnp.where(first, even, odd)
+        theirs[chip] = jnp.where(first, odd, even).astype(BF16)
 
 
 def place_updates(spans, levels, patterns, values, factors, keep, send, sums):
@@ -265,6 +282,24 @@
             copies[index, place] = value
 
 
+def spread_pair_kernel(node_blocks, mine, far, own, near, copies):
+    lane = lax.axis_index("blk")
+    for place in range(mine.shape[0]):
+        value = mine[place].astype(F32) + far[place].astype(F32)
+        value = (value * live(node_blocks, 1, 2 * place + (lane & 1))).astype(BF16)
+
+        @pl.when(lane >> 1 == place)
+        def _():
+            own[...] = value
+
+        @pl.when(near_of(lane) >> 1 == place)
+        def _():
+            near[...] = value
+
+        for index in range(copies.shape[0]):
+            copies[index, place] = value
+
+
 def root_kernel(parts, solved, copies):
     value = total_of([parts[g] for g in range(parts.shape[0])]).astype(BF16)
     solved[...] = value
@@ -296,7 +331,7 @@
     out[0], out[1] = pulled_of(level, pattern, own, other, factor, near, chosen)
 
 
-def reduce_kernel(level, pattern, own, other, factor, near, solved, *refs):
+def reduce_kernel(level, paired, pattern, own, other, factor, near, solved, *refs):
     earlier, (copies, chosen) = refs[:-2], refs[-2:]
     side = side_of()
     pulled = pulled_of(level, pattern, own, other, factor, near, chosen)
@@ -305,7 +340,7 @@
         for e in earlier:
             value = value + e[place]
         value = (solved[place].astype(F32) - value).astype(BF16)
-        which = side if place == 0 else 1 - side
+        which = place if paired else jnp.where(side == 0, place, 1 - place)
         for index in range(copies.shape[0]):
             copies[index, which] = value
 
@@ -321,9 +356,9 @@
     )
 
 
-def reduced(level, pattern, own, other, factors, solved, earlier, count):
+def reduced(level, paired, pattern, own, other, factors, solved, earlier, count):
     return call(
-        functools.partial(reduce_kernel, level),
+        functools.partial(reduce_kernel, level, paired),
         "reduced",
         array(count, 2, 64, 128),
         [pattern],
@@ -428,6 +463,26 @@
         mine, theirs = multiply_transposed(gathered, tile)
         return mine, swap_core(theirs)
 
+    def swap_far(value):
+        return lax.ppermute(value, "blk", [(i, i ^ 4) for i in range(block_count)])
+
+    def spread_middle(gathered, near):
+        tiles = [tile_middle, near]
+        mine, theirs = call(
+            transposed_pair_kernel, "multiply_transposed",
+            (array(chip_count, 64, 128, dtype=F32), array(chip_count, 64, 128)), [],
+            [gathered, *tiles],
+        )
+        mine = (mine + swap_core(theirs).astype(F32)).astype(BF16)
+        size = leaf_count >> 1
+        kept["own1"], kept["near1"], copies = call(
+            spread_pair_kernel, "spread",
+            (array(64, 128), array(64, 128), array(size, chip_count, 64, 128)),
+            [node_blocks], [mine, swap_far(mine)],
+        )
+        blocks = over_leaf(copies, 1).reshape(-1, 64, 128)
+        return blocks, swap_core(blocks)
+
     def spread(partial_sums, level):
         size = leaf_count >> level
         parts = over_chips(call(split_kernel, "split", halves, [], partial_sums))
@@ -445,11 +500,12 @@
     kept["couples"] = [couple_between, couple_lower, couple_middle]
 
     loaded = over_chips(call(first_kernel, "first", array(chip_count, 192, 128), [], [loads]))
-    lower = [couple_lower, swap_near(kept["couples"][1])]
-    middle = [couple_middle, swap_near(kept["couples"][2])]
+    cost = pl.CostEstimate(flops=int(7.5e9), bytes_accessed=0, transcendentals=0)
+    lower = [couple_lower, swap_near(couple_lower)]
+    middle = [couple_middle, swap_near(couple_middle)]
     own = loaded[:, :128]
     kept["load_root"] = loaded[:, 128:]
-    parts = over_leaf(multiply(multiply_lower_kernel, 192, own, swap_core(own), tile_lower), 2)
+    parts = over_leaf(multiply(multiply_lower_kernel, 192, own, swap_core(own), tile_lower, cost), 2)
     half = (leaf_count >> 1) * chip_count
     parts, lower[1] = lax.optimization_barrier((parts, lower[1]))
     y_lower, own, far, keep, send = call(
@@ -484,23 +540,26 @@
     )
     parts = updates(keep, send, 0)
     kept["near_between"] = near_between
+    kept["tile"] = tile_middle
     parts = over_chips(call(rest_kernel, "rest", halves, [], [parts, kept.pop("load_root")]))
     own = call(join_kernel, "join", array(chip_count, 128, 128), [], [parts])
+    near_tile = swap_near(kept.pop("tile"))
     parts = over_leaf(multiply(multiply_kernel, 128, own, swap_core(own), tile_root), 0)
     kept["y_root"], copies = call(
         root_kernel, "root", (array(128, 128), array(leaf_count, 128, 128)), [], [parts]
     )
-    own, other = spread(backward(over_leaf(copies, 0), tile_root), 0)
+    partial_sums = backward(over_leaf(copies, 0), tile_root)
+    kept["near_tile"] = near_tile
+    own, other = spread(partial_sums, 0)
     copies = reduced(
-        1, pattern_middle, own, other, middle, kept["y_middle"], [], leaf_count >> 1
+        1, True, pattern_middle, own, other, middle, kept["y_middle"], [], leaf_count >> 1
     )
     kept["own_root"], kept["other_root"] = own, other
-    gathered = over_pair(copies, 1).reshape(-1, 128, 128)
-    own, other = spread(backward(gathered, tile_middle), 1)
+    own, other = spread_middle(over_leaf(copies, 1), kept.pop("near_tile"))
     pulled = pull(2, pattern_lower, kept.pop("own_root"), kept.pop("other_root"), lower)
     between = [couple_between, kept.pop("near_between")]
     solved = jnp.stack([kept.pop("y_lower_own"), kept.pop("y_lower_near")])
-    copies = reduced(2, pattern_between, own, other, between, solved, [pulled], leaf_count >> 2)
+    copies = reduced(2, False, pattern_between, own, other, between, solved, [pulled], leaf_count >> 2)
     kept["far"] = swap_near(
         jnp.stack([kept.pop("near0"), kept.pop("near1"), kept["y_middle"][1]])
     )

time: 249 us -> 243 us (0.976)
  blocking collectives: 204 us -> 183 us
  waiting for transfers between devices: 13.1 us -> 20.8 us
  starting transfers between devices: 7.87 us -> 13.9 us
    all_to_all x16 -> x14, blocking collectives: 204 us -> 183 us  [exchange(): lax.all_to_all(value, axis, 0, 0, tiled=True, axis_index_groups=groups)]
    ppermute x0 -> x1, waiting for transfers between devices: none -> 4.96 us  [swap_far(): return lax.ppermute(value, 'blk', [(i, i ^ 4) for i in range(block_count)])]
    all_to_all x0 -> x1, starting transfers between devices: none -> 4.38 us  [exchange(): lax.all_to_all(value, axis, 0, 0, tiled=True, axis_index_groups=groups)]
    all_to_all x0 -> x1, waiting for transfers between devices: none -> 3.04 us  [exchange(): lax.all_to_all(value, axis, 0, 0, tiled=True, axis_index_groups=groups)]
    pallas_call x23 -> x22, Pallas kernels: 19.2 us -> 20.3 us  [call(): pl.pallas_call(kernel, out_shape=out_shape, in_specs=[SMEM] * len(smem) +...]
  transfers between devices with their start and end apart: 15 -> 18, of which waited for: 10 -> 12; matrix products, arithmetic and copies ran while one was open for 0% -> 0% of each run, Pallas kernels for 3% -> 4%
where the time goes in v5:
time: 243 us; the launch traced here: 242 us
  blocking collectives  183 us (75%)
  waiting for transfers between devices  20.8 us (9%)
  Pallas kernels  20.3 us (8%)
  starting transfers between devices  13.9 us (6%)
    all_to_all x14, blocking collectives, exchange(): lax.all_to_all(value, axis, 0, 0, tiled=True, axis_index_groups=groups)  183 us
    pallas_call x22, Pallas kernels, call(): pl.pallas_call(kernel, out_shape=out_shape, in_specs=[SMEM] * len(smem) +...  20.3 us
    ppermute x10, waiting for transfers between devices, swap_core(): return lax.ppermute(value, 'blk', [(i, i ^ 1) for i in range(block_count)])  12.4 us
    ppermute x1, waiting for transfers between devices, swap_far(): return lax.ppermute(value, 'blk', [(i, i ^ 4) for i in range(block_count)])  4.96 us
  transfers between devices with their start and end apart: 18, of which 12 were waited for; matrix products, arithmetic and copies ran while one was open for 0% of the time, Pallas kernels for 4%

profile of v5, /device:TPU:0, one launch (start us, length us, event | category | flops | bytes accessed | tf_op | source)
XLA Modules:
  0.0 242.0 jit_solution(17051417752374988408)
XLA Ops:
  2.3 4.4 %all-to-all-start = ((bf16[4,192,128]{2,1,0:T(8,128)(2,1)}), bf16[4,192,128]{2,1,0:T(8,128)(2,1)S(1)}, u32[]{:S(2)}, u32[]{:S(2)}) async-start(bf16[4,192,128]{2,1,0:T(8,128)(2,1)} %first.1), calls=%async_computation | async-start | bytes 393216 | tf_op jit(solution)/shard_map/all_to_all | solution.py:441
  6.7 2.0 collective-permute-start.1
  8.7 1.6 collective-permute-start.2
  10.3 3.0 %all-to-all-done = bf16[4,192,128]{2,1,0:T(8,128)(2,1)S(1)} async-done(((bf16[4,192,128]{2,1,0:T(8,128)(2,1)}), bf16[4,192,128]{2,1,0:T(8,128)(2,1)S(1)}, u32[]{:S(2)}, u32[]{:S(2)}) %all-to-all-start) | async-done | bytes 196640 | tf_op jit(solution)/shard_map/all_to_all | solution.py:441
  16.5 11.8 %all_to_all.75.parts = bf16[4,192,128]{2,1,0:T(8,128)(2,1)S(1)} all-to-all(bf16[4,192,128]{2,1,0:T(8,128)(2,1)S(1)} %multiply.3), channel_id=1, replica_groups={{0,8,16,24},{32,40,48,56},{64,72,80,88},{96,104,112,120},{1,9,17,25},{3..., dimensions={0} | all-to-all | bytes 393216 | tf_op jit(solution)/shard_map/all_to_all | solution.py:441
  28.3 1.7 lift_lower.1
  30.2 1.9 collective-permute-done.3
  32.3 13.6 %all_to_all.76.parts = bf16[8,4,64,128]{3,2,1,0:T(8,128)(2,1)S(1)} all-to-all(bf16[8,4,64,128]{3,2,1,0:T(8,128)(2,1)S(1)} %bitcast.36), channel_id=1, replica_groups={{0,8,16,24,32,40,48,56},{64,72,80,88,96,104,112,120},{1,9,17,25,33,41,4..., dimensions={0} | all-to-all | bytes 1048576 | tf_op jit(solution)/shard_map/all_to_all | solution.py:441
  46.0 13.0 %all_to_all.77.parts = bf16[4,576,128]{2,1,0:T(8,128)(2,1)S(1)} all-to-all(bf16[4,576,128]{2,1,0:T(8,128)(2,1)S(1)} %rest.2), channel_id=1, replica_groups={{0,2,4,6},{1,3,5,7},{8,10,12,14},{9,11,13,15},{16,18,20,22},{17,19,21,2..., dimensions={0} | all-to-all | bytes 1179648 | tf_op jit(solution)/shard_map/all_to_all | solution.py:441
  59.2 1.3 collective-permute-done.5.other
  61.4 13.2 %all_to_all.78 = bf16[16,64,128]{2,1,0:T(8,128)(2,1)S(1)} all-to-all(bf16[16,64,128]{2,1,0:T(8,128)(2,1)S(1)} %bitcast.25), channel_id=1, replica_groups={{0,2,8,10,16,18,24,26,32,34,40,42,48,50,56,58},{1,7,9,15,17,23,25,31,33..., dimensions={0} | all-to-all | bytes 524288 | tf_op jit(solution)/shard_map/all_to_all | solution.py:441
  74.6 3.8 %lift_pair.1 = (bf16[2,64,128]{2,1,0:T(8,128)(2,1)S(1)}, bf16[64,64,128]{2,1,0:T(8,128)(2,1)S(1)}, bf16[64,64,128]{2,1,0:T(8,128)(2,1)S(1)}) custom-call(s32[7]{0:T(128)S(1)} %copy-done.9, s32[2,64]{1,0:T(2,128)S(1)} %copy-done.12, s32[4,32]{1,0:T(4,128)S(1)} %copy-done.10, bf16[8,2,64,128]{3,2,1,0:T(8,128)(2,1)S(1)} %bitcast.28, ...), custom_call_target="tpu_custom_call" | custom-call | tf_op jit(solution)/shard_map/lift_pair/pallas_call | solution.py:46
  79.8 1.7 collective-permute-done.6
  81.9 23.6 %all_to_all.79.parts = bf16[16,4,64,128]{3,2,1,0:T(8,128)(2,1)S(1)} all-to-all(bf16[16,4,64,128]{3,2,1,0:T(8,128)(2,1)S(1)} %bitcast.35), channel_id=1, replica_groups=mesh['leaf'=16,'blk'=8] {'leaf'}, dimensions={0} | all-to-all | bytes 2097152 | tf_op jit(solution)/shard_map/all_to_all | solution.py:441
  105.6 9.8 %all_to_all.80.parts = bf16[4,4,64,128]{3,2,1,0:T(8,128)(2,1)S(1)} all-to-all(bf16[4,4,64,128]{3,2,1,0:T(8,128)(2,1)S(1)} %rest.3), channel_id=1, replica_groups={{0,2,4,6},{1,3,5,7},{8,10,12,14},{9,11,13,15},{16,18,20,22},{17,19,21,2..., dimensions={0} | all-to-all | bytes 524288 | tf_op jit(solution)/shard_map/all_to_all | solution.py:441
  116.2 1.3 collective-permute-done.8.other
  117.5 1.4 multiply.5
  118.9 14.8 %all_to_all.81.parts = bf16[16,128,128]{2,1,0:T(8,128)(2,1)S(1)} all-to-all(bf16[16,128,128]{2,1,0:T(8,128)(2,1)S(1)} %multiply.5), channel_id=1, replica_groups=mesh['leaf'=16,'blk'=8] {'leaf'}, dimensions={0} | all-to-all | bytes 1048576 | tf_op jit(solution)/shard_map/all_to_all | solution.py:441
  133.8 14.0 %all_to_all.82.gathered = bf16[16,128,128]{2,1,0:T(8,128)(2,1)S(1)} all-to-all(bf16[16,128,128]{2,1,0:T(8,128)(2,1)S(1)} %get-tuple-element.349), channel_id=1, replica_groups=mesh['leaf'=16,'blk'=8] {'leaf'}, dimensions={0} | all-to-all | bytes 1048576 | tf_op jit(solution)/shard_map/all_to_all | solution.py:441
  148.6 1.3 collective-permute-done.9.theirs
  150.0 10.1 %all_to_all.83.parts = bf16[4,4,64,128]{3,2,1,0:T(8,128)(2,1)S(1)} all-to-all(bf16[4,4,64,128]{3,2,1,0:T(8,128)(2,1)S(1)} %split.1), channel_id=1, replica_groups={{0,2,4,6},{1,3,5,7},{8,10,12,14},{9,11,13,15},{16,18,20,22},{17,19,21,2..., dimensions={0} | all-to-all | bytes 524288 | tf_op jit(solution)/shard_map/all_to_all | solution.py:441
  160.8 19.2 %all_to_all.84 = bf16[16,4,64,128]{3,2,1,0:T(8,128)(2,1)S(1)} all-to-all(bf16[16,4,64,128]{3,2,1,0:T(8,128)(2,1)S(1)} %get-tuple-element.385), channel_id=1, replica_groups=mesh['leaf'=16,'blk'=8] {'leaf'}, dimensions={0} | all-to-all | bytes 2097152 | tf_op jit(solution)/shard_map/all_to_all | solution.py:441
  180.0 2.7 %collective-permute-done.11.other = bf16[64,64,128]{2,1,0:T(8,128)(2,1)S(1)} collective-permute-done((bf16[64,64,128]{2,1,0:T(8,128)(2,1)S(1)}, bf16[64,64,128]{2,1,0:T(8,128)(2,1)S(1)}, u32[]{:S(2)}, u32[]{:S(2)}) %collective-permute-start.11) | collective-permute-done | bytes 1048608 | tf_op jit(solution)/shard_map/ppermute | solution.py:420
  182.7 2.4 reduced.2
  185.1 10.3 %all_to_all.85.gathered = bf16[8,2,64,128]{3,2,1,0:T(8,128)(2,1)S(1)} all-to-all(bf16[8,2,64,128]{3,2,1,0:T(8,128)(2,1)S(1)} %reduced.2), channel_id=1, replica_groups={{0,8,16,24,32,40,48,56},{64,72,80,88,96,104,112,120},{1,9,17,25,33,41,4..., dimensions={0} | all-to-all | bytes 524288 | tf_op jit(solution)/shard_map/all_to_all | solution.py:441
  198.4 5.0 %collective-permute-done.13.far = bf16[4,64,128]{2,1,0:T(8,128)(2,1)S(1)} collective-permute-done((bf16[4,64,128]{2,1,0:T(8,128)(2,1)S(1)}, bf16[4,64,128]{2,1,0:T(8,128)(2,1)S(1)}, u32[]{:S(2)}, u32[]{:S(2)}) %collective-permute-start.13) | collective-permute-done | bytes 65568 | tf_op jit(solution)/shard_map/ppermute | solution.py:467
  204.0 12.0 %all_to_all.86 = bf16[8,4,64,128]{3,2,1,0:T(8,128)(2,1)S(1)} all-to-all(bf16[8,4,64,128]{3,2,1,0:T(8,128)(2,1)S(1)} %get-tuple-element.434), channel_id=1, replica_groups={{0,8,16,24,32,40,48,56},{64,72,80,88,96,104,112,120},{1,9,17,25,33,41,4..., dimensions={0} | all-to-all | bytes 1048576 | tf_op jit(solution)/shard_map/all_to_all | solution.py:441
  216.6 1.6 pull.1.refs_0_
  218.2 1.6 reduced.3
  220.2 9.5 %all_to_all.87 = bf16[8,64,128]{2,1,0:T(8,128)(2,1)S(1)} all-to-all(bf16[8,64,128]{2,1,0:T(8,128)(2,1)S(1)} %bitcast.29), channel_id=1, replica_groups={{0,2,8,10,16,18,24,26},{1,7,9,15,17,23,25,31},{4,6,12,14,20,22,28,30},{..., dimensions={0} | all-to-all | bytes 262144 | tf_op jit(solution)/shard_map/all_to_all | solution.py:441
  230.0 1.3 collective-permute-start.16
  232.3 8.5 %all_to_all.88.parts = bf16[4,128,128]{2,1,0:T(8,128)(2,1)S(1)} all-to-all(bf16[4,128,128]{2,1,0:T(8,128)(2,1)S(1)} %add_convert_fusion.2), channel_id=1, replica_groups={{0,2,4,6},{1,3,5,7},{8,10,12,14},{9,11,13,15},{16,18,20,22},{17,19,21,2..., dimensions={0} | all-to-all | bytes 262144 | tf_op jit(solution)/shard_map/all_to_all | solution.py:441
  (75 shorter events, 17.8 us)
Async XLA Ops:
  0.6 0.9 copy-start.7
  2.3 11.0 %all-to-all-start = ((bf16[4,192,128]{2,1,0:T(8,128)(2,1)}), bf16[4,192,128]{2,1,0:T(8,128)(2,1)S(1)}, u32[]{:S(2)}, u32[]{:S(2)}) async-start(bf16[4,192,128]{2,1,0:T(8,128)(2,1)} %first.1), calls=%async_computation | async-start | bytes 393216 | tf_op jit(solution)/shard_map/all_to_all | solution.py:441
  6.7 21.6 %collective-permute-start.1 = (bf16[128,4096]{1,0:T(8,128)(2,1)}, bf16[128,4096]{1,0:T(8,128)(2,1)S(1)}, u32[]{:S(2)}, u32[]{:S(2)}) collective-permute-start(bf16[128,4096]{1,0:T(8,128)(2,1)} %factor.6), channel_id=1, source_target_pairs={{0,2},{1,7},{2,0},{3,5},{4,6},{5,3},{6,4},{7,1},{8,10},{9,15},{10,... | collective-permute-start | bytes 3145736 | tf_op jit(solution)/shard_map/ppermute | solution.py:423
  8.7 19.6 %collective-permute-start.2 = (bf16[128,4096]{1,0:T(8,128)(2,1)}, bf16[128,4096]{1,0:T(8,128)(2,1)S(1)}, u32[]{:S(2)}, u32[]{:S(2)}) collective-permute-start(bf16[128,4096]{1,0:T(8,128)(2,1)} %factor.7), channel_id=1, source_target_pairs={{0,8},{1,25},{2,10},{3,27},{4,12},{5,29},{6,14},{7,31},{8,0},{9,17... | collective-permute-start | bytes 3145736 | tf_op jit(solution)/shard_map/ppermute | solution.py:430
  13.3 1.4 collective-permute-start
  13.4 32.6 %collective-permute-start.4 = (bf16[128,8192]{1,0:T(8,128)(2,1)}, bf16[128,8192]{1,0:T(8,128)(2,1)S(1)}, u32[]{:S(2)}, u32[]{:S(2)}) collective-permute-start(bf16[128,8192]{1,0:T(8,128)(2,1)} %factor.5), channel_id=1, source_target_pairs={{0,2},{1,7},{2,0},{3,5},{4,6},{5,3},{6,4},{7,1},{8,10},{9,15},{10,... | collective-permute-start | bytes 6291464 | tf_op jit(solution)/shard_map/ppermute | solution.py:423
  14.8 1.2 copy-start.5
  16.0 12.3 %copy-start.3 = (bf16[128,4096]{1,0:T(8,128)(2,1)S(1)}, bf16[128,4096]{1,0:T(8,128)(2,1)}, u32[]{:S(2)}) copy-start(bf16[128,4096]{1,0:T(8,128)(2,1)} %factor.7) | copy-start | bytes 3145732
  16.0 12.3 %copy-start.9 = (s32[7]{0:T(128)S(1)}, s32[7]{0:T(128)}, u32[]{:S(2)}) copy-start(s32[7]{0:T(128)} %node_blocks.9) | copy-start | bytes 88
  16.0 12.3 %copy-start.11 = (s32[4,32]{1,0:T(4,128)S(1)}, s32[4,32]{1,0:T(4,128)}, u32[]{:S(2)}) copy-start(s32[4,32]{1,0:T(4,128)} %pattern.9) | copy-start | bytes 1540
  28.3 17.6 %copy-start.8 = (f32[3,128,128]{2,1,0:T(8,128)S(1)}, f32[3,128,128]{2,1,0:T(8,128)}, u32[]{:S(2)}) copy-start(f32[3,128,128]{2,1,0:T(8,128)} %loads.3) | copy-start | bytes 589828
  30.1 2.0 collective-permute-start.3
  32.2 28.3 %copy-start.1 = (bf16[1,1,1024,1024]{3,2,1,0:T(8,128)(2,1)S(1)}, bf16[1,1,1024,1024]{3,2,1,0:T(8,128)(2,1)}, u32[]{:S(2)}) copy-start(bf16[1,1,1024,1024]{3,2,1,0:T(8,128)(2,1)} %param.13) | copy-start | bytes 6291460
  59.0 15.6 %copy-start.2 = (bf16[128,8192]{1,0:T(8,128)(2,1)S(1)}, bf16[128,8192]{1,0:T(8,128)(2,1)}, u32[]{:S(2)}) copy-start(bf16[128,8192]{1,0:T(8,128)(2,1)} %factor.5) | copy-start | bytes 6291460
  59.0 15.6 %copy-start.4 = (bf16[128,4096]{1,0:T(8,128)(2,1)S(1)}, bf16[128,4096]{1,0:T(8,128)(2,1)}, u32[]{:S(2)}) copy-start(bf16[128,4096]{1,0:T(8,128)(2,1)} %factor.6) | copy-start | bytes 3145732
  59.0 15.6 %copy-start.10 = (s32[4,32]{1,0:T(4,128)S(1)}, s32[4,32]{1,0:T(4,128)}, u32[]{:S(2)}) copy-start(s32[4,32]{1,0:T(4,128)} %pattern.8) | copy-start | bytes 1540
  59.0 15.6 %copy-start.12 = (s32[2,64]{1,0:T(2,128)S(1)}, s32[2,64]{1,0:T(2,128)}, u32[]{:S(2)}) copy-start(s32[2,64]{1,0:T(2,128)} %pattern.7) | copy-start | bytes 1540
  59.1 1.4 collective-permute-start.5
  78.4 3.1 %collective-permute-start.6 = (bf16[64,64,128]{2,1,0:T(8,128)(2,1)S(1)}, bf16[64,64,128]{2,1,0:T(8,128)(2,1)S(1)}, u32[]{:S(2)}, u32[]{:S(2)}) collective-permute-start(bf16[64,64,128]{2,1,0:T(8,128)(2,1)S(1)} %get-tuple-element.305), channel_id=1, source_target_pairs={{0,1},{1,0},{2,3},{3,2},{4,5},{5,4},{6,7},{7,6},{8,9},{9,8},{10,11... | collective-permute-start | bytes 3145736 | tf_op jit(solution)/shard_map/ppermute | solution.py:420
  79.2 26.4 %collective-permute-start.7 = (bf16[128,4096]{1,0:T(8,128)(2,1)S(1)}, bf16[128,4096]{1,0:T(8,128)(2,1)S(1)}, u32[]{:S(2)}, u32[]{:S(2)}) collective-permute-start(bf16[128,4096]{1,0:T(8,128)(2,1)S(1)} %copy-done.3), channel_id=1, source_target_pairs={{0,2},{1,7},{2,0},{3,5},{4,6},{5,3},{6,4},{7,1},{8,10},{9,15},{10,... | collective-permute-start | bytes 3145736 | tf_op jit(solution)/shard_map/ppermute | solution.py:423
  81.9 35.6 %copy-start = (bf16[1,1,2048,1024]{3,2,1,0:T(8,128)(2,1)S(1)}, bf16[1,1,2048,1024]{3,2,1,0:T(8,128)(2,1)}, u32[]{:S(2)}) copy-start(bf16[1,1,2048,1024]{3,2,1,0:T(8,128)(2,1)} %param.12) | copy-start | bytes 12582916
  115.5 34.5 %collective-permute-start.10 = (bf16[1024,1024]{1,0:T(8,128)(2,1)S(1)}, bf16[1024,1024]{1,0:T(8,128)(2,1)S(1)}, u32[]{:S(2)}, u32[]{:S(2)}) collective-permute-start(bf16[1024,1024]{1,0:T(8,128)(2,1)S(1)} %bitcast.21), channel_id=1, source_target_pairs={{0,2},{1,7},{2,0},{3,5},{4,6},{5,3},{6,4},{7,1},{8,10},{9,15},{10,... | collective-permute-start | bytes 6291464 | tf_op jit(solution)/shard_map/ppermute | solution.py:423
  116.1 1.4 collective-permute-start.8
  148.5 1.4 collective-permute-start.9
  180.0 2.7 %collective-permute-start.11 = (bf16[64,64,128]{2,1,0:T(8,128)(2,1)S(1)}, bf16[64,64,128]{2,1,0:T(8,128)(2,1)S(1)}, u32[]{:S(2)}, u32[]{:S(2)}) collective-permute-start(bf16[64,64,128]{2,1,0:T(8,128)(2,1)S(1)} %bitcast.17), channel_id=1, source_target_pairs={{0,1},{1,0},{2,3},{3,2},{4,5},{5,4},{6,7},{7,6},{8,9},{9,8},{10,11... | collective-permute-start | bytes 3145736 | tf_op jit(solution)/shard_map/ppermute | solution.py:420
  196.2 1.3 collective-permute-start.12
  197.5 5.8 %collective-permute-start.13 = (bf16[4,64,128]{2,1,0:T(8,128)(2,1)S(1)}, bf16[4,64,128]{2,1,0:T(8,128)(2,1)S(1)}, u32[]{:S(2)}, u32[]{:S(2)}) collective-permute-start(bf16[4,64,128]{2,1,0:T(8,128)(2,1)S(1)} %add_convert_fusion.3.mine), channel_id=1, source_target_pairs={{0,4},{1,5},{2,6},{3,7},{4,0},{5,1},{6,2},{7,3},{8,12},{9,13},{10,... | collective-permute-start | bytes 196616 | tf_op jit(solution)/shard_map/ppermute | solution.py:467
  216.0 2.2 collective-permute-start.14
  216.0 4.2 %collective-permute-start.15 = (bf16[3,64,128]{2,1,0:T(8,128)(2,1)S(1)}, bf16[3,64,128]{2,1,0:T(8,128)(2,1)S(1)}, u32[]{:S(2)}, u32[]{:S(2)}) collective-permute-start(bf16[3,64,128]{2,1,0:T(8,128)(2,1)S(1)} %pad_maximum_fusion), channel_id=1, source_target_pairs={{0,2},{1,7},{2,0},{3,5},{4,6},{5,3},{6,4},{7,1},{8,10},{9,15},{10,... | collective-permute-start | bytes 147464 | tf_op jit(solution)/shard_map/ppermute | solution.py:423
  218.2 11.4 %copy-start.6 = (bf16[1,1,512,1024]{3,2,1,0:T(8,128)(2,1)S(1)}, bf16[1,1,512,1024]{3,2,1,0:T(8,128)(2,1)}, u32[]{:S(2)}) copy-start(bf16[1,1,512,1024]{3,2,1,0:T(8,128)(2,1)} %param.14) | copy-start | bytes 3145732
  230.0 2.3 collective-permute-start.16

commit v6 on v5

--- a/solution.py
+++ b/solution.py
@@ -12,6 +12,7 @@
 MIB = 1024 * 1024
 SMEM = pl.BlockSpec(memory_space=pltpu.SMEM)
 VMEM = pl.BlockSpec(memory_space=pltpu.VMEM)
+ANY = pl.BlockSpec(memory_space=pl.ANY)
 
 
 def near_of(lane):
@@ -42,11 +43,15 @@
     return jnp.where(position < limit, 1.0, 0.0).astype(F32)
 
 
-def call(kernel, name, out_shape, smem, vmem, scratch=(), limit=24, cost=None):
+def with_scalars(count, kernel):
+    return lambda *refs: kernel(refs[:count], *refs[count:])
+
+
+def call(kernel, name, out_shape, smem, vmem, scratch=(), limit=24, cost=None, smem_spec=SMEM):
     return pl.pallas_call(
         kernel,
         out_shape=out_shape,
-        in_specs=[SMEM] * len(smem) + [VMEM] * len(vmem),
+        in_specs=[smem_spec] * len(smem) + [VMEM] * len(vmem),
         out_specs=jax.tree.map(lambda _: VMEM, out_shape),
         scratch_shapes=list(scratch),
         compiler_params=pltpu.CompilerParams(vmem_limit_bytes=limit * MIB),
@@ -93,6 +98,34 @@
     gather_columns(True, own, other, columns)
     for group in range(out.shape[0]):
         out[group] = partial_of(tile, columns, group)
+
+
+def columns_of(blocks, core, tile, group):
+    rows = slice(group * 128, group * 128 + 128)
+    factors = [
+        tile[rows, pl.ds(pl.multiple_of((2 * chip + core) * 128, 128), 128)]
+        for chip in range(blocks.shape[0] // 128)
+    ]
+    factors = jnp.concatenate(factors, axis=1)
+    return jnp.dot(factors, blocks[...], preferred_element_type=F32)
+
+
+def stack_columns(blocks, columns):
+    for chip in range(blocks.shape[0]):
+        columns[chip * 128 : chip * 128 + 128, :] = blocks[chip].T
+
+
+def multiply_own_kernel(own, tile, out, columns):
+    stack_columns(own, columns)
+    for group in range(out.shape[0]):
+        out[group] = columns_of(columns, core_of(), tile, group)
+
+
+def multiply_rest_kernel(other, mine, tile, out, columns):
+    stack_columns(other, columns)
+    for group in range(out.shape[0]):
+        product = mine[group] + columns_of(columns, 1 - core_of(), tile, group)
+        out[group] = product.astype(BF16).T
 
 
 def multiply_lower_kernel(own, other, tile, out, columns):
@@ -155,10 +188,26 @@
         theirs[chip] = jnp.where(first, odd, even).astype(BF16)
 
 
+def fetch_scalars(sources, targets, semaphores, sums):
+    copies = [
+        pltpu.make_async_copy(source, target, semaphores.at[index])
+        for index, (source, target) in enumerate(zip(sources, targets))
+    ]
+    for copy in copies:
+        copy.start()
+    sums[...] = jnp.zeros_like(sums)
+    for copy in copies:
+        copy.wait()
+
+
+def scalar_scratch(*sources):
+    shapes = [pltpu.SMEM(source.shape, jnp.int32) for source in sources]
+    return [*shapes, pltpu.SemaphoreType.DMA((len(sources),))]
+
+
 def place_updates(spans, levels, patterns, values, factors, keep, send, sums):
     core = core_of()
     half = keep.shape[0]
-    sums[...] = jnp.zeros_like(sums)
     for index, span in enumerate(spans):
         node = node_of(levels[index])
 
@@ -172,7 +221,7 @@
                 sums[slot] += product[:, part * 128 : part * 128 + 128]
             return carry
 
-        lax.fori_loop(0, span // 1024, chunk, 0)
+        lax.fori_loop(0, span // 1024, chunk, 0, unroll=2)
 
     def emit(slot, carry):
         keep[slot] = sums[slot].astype(BF16)
@@ -182,13 +231,20 @@
     lax.fori_loop(0, half, emit, 0, unroll=4)
 
 
-def lower_kernel(node_blocks, pattern, parts, factor, near, solved, own, far, keep, send, sums):
+def lower_kernel(
+    scalars, parts, factor, near, solved, own, far, masks, keep, send, sums, *scratch
+):
+    node_blocks, pattern, semaphores = scratch
+    fetch_scalars(scalars, scratch[:-1], semaphores, sums)
     leaf, lane = lax.axis_index("leaf"), lax.axis_index("blk")
     total = total_of([parts[g, :128, :] for g in range(parts.shape[0])])
     value = (total * live(node_blocks, 2, lane)).astype(BF16)
     total = total_of([parts[g, 128:, :] for g in range(parts.shape[0])])
     partner = (total * live(node_blocks, 2, lane, leaf_near_of(leaf, lane))).astype(BF16)
     solved[...] = value
+    for place in range(masks.shape[0] - 1):
+        masks[place] = jnp.full((8, 128), live(node_blocks, 1, 2 * place + (lane & 1)), F32)
+    masks[masks.shape[0] - 1] = jnp.full((8, 128), live(node_blocks, 2, lane), F32)
     first = side_of() == 0
     low, high = value[:64], value[64:]
     own[...] = jnp.where(first, low, high)
@@ -198,8 +254,10 @@
     place_updates(spans, (2,), [pattern], [values], [[factor, near]], keep, send, sums)
 
 
-def pair_kernel(node_blocks, pattern, pattern_lower, parts, lower, lower_near, *refs):
-    factors, (solved, keep, send, sums) = refs[:4], refs[4:]
+def pair_kernel(scalars, parts, lower, lower_near, *refs):
+    factors, (solved, keep, send, sums, *scratch) = refs[:4], refs[4:]
+    node_blocks, pattern, pattern_lower, semaphores = scratch
+    fetch_scalars(scalars, scratch[:-1], semaphores, sums)
     side, lane = side_of(), lax.axis_index("blk")
     for place in range(2):
         which = side if place == 0 else 1 - side
@@ -227,24 +285,15 @@
             copies[index, place] = value
 
 
-def rest_middle_kernel(parts, loads, far, copies):
+def rest_middle_kernel(parts, loads, far, out):
     chip = lax.axis_index("blk") >> 1
     load = loads[1].T
     for place in range(parts.shape[1]):
         total = [total_of([parts[g, place] for g in range(y, parts.shape[0], 2)]) for y in range(2)]
         total = jnp.concatenate(total, axis=0)
         value = (jnp.where(chip == place, load, 0.0) - total).astype(BF16)
-        for index in range(copies.shape[0]):
-            copies[index, place * 128 : place * 128 + 128, :] = value
-    for index in range(copies.shape[0]):
-        copies[index, parts.shape[1] * 128 :, :] = far[...]
-
-
-def join_middle_kernel(parts, out, near):
-    for place in range(out.shape[0]):
-        rows = pl.ds(place * 128, 128)
-        out[place] = total_of([parts[x, rows, :] for x in range(parts.shape[0])]).astype(BF16)
-    near[...] = parts[near_of(lax.axis_index("blk")) >> 1, out.shape[0] * 128 :, :]
+        out[place * 128 : place * 128 + 128, :] = value
+    out[parts.shape[1] * 128 :, :] = far[...]
 
 
 def join_kernel(parts, out):
@@ -262,12 +311,10 @@
             out[chip, place] = value[side : side + 64]
 
 
-def spread_kernel(level, node_blocks, parts, own, near, copies):
+def spread_kernel(parts, own, near, copies):
     lane = lax.axis_index("blk")
     for place in range(parts.shape[1]):
         value = total_of([parts[x, place] for x in range(parts.shape[0])])
-        if level:
-            value = value * live(node_blocks, level, 2 * place + (lane & 1))
         value = value.astype(BF16)
 
         @pl.when(lane >> 1 == place)
@@ -282,11 +329,11 @@
             copies[index, place] = value
 
 
-def spread_pair_kernel(node_blocks, mine, far, own, near, copies):
+def spread_pair_kernel(mine, far, masks, own, near, copies):
     lane = lax.axis_index("blk")
     for place in range(mine.shape[0]):
         value = mine[place].astype(F32) + far[place].astype(F32)
-        value = (value * live(node_blocks, 1, 2 * place + (lane & 1))).astype(BF16)
+        value = (value * masks[place, :1, :]).astype(BF16)
 
         @pl.when(lane >> 1 == place)
         def _():
@@ -318,13 +365,14 @@
         return carry
 
     lax.fori_loop(0, pattern.shape[1], pick, 0, unroll=4)
-    result = []
-    for rows in (factor, near):
-        product = lax.dot_general(
-            rows[...], chosen[...], (((1,), (1,)), ((), ())), preferred_element_type=F32
+    product = jnp.zeros((256, 64), F32)
+    for start in range(0, chosen.shape[1], 1024):
+        columns = slice(start, start + 1024)
+        rows = jnp.concatenate([factor[:, columns], near[:, columns]], axis=0)
+        product = product + lax.dot_general(
+            rows, chosen[:, columns], (((1,), (1,)), ((), ())), preferred_element_type=F32
         )
-        result.append(product.T)
-    return result
+    return product[:128].T, product[128:].T
 
 
 def pull_kernel(level, pattern, own, other, factor, near, out, chosen):
@@ -379,11 +427,11 @@
     out[2] = lower[...].T
 
 
-def last_kernel(node_blocks, parts, root, middle, far, out):
+def last_kernel(masks, parts, root, middle, far, out):
     out[0] = whole(root[...], far[0])
     out[1] = whole(middle[...], far[1])
     total = total_of([parts[x] for x in range(parts.shape[0])])
-    out[2] = (total * live(node_blocks, 2, lax.axis_index("blk"))).astype(BF16).T
+    out[2] = (total * masks[masks.shape[0] - 1, :1, :]).astype(BF16).T
 
 
 def shards(
@@ -422,6 +470,9 @@
     def swap_near(value):
         return lax.ppermute(value, "blk", [(i, near_of(i)) for i in range(block_count)])
 
+    def swap_far(value):
+        return lax.ppermute(value, "blk", [(i, i ^ 4) for i in range(block_count)])
+
     def swap_leaf_near(value):
         pairs = []
         for i in range(leaf_count * block_count):
@@ -462,9 +513,6 @@
     def backward(gathered, tile):
         mine, theirs = multiply_transposed(gathered, tile)
         return mine, swap_core(theirs)
-
-    def swap_far(value):
-        return lax.ppermute(value, "blk", [(i, i ^ 4) for i in range(block_count)])
 
     def spread_middle(gathered, near):
         tiles = [tile_middle, near]
@@ -475,24 +523,25 @@
         )
         mine = (mine + swap_core(theirs).astype(F32)).astype(BF16)
         size = leaf_count >> 1
+        kept["pulled"] = pull(
+            2, pattern_lower, kept.pop("own_root"), kept.pop("other_root"), kept.pop("lower")
+        )
         kept["own1"], kept["near1"], copies = call(
             spread_pair_kernel, "spread",
             (array(64, 128), array(64, 128), array(size, chip_count, 64, 128)),
-            [node_blocks], [mine, swap_far(mine)],
+            [], [mine, swap_far(mine), kept["masks"]],
         )
         blocks = over_leaf(copies, 1).reshape(-1, 64, 128)
         return blocks, swap_core(blocks)
 
-    def spread(partial_sums, level):
-        size = leaf_count >> level
+    def spread_root(partial_sums):
         parts = over_chips(call(split_kernel, "split", halves, [], partial_sums))
-        own, near, copies = call(
-            functools.partial(spread_kernel, level), "spread",
-            (array(64, 128), array(64, 128), array(size, chip_count, 64, 128)),
-            [node_blocks], [parts],
+        kept["own0"], kept["near0"], copies = call(
+            spread_kernel, "spread",
+            (array(64, 128), array(64, 128), array(leaf_count, chip_count, 64, 128)),
+            [], [parts],
         )
-        kept[f"own{level}"], kept[f"near{level}"] = own, near
-        blocks = over_leaf(copies, level).reshape(-1, 64, 128)
+        blocks = over_leaf(copies, 0).reshape(-1, 64, 128)
         return blocks, swap_core(blocks)
 
     tile_root, tile_middle, tile_lower = inverse_root[0, 0], inverse_middle[0, 0], inverse_lower[0, 0]
@@ -508,35 +557,43 @@
     parts = over_leaf(multiply(multiply_lower_kernel, 192, own, swap_core(own), tile_lower, cost), 2)
     half = (leaf_count >> 1) * chip_count
     parts, lower[1] = lax.optimization_barrier((parts, lower[1]))
-    y_lower, own, far, keep, send = call(
-        lower_kernel, "lift_lower",
-        (array(128, 128), array(64, 128), array(64, 128), array(half, 64, 128), array(half, 64, 128)),
+    y_lower, own, far, kept["masks"], keep, send = call(
+        with_scalars(2, lower_kernel), "lift_lower",
+        (
+            array(128, 128), array(64, 128), array(64, 128),
+            array(chip_count + 1, 8, 128, dtype=F32), array(half, 64, 128), array(half, 64, 128),
+        ),
         [node_blocks, pattern_between], [parts, couple_between, leaf_near_between],
-        [pltpu.VMEM((2 * half, 64, 128), F32)],
+        [pltpu.VMEM((2 * half, 64, 128), F32), *scalar_scratch(node_blocks, pattern_between)],
+        smem_spec=ANY,
     )
     kept["y_lower"], kept["y_lower_own"], kept["far"], kept["lower"] = y_lower, own, far, lower[1]
     parts = updates(keep, send, 1)
+    rows = chip_count * 128
+    share = call(
+        rest_middle_kernel, "rest", array(rows + 64, 128), [], [parts, loads, kept.pop("far")]
+    )
+    share, middle[1] = lax.optimization_barrier((share, middle[1]))
+    near = swap_near(share)
+    kept["y_lower_near"] = near[rows:]
+    summed = (share[:rows].astype(F32) + near[:rows].astype(F32)).astype(BF16)
+    own = (summed.astype(F32) + swap_far(summed).astype(F32)).astype(BF16)
+    own = own.reshape(chip_count, 128, 128)
     kept["middle"] = middle[1]
-    rows = chip_count * 128 + 64
-    parts = over_chips(
-        call(
-            rest_middle_kernel, "rest", array(chip_count, rows, 128), [],
-            [parts, loads, kept.pop("far")],
-        )
-    )
-    own, kept["y_lower_near"] = call(
-        join_middle_kernel, "join", (array(chip_count, 128, 128), array(64, 128)), [], [parts]
-    )
     parts = over_pair(multiply(multiply_kernel, 128, own, swap_core(own), tile_middle), 1)
     lower[1], middle[1] = kept.pop("lower"), kept.pop("middle")
     near_between = swap_near(kept.pop("couples")[0])
     half = leaf_count * chip_count
     kept["y_middle"], keep, send = call(
-        pair_kernel, "lift_pair",
+        with_scalars(3, pair_kernel), "lift_pair",
         (array(2, 64, 128), array(half, 64, 128), array(half, 64, 128)),
         [node_blocks, pattern_middle, pattern_lower],
         [parts, kept["y_lower_own"], kept["y_lower_near"], *middle, *lower],
-        [pltpu.VMEM((2 * half, 64, 128), F32)], 16,
+        [
+            pltpu.VMEM((2 * half, 64, 128), F32),
+            *scalar_scratch(node_blocks, pattern_middle, pattern_lower),
+        ],
+        16, smem_spec=ANY,
     )
     parts = updates(keep, send, 0)
     kept["near_between"] = near_between
@@ -544,22 +601,31 @@
     parts = over_chips(call(rest_kernel, "rest", halves, [], [parts, kept.pop("load_root")]))
     own = call(join_kernel, "join", array(chip_count, 128, 128), [], [parts])
     near_tile = swap_near(kept.pop("tile"))
-    parts = over_leaf(multiply(multiply_kernel, 128, own, swap_core(own), tile_root), 0)
+    scratch = [pltpu.VMEM((chip_count * 128, 128), BF16)]
+    other = swap_core(own)
+    mine = call(
+        multiply_own_kernel, "multiply_own", array(leaf_count, 128, 128, dtype=F32), [],
+        [own, tile_root], scratch,
+    )
+    parts = call(
+        multiply_rest_kernel, "multiply_rest", array(leaf_count, 128, 128), [],
+        [other, mine, tile_root], scratch,
+    )
+    parts = over_leaf(parts, 0)
     kept["y_root"], copies = call(
         root_kernel, "root", (array(128, 128), array(leaf_count, 128, 128)), [], [parts]
     )
     partial_sums = backward(over_leaf(copies, 0), tile_root)
     kept["near_tile"] = near_tile
-    own, other = spread(partial_sums, 0)
+    own, other = spread_root(partial_sums)
     copies = reduced(
         1, True, pattern_middle, own, other, middle, kept["y_middle"], [], leaf_count >> 1
     )
-    kept["own_root"], kept["other_root"] = own, other
+    kept["own_root"], kept["other_root"], kept["lower"] = own, other, lower
     own, other = spread_middle(over_leaf(copies, 1), kept.pop("near_tile"))
-    pulled = pull(2, pattern_lower, kept.pop("own_root"), kept.pop("other_root"), lower)
     between = [couple_between, kept.pop("near_between")]
     solved = jnp.stack([kept.pop("y_lower_own"), kept.pop("y_lower_near")])
-    copies = reduced(2, False, pattern_between, own, other, between, solved, [pulled], leaf_count >> 2)
+    copies = reduced(2, False, pattern_between, own, other, between, solved, [kept.pop("pulled")], leaf_count >> 2)
     kept["far"] = swap_near(
         jnp.stack([kept.pop("near0"), kept.pop("near1"), kept["y_middle"][1]])
     )
@@ -571,8 +637,8 @@
     )
     parts = over_chips((mine + theirs.astype(F32)).astype(BF16))
     answer = call(
-        last_kernel, "last", array(3, 128, 128), [node_blocks],
-        [parts, kept["own0"], kept["own1"], kept["far"]],
+        last_kernel, "last", array(3, 128, 128), [],
+        [kept["masks"], parts, kept["own0"], kept["own1"], kept["far"]],
     )
     return (kept["forward"], answer)
 

time: 243 us -> 238 us (0.979)
  blocking collectives: 183 us -> 170 us
  waiting for transfers between devices: 20.8 us -> 29.7 us
  Pallas kernels: 20.3 us -> 17.5 us
    all_to_all x14 -> x13, blocking collectives: 183 us -> 170 us  [exchange(): lax.all_to_all(value, axis, 0, 0, tiled=True, axis_index_groups=groups)]
    ppermute x5 -> x6, waiting for transfers between devices: 0.33 us -> 5.42 us  [swap_near(): lax.ppermute(value, 'blk', [(i, near_of(i)) for i in range(block_count)])]
    ppermute x1 -> x2, waiting for transfers between devices: 4.96 us -> 7.84 us  [swap_far(): return lax.ppermute(value, 'blk', [(i, i ^ 4) for i in range(block_count)])]
    pallas_call x22, Pallas kernels: 20.3 us -> 17.5 us  [call(): pl.pallas_call(kernel, out_shape=out_shape, in_specs=[smem_spec] * len(sm...]
    ppermute x1 -> x2, starting transfers between devices: 0.89 us -> 3.59 us  [swap_far(): return lax.ppermute(value, 'blk', [(i, i ^ 4) for i in range(block_count)])]
  transfers between devices with their start and end apart: 18 -> 20, of which waited for: 12 -> 15; matrix products, arithmetic and copies ran while one was open for 0% -> 0% of each run, Pallas kernels for 4% -> 4%
where the time goes in v6:
time: 238 us; the launch traced here: 237 us
  blocking collectives  170 us (71%)
  waiting for transfers between devices  29.7 us (12%)
  Pallas kernels  17.5 us (7%)
  starting transfers between devices  16.1 us (7%)
    all_to_all x13, blocking collectives, exchange(): lax.all_to_all(value, axis, 0, 0, tiled=True, axis_index_groups=groups)  170 us
    pallas_call x22, Pallas kernels, call(): pl.pallas_call(kernel, out_shape=out_shape, in_specs=[smem_spec] * len(sm...  17.5 us
    ppermute x10, waiting for transfers between devices, swap_core(): return lax.ppermute(value, 'blk', [(i, i ^ 1) for i in range(block_count)])  13.4 us
    ppermute x2, waiting for transfers between devices, swap_far(): return lax.ppermute(value, 'blk', [(i, i ^ 4) for i in range(block_count)])  7.84 us
    ppermute x6, waiting for transfers between devices, swap_near(): lax.ppermute(value, 'blk', [(i, near_of(i)) for i in range(block_count)])  5.42 us
  transfers between devices with their start and end apart: 20, of which 15 were waited for; matrix products, arithmetic and copies ran while one was open for 0% of the time, Pallas kernels for 4%

profile of v6, /device:TPU:0, one launch (start us, length us, event | category | flops | bytes accessed | tf_op | source)
XLA Modules:
  0.0 237.4 jit_solution(10499281694702885030)
XLA Ops:
  2.3 4.4 %all-to-all-start = ((bf16[4,192,128]{2,1,0:T(8,128)(2,1)}), bf16[4,192,128]{2,1,0:T(8,128)(2,1)S(1)}, u32[]{:S(2)}, u32[]{:S(2)}) async-start(bf16[4,192,128]{2,1,0:T(8,128)(2,1)} %first.1), calls=%async_computation | async-start | bytes 393216 | tf_op jit(solution)/shard_map/all_to_all | solution.py:492
  6.7 2.0 collective-permute-start.1
  8.7 1.6 collective-permute-start.2
  10.3 3.0 %all-to-all-done = bf16[4,192,128]{2,1,0:T(8,128)(2,1)S(1)} async-done(((bf16[4,192,128]{2,1,0:T(8,128)(2,1)}), bf16[4,192,128]{2,1,0:T(8,128)(2,1)S(1)}, u32[]{:S(2)}, u32[]{:S(2)}) %all-to-all-start) | async-done | bytes 196640 | tf_op jit(solution)/shard_map/all_to_all | solution.py:492
  16.5 11.8 %all_to_all.70.refs_2_ = bf16[4,192,128]{2,1,0:T(8,128)(2,1)S(1)} all-to-all(bf16[4,192,128]{2,1,0:T(8,128)(2,1)S(1)} %multiply.2), channel_id=1, replica_groups={{0,8,16,24},{32,40,48,56},{64,72,80,88},{96,104,112,120},{1,9,17,25},{3..., dimensions={0} | all-to-all | bytes 393216 | tf_op jit(solution)/shard_map/all_to_all | solution.py:492
  28.3 1.4 lift_lower.1
  29.8 1.9 collective-permute-done.3
  31.9 13.6 %all_to_all.71.parts = bf16[8,4,64,128]{3,2,1,0:T(8,128)(2,1)S(1)} all-to-all(bf16[8,4,64,128]{3,2,1,0:T(8,128)(2,1)S(1)} %bitcast.40), channel_id=1, replica_groups={{0,8,16,24,32,40,48,56},{64,72,80,88,96,104,112,120},{1,9,17,25,33,41,4..., dimensions={0} | all-to-all | bytes 1048576 | tf_op jit(solution)/shard_map/all_to_all | solution.py:492
  46.2 4.7 %collective-permute-done.5 = bf16[576,128]{1,0:T(8,128)(2,1)S(1)} collective-permute-done((bf16[576,128]{1,0:T(8,128)(2,1)S(1)}, bf16[576,128]{1,0:T(8,128)(2,1)S(1)}, u32[]{:S(2)}, u32[]{:S(2)}) %collective-permute-start.5) | collective-permute-done | bytes 147488 | tf_op jit(solution)/shard_map/ppermute | solution.py:471
  51.0 2.7 %collective-permute-start.6 = (bf16[512,128]{1,0:T(8,128)(2,1)S(1)}, bf16[512,128]{1,0:T(8,128)(2,1)S(1)}, u32[]{:S(2)}, u32[]{:S(2)}) collective-permute-start(bf16[512,128]{1,0:T(8,128)(2,1)S(1)} %add_convert_fusion.4), channel_id=1, source_target_pairs={{0,4},{1,5},{2,6},{3,7},{4,0},{5,1},{6,2},{7,3},{8,12},{9,13},{10,... | collective-permute-start | bytes 393224 | tf_op jit(solution)/shard_map/ppermute | solution.py:474
  53.6 4.5 %collective-permute-done.6 = bf16[512,128]{1,0:T(8,128)(2,1)S(1)} collective-permute-done((bf16[512,128]{1,0:T(8,128)(2,1)S(1)}, bf16[512,128]{1,0:T(8,128)(2,1)S(1)}, u32[]{:S(2)}, u32[]{:S(2)}) %collective-permute-start.6) | collective-permute-done | bytes 131104 | tf_op jit(solution)/shard_map/ppermute | solution.py:474
  58.3 1.3 collective-permute-done.7.other
  60.4 13.2 %all_to_all.72 = bf16[16,64,128]{2,1,0:T(8,128)(2,1)S(1)} all-to-all(bf16[16,64,128]{2,1,0:T(8,128)(2,1)S(1)} %bitcast.27), channel_id=1, replica_groups={{0,2,8,10,16,18,24,26,32,34,40,42,48,50,56,58},{1,7,9,15,17,23,25,31,33..., dimensions={0} | all-to-all | bytes 524288 | tf_op jit(solution)/shard_map/all_to_all | solution.py:492
  73.6 2.8 %lift_pair.1 = (bf16[2,64,128]{2,1,0:T(8,128)(2,1)S(1)}, bf16[64,64,128]{2,1,0:T(8,128)(2,1)S(1)}, bf16[64,64,128]{2,1,0:T(8,128)(2,1)S(1)}) custom-call(s32[7]{0:T(128)S(1)} %copy-done.12, s32[2,64]{1,0:T(2,128)S(1)} %copy-done.11, s32[4,32]{1,0:T(4,128)S(1)} %copy-done.9, bf16[8,2,64,128]{3,2,1,0:T(8,128)(2,1)S(1)} %bitcast.30, ...), custom_call_target="tpu_custom_call" | custom-call | tf_op jit(solution)/shard_map/lift_pair/pallas_call | solution.py:51
  77.3 2.2 collective-permute-done.8
  80.0 23.9 %all_to_all.73.parts = bf16[16,4,64,128]{3,2,1,0:T(8,128)(2,1)S(1)} all-to-all(bf16[16,4,64,128]{3,2,1,0:T(8,128)(2,1)S(1)} %bitcast.39), channel_id=1, replica_groups=mesh['leaf'=16,'blk'=8] {'leaf'}, dimensions={0} | all-to-all | bytes 2097152 | tf_op jit(solution)/shard_map/all_to_all | solution.py:492
  104.1 9.8 %all_to_all.74.parts = bf16[4,4,64,128]{3,2,1,0:T(8,128)(2,1)S(1)} all-to-all(bf16[4,4,64,128]{3,2,1,0:T(8,128)(2,1)S(1)} %rest.3), channel_id=1, replica_groups={{0,2,4,6},{1,3,5,7},{8,10,12,14},{9,11,13,15},{16,18,20,22},{17,19,21,2..., dimensions={0} | all-to-all | bytes 524288 | tf_op jit(solution)/shard_map/all_to_all | solution.py:492
  116.8 14.8 %all_to_all.75.parts = bf16[16,128,128]{2,1,0:T(8,128)(2,1)S(1)} all-to-all(bf16[16,128,128]{2,1,0:T(8,128)(2,1)S(1)} %multiply_rest.1), channel_id=1, replica_groups=mesh['leaf'=16,'blk'=8] {'leaf'}, dimensions={0} | all-to-all | bytes 1048576 | tf_op jit(solution)/shard_map/all_to_all | solution.py:492
  131.7 14.0 %all_to_all.76.gathered = bf16[16,128,128]{2,1,0:T(8,128)(2,1)S(1)} all-to-all(bf16[16,128,128]{2,1,0:T(8,128)(2,1)S(1)} %get-tuple-element.359), channel_id=1, replica_groups=mesh['leaf'=16,'blk'=8] {'leaf'}, dimensions={0} | all-to-all | bytes 1048576 | tf_op jit(solution)/shard_map/all_to_all | solution.py:492
  146.5 1.3 collective-permute-done.11.theirs
  147.9 10.1 %all_to_all.77.parts = bf16[4,4,64,128]{3,2,1,0:T(8,128)(2,1)S(1)} all-to-all(bf16[4,4,64,128]{3,2,1,0:T(8,128)(2,1)S(1)} %split.1), channel_id=1, replica_groups={{0,2,4,6},{1,3,5,7},{8,10,12,14},{9,11,13,15},{16,18,20,22},{17,19,21,2..., dimensions={0} | all-to-all | bytes 524288 | tf_op jit(solution)/shard_map/all_to_all | solution.py:492
  158.2 19.2 %all_to_all.78 = bf16[16,4,64,128]{3,2,1,0:T(8,128)(2,1)S(1)} all-to-all(bf16[16,4,64,128]{3,2,1,0:T(8,128)(2,1)S(1)} %get-tuple-element.399), channel_id=1, replica_groups=mesh['leaf'=16,'blk'=8] {'leaf'}, dimensions={0} | all-to-all | bytes 2097152 | tf_op jit(solution)/shard_map/all_to_all | solution.py:492
  177.4 2.7 %collective-permute-done.13.other = bf16[64,64,128]{2,1,0:T(8,128)(2,1)S(1)} collective-permute-done((bf16[64,64,128]{2,1,0:T(8,128)(2,1)S(1)}, bf16[64,64,128]{2,1,0:T(8,128)(2,1)S(1)}, u32[]{:S(2)}, u32[]{:S(2)}) %collective-permute-start.13) | collective-permute-done | bytes 1048608 | tf_op jit(solution)/shard_map/ppermute | solution.py:468
  180.0 2.4 %reduced.2 = bf16[8,2,64,128]{3,2,1,0:T(8,128)(2,1)S(1)} custom-call(s32[2,64]{1,0:T(2,128)S(1)} %copy-done.11, bf16[64,64,128]{2,1,0:T(8,128)(2,1)S(1)} %bitcast.20, bf16[64,64,128]{2,1,0:T(8,128)(2,1)S(1)} %collective-permute-done.13.other, bf16[128,8192]{1,0:T(8,128)(2,1)S(1)} %copy-done.2, bf16[128,8192]{1,0:T(8,128)(2,1)S(1)} %collective-permute-done.4.refs_7_.near, ...), custom_call_target="tpu_custom_call" | custom-call | tf_op jit(solution)/shard_map/reduced/pallas_call | solution.py:51
  182.4 10.3 %all_to_all.79.gathered = bf16[8,2,64,128]{3,2,1,0:T(8,128)(2,1)S(1)} all-to-all(bf16[8,2,64,128]{3,2,1,0:T(8,128)(2,1)S(1)} %reduced.2), channel_id=1, replica_groups={{0,8,16,24,32,40,48,56},{64,72,80,88,96,104,112,120},{1,9,17,25,33,41,4..., dimensions={0} | all-to-all | bytes 524288 | tf_op jit(solution)/shard_map/all_to_all | solution.py:492
  195.8 1.6 pull.1.refs_0_
  197.4 3.4 %collective-permute-done.15.far = bf16[4,64,128]{2,1,0:T(8,128)(2,1)S(1)} collective-permute-done((bf16[4,64,128]{2,1,0:T(8,128)(2,1)S(1)}, bf16[4,64,128]{2,1,0:T(8,128)(2,1)S(1)}, u32[]{:S(2)}, u32[]{:S(2)}) %collective-permute-start.15) | collective-permute-done | bytes 65568 | tf_op jit(solution)/shard_map/ppermute | solution.py:474
  200.8 12.0 %all_to_all.80 = bf16[8,4,64,128]{3,2,1,0:T(8,128)(2,1)S(1)} all-to-all(bf16[8,4,64,128]{3,2,1,0:T(8,128)(2,1)S(1)} %get-tuple-element.456), channel_id=1, replica_groups={{0,8,16,24,32,40,48,56},{64,72,80,88,96,104,112,120},{1,9,17,25,33,41,4..., dimensions={0} | all-to-all | bytes 1048576 | tf_op jit(solution)/shard_map/all_to_all | solution.py:492
  213.4 1.2 collective-permute-done.16.other
  214.7 1.6 reduced.3
  216.9 9.1 %all_to_all.81 = bf16[8,64,128]{2,1,0:T(8,128)(2,1)S(1)} all-to-all(bf16[8,64,128]{2,1,0:T(8,128)(2,1)S(1)} %bitcast.33), channel_id=1, replica_groups={{0,2,8,10,16,18,24,26},{1,7,9,15,17,23,25,31},{4,6,12,14,20,22,28,30},{..., dimensions={0} | all-to-all | bytes 262144 | tf_op jit(solution)/shard_map/all_to_all | solution.py:492
  228.2 8.5 %all_to_all.82.parts = bf16[4,128,128]{2,1,0:T(8,128)(2,1)S(1)} all-to-all(bf16[4,128,128]{2,1,0:T(8,128)(2,1)S(1)} %add_convert_fusion.2), channel_id=1, replica_groups={{0,2,4,6},{1,3,5,7},{8,10,12,14},{9,11,13,15},{16,18,20,22},{17,19,21,2..., dimensions={0} | all-to-all | bytes 262144 | tf_op jit(solution)/shard_map/all_to_all | solution.py:492
  (81 shorter events, 19.5 us)
Async XLA Ops:
  2.3 11.0 %all-to-all-start = ((bf16[4,192,128]{2,1,0:T(8,128)(2,1)}), bf16[4,192,128]{2,1,0:T(8,128)(2,1)S(1)}, u32[]{:S(2)}, u32[]{:S(2)}) async-start(bf16[4,192,128]{2,1,0:T(8,128)(2,1)} %first.1), calls=%async_computation | async-start | bytes 393216 | tf_op jit(solution)/shard_map/all_to_all | solution.py:492
  6.7 21.6 %collective-permute-start.1 = (bf16[128,4096]{1,0:T(8,128)(2,1)}, bf16[128,4096]{1,0:T(8,128)(2,1)S(1)}, u32[]{:S(2)}, u32[]{:S(2)}) collective-permute-start(bf16[128,4096]{1,0:T(8,128)(2,1)} %factor.3), channel_id=1, source_target_pairs={{0,2},{1,7},{2,0},{3,5},{4,6},{5,3},{6,4},{7,1},{8,10},{9,15},{10,... | collective-permute-start | bytes 3145736 | tf_op jit(solution)/shard_map/ppermute | solution.py:471
  8.7 19.6 %collective-permute-start.2 = (bf16[128,4096]{1,0:T(8,128)(2,1)}, bf16[128,4096]{1,0:T(8,128)(2,1)S(1)}, u32[]{:S(2)}, u32[]{:S(2)}) collective-permute-start(bf16[128,4096]{1,0:T(8,128)(2,1)} %factor.4), channel_id=1, source_target_pairs={{0,8},{1,25},{2,10},{3,27},{4,12},{5,29},{6,14},{7,31},{8,0},{9,17... | collective-permute-start | bytes 3145736 | tf_op jit(solution)/shard_map/ppermute | solution.py:481
  13.3 1.4 collective-permute-start
  13.4 32.3 %collective-permute-start.4 = (bf16[128,8192]{1,0:T(8,128)(2,1)}, bf16[128,8192]{1,0:T(8,128)(2,1)S(1)}, u32[]{:S(2)}, u32[]{:S(2)}) collective-permute-start(bf16[128,8192]{1,0:T(8,128)(2,1)} %factor.2), channel_id=1, source_target_pairs={{0,2},{1,7},{2,0},{3,5},{4,6},{5,3},{6,4},{7,1},{8,10},{9,15},{10,... | collective-permute-start | bytes 6291464 | tf_op jit(solution)/shard_map/ppermute | solution.py:471
  14.8 1.2 copy-start.5
  16.0 12.3 %copy-start.3 = (bf16[128,4096]{1,0:T(8,128)(2,1)S(1)}, bf16[128,4096]{1,0:T(8,128)(2,1)}, u32[]{:S(2)}) copy-start(bf16[128,4096]{1,0:T(8,128)(2,1)} %factor.4) | copy-start | bytes 3145732
  16.0 12.3 %copy-start.10 = (s32[4,32]{1,0:T(4,128)S(1)}, s32[4,32]{1,0:T(4,128)}, u32[]{:S(2)}) copy-start(s32[4,32]{1,0:T(4,128)} %pattern.5) | copy-start | bytes 1540
  16.0 12.3 %copy-start.12 = (s32[7]{0:T(128)S(1)}, s32[7]{0:T(128)}, u32[]{:S(2)}) copy-start(s32[7]{0:T(128)} %refs_0_.3) | copy-start | bytes 88
  28.3 17.3 %copy-start.8 = (f32[3,128,128]{2,1,0:T(8,128)S(1)}, f32[3,128,128]{2,1,0:T(8,128)}, u32[]{:S(2)}) copy-start(f32[3,128,128]{2,1,0:T(8,128)} %loads.3) | copy-start | bytes 589828
  29.7 2.0 collective-permute-start.3
  31.7 27.9 %copy-start.1 = (bf16[1,1,1024,1024]{3,2,1,0:T(8,128)(2,1)S(1)}, bf16[1,1,1024,1024]{3,2,1,0:T(8,128)(2,1)}, u32[]{:S(2)}) copy-start(bf16[1,1,1024,1024]{3,2,1,0:T(8,128)(2,1)} %param.13) | copy-start | bytes 6291460
  45.6 28.0 %copy-start.2 = (bf16[128,8192]{1,0:T(8,128)(2,1)S(1)}, bf16[128,8192]{1,0:T(8,128)(2,1)}, u32[]{:S(2)}) copy-start(bf16[128,8192]{1,0:T(8,128)(2,1)} %factor.2) | copy-start | bytes 6291460
  45.6 28.0 %copy-start.4 = (bf16[128,4096]{1,0:T(8,128)(2,1)S(1)}, bf16[128,4096]{1,0:T(8,128)(2,1)}, u32[]{:S(2)}) copy-start(bf16[128,4096]{1,0:T(8,128)(2,1)} %factor.3) | copy-start | bytes 3145732
  45.7 28.0 %copy-start.9 = (s32[4,32]{1,0:T(4,128)S(1)}, s32[4,32]{1,0:T(4,128)}, u32[]{:S(2)}) copy-start(s32[4,32]{1,0:T(4,128)} %pattern.4) | copy-start | bytes 1540
  45.7 27.9 %copy-start.11 = (s32[2,64]{1,0:T(2,128)S(1)}, s32[2,64]{1,0:T(2,128)}, u32[]{:S(2)}) copy-start(s32[2,64]{1,0:T(2,128)} %pattern.3) | copy-start | bytes 1540
  45.7 5.2 %collective-permute-start.5 = (bf16[576,128]{1,0:T(8,128)(2,1)S(1)}, bf16[576,128]{1,0:T(8,128)(2,1)S(1)}, u32[]{:S(2)}, u32[]{:S(2)}) collective-permute-start(bf16[576,128]{1,0:T(8,128)(2,1)S(1)} %rest.2), channel_id=1, source_target_pairs={{0,2},{1,7},{2,0},{3,5},{4,6},{5,3},{6,4},{7,1},{8,10},{9,15},{10,... | collective-permute-start | bytes 442376 | tf_op jit(solution)/shard_map/ppermute | solution.py:471
  51.0 7.2 %collective-permute-start.6 = (bf16[512,128]{1,0:T(8,128)(2,1)S(1)}, bf16[512,128]{1,0:T(8,128)(2,1)S(1)}, u32[]{:S(2)}, u32[]{:S(2)}) collective-permute-start(bf16[512,128]{1,0:T(8,128)(2,1)S(1)} %add_convert_fusion.4), channel_id=1, source_target_pairs={{0,4},{1,5},{2,6},{3,7},{4,0},{5,1},{6,2},{7,3},{8,12},{9,13},{10,... | collective-permute-start | bytes 393224 | tf_op jit(solution)/shard_map/ppermute | solution.py:474
  58.1 1.4 collective-permute-start.7
  76.4 3.1 %collective-permute-start.8 = (bf16[64,64,128]{2,1,0:T(8,128)(2,1)S(1)}, bf16[64,64,128]{2,1,0:T(8,128)(2,1)S(1)}, u32[]{:S(2)}, u32[]{:S(2)}) collective-permute-start(bf16[64,64,128]{2,1,0:T(8,128)(2,1)S(1)} %get-tuple-element.308), channel_id=1, source_target_pairs={{0,1},{1,0},{2,3},{3,2},{4,5},{5,4},{6,7},{7,6},{8,9},{9,8},{10,11... | collective-permute-start | bytes 3145736 | tf_op jit(solution)/shard_map/ppermute | solution.py:468
  77.3 26.8 %collective-permute-start.9 = (bf16[128,4096]{1,0:T(8,128)(2,1)S(1)}, bf16[128,4096]{1,0:T(8,128)(2,1)S(1)}, u32[]{:S(2)}, u32[]{:S(2)}) collective-permute-start(bf16[128,4096]{1,0:T(8,128)(2,1)S(1)} %copy-done.3), channel_id=1, source_target_pairs={{0,2},{1,7},{2,0},{3,5},{4,6},{5,3},{6,4},{7,1},{8,10},{9,15},{10,... | collective-permute-start | bytes 3145736 | tf_op jit(solution)/shard_map/ppermute | solution.py:471
  80.0 34.6 %copy-start = (bf16[1,1,2048,1024]{3,2,1,0:T(8,128)(2,1)S(1)}, bf16[1,1,2048,1024]{3,2,1,0:T(8,128)(2,1)}, u32[]{:S(2)}) copy-start(bf16[1,1,2048,1024]{3,2,1,0:T(8,128)(2,1)} %param.12) | copy-start | bytes 12582916
  113.9 34.0 %collective-permute-start.12 = (bf16[1024,1024]{1,0:T(8,128)(2,1)S(1)}, bf16[1024,1024]{1,0:T(8,128)(2,1)S(1)}, u32[]{:S(2)}, u32[]{:S(2)}) collective-permute-start(bf16[1024,1024]{1,0:T(8,128)(2,1)S(1)} %bitcast.23), channel_id=1, source_target_pairs={{0,2},{1,7},{2,0},{3,5},{4,6},{5,3},{6,4},{7,1},{8,10},{9,15},{10,... | collective-permute-start | bytes 6291464 | tf_op jit(solution)/shard_map/ppermute | solution.py:471
  114.5 1.4 collective-permute-start.10
  146.4 1.4 collective-permute-start.11
  177.4 2.7 %collective-permute-start.13 = (bf16[64,64,128]{2,1,0:T(8,128)(2,1)S(1)}, bf16[64,64,128]{2,1,0:T(8,128)(2,1)S(1)}, u32[]{:S(2)}, u32[]{:S(2)}) collective-permute-start(bf16[64,64,128]{2,1,0:T(8,128)(2,1)S(1)} %bitcast.19), channel_id=1, source_target_pairs={{0,1},{1,0},{2,3},{3,2},{4,5},{5,4},{6,7},{7,6},{8,9},{9,8},{10,11... | collective-permute-start | bytes 3145736 | tf_op jit(solution)/shard_map/ppermute | solution.py:468
  193.5 1.3 collective-permute-start.14
  194.9 5.8 %collective-permute-start.15 = (bf16[4,64,128]{2,1,0:T(8,128)(2,1)S(1)}, bf16[4,64,128]{2,1,0:T(8,128)(2,1)S(1)}, u32[]{:S(2)}, u32[]{:S(2)}) collective-permute-start(bf16[4,64,128]{2,1,0:T(8,128)(2,1)S(1)} %add_convert_fusion.5.mine), channel_id=1, source_target_pairs={{0,4},{1,5},{2,6},{3,7},{4,0},{5,1},{6,2},{7,3},{8,12},{9,13},{10,... | collective-permute-start | bytes 196616 | tf_op jit(solution)/shard_map/ppermute | solution.py:474
  212.7 13.3 %copy-start.6 = (bf16[1,1,512,1024]{3,2,1,0:T(8,128)(2,1)S(1)}, bf16[1,1,512,1024]{3,2,1,0:T(8,128)(2,1)}, u32[]{:S(2)}) copy-start(bf16[1,1,512,1024]{3,2,1,0:T(8,128)(2,1)} %param.14) | copy-start | bytes 3145732
  212.7 1.9 collective-permute-start.16
  212.8 4.2 %collective-permute-start.17 = (bf16[3,64,128]{2,1,0:T(8,128)(2,1)S(1)}, bf16[3,64,128]{2,1,0:T(8,128)(2,1)S(1)}, u32[]{:S(2)}, u32[]{:S(2)}) collective-permute-start(bf16[3,64,128]{2,1,0:T(8,128)(2,1)S(1)} %pad_maximum_fusion), channel_id=1, source_target_pairs={{0,2},{1,7},{2,0},{3,5},{4,6},{5,3},{6,4},{7,1},{8,10},{9,15},{10,... | collective-permute-start | bytes 147464 | tf_op jit(solution)/shard_map/ppermute | solution.py:471
  226.3 1.8 collective-permute-start.18
  (1 other events, 0.9 us)

commit v7 on v6

--- a/solution.py
+++ b/solution.py
@@ -71,14 +71,6 @@
     return total
 
 
-def first_kernel(loads, out):
-    lower, root = loads[2].astype(BF16), loads[0].astype(BF16).T
-    for chip in range(out.shape[0]):
-        side = (chip & 1) * 64
-        out[chip, :128, :] = lower
-        out[chip, 128:192, :] = root[side : side + 64]
-
-
 def gather_columns(transposed, own, other, columns):
     first = core_of() == 0
     for chip in range(own.shape[0]):
@@ -92,12 +84,6 @@
 def partial_of(tile, columns, group):
     rows = tile[group * 128 : group * 128 + 128, :]
     return jnp.dot(rows, columns[...], preferred_element_type=F32).astype(BF16).T
-
-
-def multiply_kernel(own, other, tile, out, columns):
-    gather_columns(True, own, other, columns)
-    for group in range(out.shape[0]):
-        out[group] = partial_of(tile, columns, group)
 
 
 def columns_of(blocks, core, tile, group):
@@ -221,14 +207,14 @@
                 sums[slot] += product[:, part * 128 : part * 128 + 128]
             return carry
 
-        lax.fori_loop(0, span // 1024, chunk, 0, unroll=2)
+        lax.fori_loop(0, span // 1024, chunk, 0, unroll=4)
 
     def emit(slot, carry):
         keep[slot] = sums[slot].astype(BF16)
         send[slot] = sums[half + slot].astype(BF16)
         return carry
 
-    lax.fori_loop(0, half, emit, 0, unroll=4)
+    lax.fori_loop(0, half, emit, 0, unroll=8)
 
 
 def lower_kernel(
@@ -275,17 +261,18 @@
     )
 
 
-def rest_kernel(parts, load, copies):
+def rest_kernel(parts, load, load_near, copies):
     chip, near = lax.axis_index("blk") >> 1, near_of(lax.axis_index("blk")) >> 1
     for place in range(parts.shape[1]):
         total = total_of([parts[g, place] for g in range(parts.shape[0])])
-        given = (chip == place) | (near == place)
-        value = (jnp.where(given, load[place].astype(F32), 0.0) - total).astype(BF16)
+        given = jnp.where(chip == place, load[...], load_near[...]).astype(F32)
+        value = jnp.where((chip == place) | (near == place), given, 0.0) - total
+        value = value.astype(BF16)
         for index in range(copies.shape[0]):
             copies[index, place] = value
 
 
-def rest_middle_kernel(parts, loads, far, out):
+def rest_middle_kernel(parts, loads, far, out, load_own):
     chip = lax.axis_index("blk") >> 1
     load = loads[1].T
     for place in range(parts.shape[1]):
@@ -293,7 +280,10 @@
         total = jnp.concatenate(total, axis=0)
         value = (jnp.where(chip == place, load, 0.0) - total).astype(BF16)
         out[place * 128 : place * 128 + 128, :] = value
-    out[parts.shape[1] * 128 :, :] = far[...]
+    last, root, first = parts.shape[1] * 128, loads[0].astype(BF16).T, side_of() == 0
+    out[last : last + 64, :] = far[...]
+    out[last + 64 :, :] = jnp.where(first, root[64:], root[:64])
+    load_own[...] = jnp.where(first, root[:64], root[64:])
 
 
 def join_kernel(parts, out):
@@ -364,7 +354,7 @@
         chosen[:, pl.ds(column, 128)] = jnp.where(mine, own[block >> 1], other[block >> 1])
         return carry
 
-    lax.fori_loop(0, pattern.shape[1], pick, 0, unroll=4)
+    lax.fori_loop(0, pattern.shape[1], pick, 0, unroll=16)
     product = jnp.zeros((256, 64), F32)
     for start in range(0, chosen.shape[1], 1024):
         columns = slice(start, start + 1024)
@@ -472,6 +462,18 @@
 
     def swap_far(value):
         return lax.ppermute(value, "blk", [(i, i ^ 4) for i in range(block_count)])
+
+    def forward_solve(own, tile):
+        count, scratch = tile.shape[0] // 128, [pltpu.VMEM((chip_count * 128, 128), BF16)]
+        other = swap_core(own)
+        mine = call(
+            multiply_own_kernel, "multiply_own", array(count, 128, 128, dtype=F32), [],
+            [own, tile], scratch,
+        )
+        return call(
+            multiply_rest_kernel, "multiply_rest", array(count, 128, 128), [],
+            [other, mine, tile], scratch,
+        )
 
     def swap_leaf_near(value):
         pairs = []
@@ -548,12 +550,11 @@
     leaf_near_between = swap_leaf_near(couple_between)
     kept["couples"] = [couple_between, couple_lower, couple_middle]
 
-    loaded = over_chips(call(first_kernel, "first", array(chip_count, 192, 128), [], [loads]))
+    load_lower = jnp.broadcast_to(loads[2].astype(BF16)[None], (chip_count, 128, 128))
+    own = over_chips(load_lower)
     cost = pl.CostEstimate(flops=int(7.5e9), bytes_accessed=0, transcendentals=0)
     lower = [couple_lower, swap_near(couple_lower)]
     middle = [couple_middle, swap_near(couple_middle)]
-    own = loaded[:, :128]
-    kept["load_root"] = loaded[:, 128:]
     parts = over_leaf(multiply(multiply_lower_kernel, 192, own, swap_core(own), tile_lower, cost), 2)
     half = (leaf_count >> 1) * chip_count
     parts, lower[1] = lax.optimization_barrier((parts, lower[1]))
@@ -570,17 +571,18 @@
     kept["y_lower"], kept["y_lower_own"], kept["far"], kept["lower"] = y_lower, own, far, lower[1]
     parts = updates(keep, send, 1)
     rows = chip_count * 128
-    share = call(
-        rest_middle_kernel, "rest", array(rows + 64, 128), [], [parts, loads, kept.pop("far")]
+    share, kept["load_own"] = call(
+        rest_middle_kernel, "rest", (array(rows + 128, 128), array(64, 128)), [],
+        [parts, loads, kept.pop("far")],
     )
     share, middle[1] = lax.optimization_barrier((share, middle[1]))
     near = swap_near(share)
-    kept["y_lower_near"] = near[rows:]
+    kept["y_lower_near"], kept["load_near"] = near[rows : rows + 64], near[rows + 64 :]
     summed = (share[:rows].astype(F32) + near[:rows].astype(F32)).astype(BF16)
     own = (summed.astype(F32) + swap_far(summed).astype(F32)).astype(BF16)
     own = own.reshape(chip_count, 128, 128)
     kept["middle"] = middle[1]
-    parts = over_pair(multiply(multiply_kernel, 128, own, swap_core(own), tile_middle), 1)
+    parts = over_pair(forward_solve(own, tile_middle), 1)
     lower[1], middle[1] = kept.pop("lower"), kept.pop("middle")
     near_between = swap_near(kept.pop("couples")[0])
     half = leaf_count * chip_count
@@ -598,19 +600,10 @@
     parts = updates(keep, send, 0)
     kept["near_between"] = near_between
     kept["tile"] = tile_middle
-    parts = over_chips(call(rest_kernel, "rest", halves, [], [parts, kept.pop("load_root")]))
+    parts = over_chips(call(rest_kernel, "rest", halves, [], [parts, kept.pop("load_own"), kept.pop("load_near")]))
     own = call(join_kernel, "join", array(chip_count, 128, 128), [], [parts])
     near_tile = swap_near(kept.pop("tile"))
-    scratch = [pltpu.VMEM((chip_count * 128, 128), BF16)]
-    other = swap_core(own)
-    mine = call(
-        multiply_own_kernel, "multiply_own", array(leaf_count, 128, 128, dtype=F32), [],
-        [own, tile_root], scratch,
-    )
-    parts = call(
-        multiply_rest_kernel, "multiply_rest", array(leaf_count, 128, 128), [],
-        [other, mine, tile_root], scratch,
-    )
+    parts = forward_solve(own, tile_root)
     parts = over_leaf(parts, 0)
     kept["y_root"], copies = call(
         root_kernel, "root", (array(128, 128), array(leaf_count, 128, 128)), [], [parts]

time: 238 us -> 237 us (level)
  no operation moved by 1% of the time
where the time goes in v7:
time: 237 us
  blocking collectives  171 us (72%)
  waiting for transfers between devices  28.3 us (12%)
  Pallas kernels  16.6 us (7%)
  starting transfers between devices  16.5 us (7%)
  local copies, waits for them, and re-layouts  2.79 us (1%)
    all_to_all x13, blocking collectives, exchange(): lax.all_to_all(value, axis, 0, 0, tiled=True, axis_index_groups=groups)  171 us
    pallas_call x22, Pallas kernels, call(): pl.pallas_call(kernel, out_shape=out_shape, in_specs=[smem_spec] * len(sm...  16.6 us
    ppermute x10, waiting for transfers between devices, swap_core(): return lax.ppermute(value, 'blk', [(i, i ^ 1) for i in range(block_count)])  12.8 us
    ppermute x2, waiting for transfers between devices, swap_far(): return lax.ppermute(value, 'blk', [(i, i ^ 4) for i in range(block_count)])  7.61 us
    ppermute x6, waiting for transfers between devices, swap_near(): lax.ppermute(value, 'blk', [(i, near_of(i)) for i in range(block_count)])  5.36 us
  transfers between devices with their start and end apart: 20, of which 15 were waited for; matrix products, arithmetic and copies ran while one was open for 0% of the time, Pallas kernels for 4%

profile of v7, /device:TPU:0, one launch (start us, length us, event | category | flops | bytes accessed | tf_op | source)
XLA Modules:
  0.0 236.7 jit_solution(15838127791222641578)
XLA Ops:
  2.1 4.4 %all-to-all-start = ((bf16[4,128,128]{2,1,0:T(8,128)(2,1)}), bf16[4,128,128]{2,1,0:T(8,128)(2,1)S(1)}, u32[]{:S(2)}, u32[]{:S(2)}) async-start(bf16[4,128,128]{2,1,0:T(8,128)(2,1)} %broadcast_in_dim.9), calls=%async_computation | async-start | bytes 262144 | tf_op jit(solution)/shard_map/all_to_all | solution.py:494
  6.5 2.0 collective-permute-start.1
  8.5 1.6 collective-permute-start.2
  10.1 2.5 %all-to-all-done.own = bf16[4,128,128]{2,1,0:T(8,128)(2,1)S(1)} async-done(((bf16[4,128,128]{2,1,0:T(8,128)(2,1)}), bf16[4,128,128]{2,1,0:T(8,128)(2,1)S(1)}, u32[]{:S(2)}, u32[]{:S(2)}) %all-to-all-start) | async-done | bytes 131104 | tf_op jit(solution)/shard_map/all_to_all | solution.py:494
  13.9 1.2 copy-done.5
  15.7 12.4 %all_to_all.70.refs_2_ = bf16[4,192,128]{2,1,0:T(8,128)(2,1)S(1)} all-to-all(bf16[4,192,128]{2,1,0:T(8,128)(2,1)S(1)} %multiply.1), channel_id=1, replica_groups={{0,8,16,24},{32,40,48,56},{64,72,80,88},{96,104,112,120},{1,9,17,25},{3..., dimensions={0} | all-to-all | bytes 393216 | tf_op jit(solution)/shard_map/all_to_all | solution.py:494
  29.5 1.9 collective-permute-done.3
  31.5 13.6 %all_to_all.71.parts = bf16[8,4,64,128]{3,2,1,0:T(8,128)(2,1)S(1)} all-to-all(bf16[8,4,64,128]{3,2,1,0:T(8,128)(2,1)S(1)} %bitcast.43), channel_id=1, replica_groups={{0,8,16,24,32,40,48,56},{64,72,80,88,96,104,112,120},{1,9,17,25,33,41,4..., dimensions={0} | all-to-all | bytes 1048576 | tf_op jit(solution)/shard_map/all_to_all | solution.py:494
  46.0 4.7 %collective-permute-done.5 = bf16[640,128]{1,0:T(8,128)(2,1)S(1)} collective-permute-done((bf16[640,128]{1,0:T(8,128)(2,1)S(1)}, bf16[640,128]{1,0:T(8,128)(2,1)S(1)}, u32[]{:S(2)}, u32[]{:S(2)}) %collective-permute-start.5) | collective-permute-done | bytes 163872 | tf_op jit(solution)/shard_map/ppermute | solution.py:461
  50.7 2.7 %collective-permute-start.6 = (bf16[512,128]{1,0:T(8,128)(2,1)S(1)}, bf16[512,128]{1,0:T(8,128)(2,1)S(1)}, u32[]{:S(2)}, u32[]{:S(2)}) collective-permute-start(bf16[512,128]{1,0:T(8,128)(2,1)S(1)} %add_convert_fusion.4), channel_id=1, source_target_pairs={{0,4},{1,5},{2,6},{3,7},{4,0},{5,1},{6,2},{7,3},{8,12},{9,13},{10,... | collective-permute-start | bytes 393224 | tf_op jit(solution)/shard_map/ppermute | solution.py:464
  53.4 4.3 %collective-permute-done.6 = bf16[512,128]{1,0:T(8,128)(2,1)S(1)} collective-permute-done((bf16[512,128]{1,0:T(8,128)(2,1)S(1)}, bf16[512,128]{1,0:T(8,128)(2,1)S(1)}, u32[]{:S(2)}, u32[]{:S(2)}) %collective-permute-start.6) | collective-permute-done | bytes 131104 | tf_op jit(solution)/shard_map/ppermute | solution.py:464
  59.8 13.0 %all_to_all.72 = bf16[16,64,128]{2,1,0:T(8,128)(2,1)S(1)} all-to-all(bf16[16,64,128]{2,1,0:T(8,128)(2,1)S(1)} %bitcast.30), channel_id=1, replica_groups={{0,2,8,10,16,18,24,26,32,34,40,42,48,50,56,58},{1,7,9,15,17,23,25,31,33..., dimensions={0} | all-to-all | bytes 524288 | tf_op jit(solution)/shard_map/all_to_all | solution.py:494
  72.8 2.4 %lift_pair.1 = (bf16[2,64,128]{2,1,0:T(8,128)(2,1)S(1)}, bf16[64,64,128]{2,1,0:T(8,128)(2,1)S(1)}, bf16[64,64,128]{2,1,0:T(8,128)(2,1)S(1)}) custom-call(s32[7]{0:T(128)S(1)} %copy-done.11, s32[2,64]{1,0:T(2,128)S(1)} %copy-done.10, s32[4,32]{1,0:T(4,128)S(1)} %copy-done.8, bf16[8,2,64,128]{3,2,1,0:T(8,128)(2,1)S(1)} %bitcast.33, ...), custom_call_target="tpu_custom_call" | custom-call | tf_op jit(solution)/shard_map/lift_pair/pallas_call | solution.py:51
  76.4 2.2 collective-permute-done.8
  79.0 24.1 %all_to_all.73.parts = bf16[16,4,64,128]{3,2,1,0:T(8,128)(2,1)S(1)} all-to-all(bf16[16,4,64,128]{3,2,1,0:T(8,128)(2,1)S(1)} %bitcast.42), channel_id=1, replica_groups=mesh['leaf'=16,'blk'=8] {'leaf'}, dimensions={0} | all-to-all | bytes 2097152 | tf_op jit(solution)/shard_map/all_to_all | solution.py:494
  103.3 9.8 %all_to_all.74.parts = bf16[4,4,64,128]{3,2,1,0:T(8,128)(2,1)S(1)} all-to-all(bf16[4,4,64,128]{3,2,1,0:T(8,128)(2,1)S(1)} %rest.3), channel_id=1, replica_groups={{0,2,4,6},{1,3,5,7},{8,10,12,14},{9,11,13,15},{16,18,20,22},{17,19,21,2..., dimensions={0} | all-to-all | bytes 524288 | tf_op jit(solution)/shard_map/all_to_all | solution.py:494
  116.0 14.8 %all_to_all.75.parts = bf16[16,128,128]{2,1,0:T(8,128)(2,1)S(1)} all-to-all(bf16[16,128,128]{2,1,0:T(8,128)(2,1)S(1)} %multiply_rest.3), channel_id=1, replica_groups=mesh['leaf'=16,'blk'=8] {'leaf'}, dimensions={0} | all-to-all | bytes 1048576 | tf_op jit(solution)/shard_map/all_to_all | solution.py:494
  130.9 14.0 %all_to_all.76.gathered = bf16[16,128,128]{2,1,0:T(8,128)(2,1)S(1)} all-to-all(bf16[16,128,128]{2,1,0:T(8,128)(2,1)S(1)} %get-tuple-element.363), channel_id=1, replica_groups=mesh['leaf'=16,'blk'=8] {'leaf'}, dimensions={0} | all-to-all | bytes 1048576 | tf_op jit(solution)/shard_map/all_to_all | solution.py:494
  145.7 1.3 collective-permute-done.11.theirs
  147.1 10.1 %all_to_all.77.parts = bf16[4,4,64,128]{3,2,1,0:T(8,128)(2,1)S(1)} all-to-all(bf16[4,4,64,128]{3,2,1,0:T(8,128)(2,1)S(1)} %split.1), channel_id=1, replica_groups={{0,2,4,6},{1,3,5,7},{8,10,12,14},{9,11,13,15},{16,18,20,22},{17,19,21,2..., dimensions={0} | all-to-all | bytes 524288 | tf_op jit(solution)/shard_map/all_to_all | solution.py:494
  157.4 19.2 %all_to_all.78 = bf16[16,4,64,128]{3,2,1,0:T(8,128)(2,1)S(1)} all-to-all(bf16[16,4,64,128]{3,2,1,0:T(8,128)(2,1)S(1)} %get-tuple-element.403), channel_id=1, replica_groups=mesh['leaf'=16,'blk'=8] {'leaf'}, dimensions={0} | all-to-all | bytes 2097152 | tf_op jit(solution)/shard_map/all_to_all | solution.py:494
  176.6 2.7 %collective-permute-done.13.other = bf16[64,64,128]{2,1,0:T(8,128)(2,1)S(1)} collective-permute-done((bf16[64,64,128]{2,1,0:T(8,128)(2,1)S(1)}, bf16[64,64,128]{2,1,0:T(8,128)(2,1)S(1)}, u32[]{:S(2)}, u32[]{:S(2)}) %collective-permute-start.13) | collective-permute-done | bytes 1048608 | tf_op jit(solution)/shard_map/ppermute | solution.py:458
  179.2 2.4 %reduced.2 = bf16[8,2,64,128]{3,2,1,0:T(8,128)(2,1)S(1)} custom-call(s32[2,64]{1,0:T(2,128)S(1)} %copy-done.10, bf16[64,64,128]{2,1,0:T(8,128)(2,1)S(1)} %bitcast.26, bf16[64,64,128]{2,1,0:T(8,128)(2,1)S(1)} %collective-permute-done.13.other, bf16[128,8192]{1,0:T(8,128)(2,1)S(1)} %copy-done.2, bf16[128,8192]{1,0:T(8,128)(2,1)S(1)} %collective-permute-done.4.refs_7_.near, ...), custom_call_target="tpu_custom_call" | custom-call | tf_op jit(solution)/shard_map/reduced/pallas_call | solution.py:51
  181.7 10.3 %all_to_all.79.gathered = bf16[8,2,64,128]{3,2,1,0:T(8,128)(2,1)S(1)} all-to-all(bf16[8,2,64,128]{3,2,1,0:T(8,128)(2,1)S(1)} %reduced.2), channel_id=1, replica_groups={{0,8,16,24,32,40,48,56},{64,72,80,88,96,104,112,120},{1,9,17,25,33,41,4..., dimensions={0} | all-to-all | bytes 524288 | tf_op jit(solution)/shard_map/all_to_all | solution.py:494
  192.9 1.2 collective-permute-done.14
  195.0 1.6 pull.1.refs_0_
  196.7 3.3 %collective-permute-done.15.far = bf16[4,64,128]{2,1,0:T(8,128)(2,1)S(1)} collective-permute-done((bf16[4,64,128]{2,1,0:T(8,128)(2,1)S(1)}, bf16[4,64,128]{2,1,0:T(8,128)(2,1)S(1)}, u32[]{:S(2)}, u32[]{:S(2)}) %collective-permute-start.15) | collective-permute-done | bytes 65568 | tf_op jit(solution)/shard_map/ppermute | solution.py:464
  200.1 12.0 %all_to_all.80 = bf16[8,4,64,128]{3,2,1,0:T(8,128)(2,1)S(1)} all-to-all(bf16[8,4,64,128]{3,2,1,0:T(8,128)(2,1)S(1)} %get-tuple-element.460), channel_id=1, replica_groups={{0,8,16,24,32,40,48,56},{64,72,80,88,96,104,112,120},{1,9,17,25,33,41,4..., dimensions={0} | all-to-all | bytes 1048576 | tf_op jit(solution)/shard_map/all_to_all | solution.py:494
  212.7 1.2 collective-permute-done.16.other
  213.9 1.6 reduced.3
  216.2 9.1 %all_to_all.81 = bf16[8,64,128]{2,1,0:T(8,128)(2,1)S(1)} all-to-all(bf16[8,64,128]{2,1,0:T(8,128)(2,1)S(1)} %bitcast.34), channel_id=1, replica_groups={{0,2,8,10,16,18,24,26},{1,7,9,15,17,23,25,31},{4,6,12,14,20,22,28,30},{..., dimensions={0} | all-to-all | bytes 262144 | tf_op jit(solution)/shard_map/all_to_all | solution.py:494
  227.4 8.5 %all_to_all.82.parts = bf16[4,128,128]{2,1,0:T(8,128)(2,1)S(1)} all-to-all(bf16[4,128,128]{2,1,0:T(8,128)(2,1)S(1)} %add_convert_fusion.2), channel_id=1, replica_groups={{0,2,4,6},{1,3,5,7},{8,10,12,14},{9,11,13,15},{16,18,20,22},{17,19,21,2..., dimensions={0} | all-to-all | bytes 262144 | tf_op jit(solution)/shard_map/all_to_all | solution.py:494
  (79 shorter events, 19.6 us)
Async XLA Ops:
  2.1 10.5 %all-to-all-start = ((bf16[4,128,128]{2,1,0:T(8,128)(2,1)}), bf16[4,128,128]{2,1,0:T(8,128)(2,1)S(1)}, u32[]{:S(2)}, u32[]{:S(2)}) async-start(bf16[4,128,128]{2,1,0:T(8,128)(2,1)} %broadcast_in_dim.9), calls=%async_computation | async-start | bytes 262144 | tf_op jit(solution)/shard_map/all_to_all | solution.py:494
  6.5 21.6 %collective-permute-start.1 = (bf16[128,4096]{1,0:T(8,128)(2,1)}, bf16[128,4096]{1,0:T(8,128)(2,1)S(1)}, u32[]{:S(2)}, u32[]{:S(2)}) collective-permute-start(bf16[128,4096]{1,0:T(8,128)(2,1)} %factor.3), channel_id=1, source_target_pairs={{0,2},{1,7},{2,0},{3,5},{4,6},{5,3},{6,4},{7,1},{8,10},{9,15},{10,... | collective-permute-start | bytes 3145736 | tf_op jit(solution)/shard_map/ppermute | solution.py:461
  8.5 19.6 %collective-permute-start.2 = (bf16[128,4096]{1,0:T(8,128)(2,1)}, bf16[128,4096]{1,0:T(8,128)(2,1)S(1)}, u32[]{:S(2)}, u32[]{:S(2)}) collective-permute-start(bf16[128,4096]{1,0:T(8,128)(2,1)} %factor.4), channel_id=1, source_target_pairs={{0,8},{1,25},{2,10},{3,27},{4,12},{5,29},{6,14},{7,31},{8,0},{9,17... | collective-permute-start | bytes 3145736 | tf_op jit(solution)/shard_map/ppermute | solution.py:483
  12.6 1.3 collective-permute-start
  12.6 32.7 %collective-permute-start.4 = (bf16[128,8192]{1,0:T(8,128)(2,1)}, bf16[128,8192]{1,0:T(8,128)(2,1)S(1)}, u32[]{:S(2)}, u32[]{:S(2)}) collective-permute-start(bf16[128,8192]{1,0:T(8,128)(2,1)} %factor.2), channel_id=1, source_target_pairs={{0,2},{1,7},{2,0},{3,5},{4,6},{5,3},{6,4},{7,1},{8,10},{9,15},{10,... | collective-permute-start | bytes 6291464 | tf_op jit(solution)/shard_map/ppermute | solution.py:461
  13.9 1.2 copy-start.5
  15.2 12.9 %copy-start.3 = (bf16[128,4096]{1,0:T(8,128)(2,1)S(1)}, bf16[128,4096]{1,0:T(8,128)(2,1)}, u32[]{:S(2)}) copy-start(bf16[128,4096]{1,0:T(8,128)(2,1)} %factor.4) | copy-start | bytes 3145732
  15.2 13.0 %copy-start.9 = (s32[4,32]{1,0:T(4,128)S(1)}, s32[4,32]{1,0:T(4,128)}, u32[]{:S(2)}) copy-start(s32[4,32]{1,0:T(4,128)} %pattern.5) | copy-start | bytes 1540
  15.2 13.0 %copy-start.11 = (s32[7]{0:T(128)S(1)}, s32[7]{0:T(128)}, u32[]{:S(2)}) copy-start(s32[7]{0:T(128)} %refs_0_.3) | copy-start | bytes 88
  28.1 17.1 %copy-start.7 = (f32[3,128,128]{2,1,0:T(8,128)S(1)}, f32[3,128,128]{2,1,0:T(8,128)}, u32[]{:S(2)}) copy-start(f32[3,128,128]{2,1,0:T(8,128)} %loads.1) | copy-start | bytes 589828
  29.4 2.0 collective-permute-start.3
  31.4 26.5 %copy-start.1 = (bf16[1,1,1024,1024]{3,2,1,0:T(8,128)(2,1)S(1)}, bf16[1,1,1024,1024]{3,2,1,0:T(8,128)(2,1)}, u32[]{:S(2)}) copy-start(bf16[1,1,1024,1024]{3,2,1,0:T(8,128)(2,1)} %param.13) | copy-start | bytes 6291460
  45.3 5.4 %collective-permute-start.5 = (bf16[640,128]{1,0:T(8,128)(2,1)S(1)}, bf16[640,128]{1,0:T(8,128)(2,1)S(1)}, u32[]{:S(2)}, u32[]{:S(2)}) collective-permute-start(bf16[640,128]{1,0:T(8,128)(2,1)S(1)} %get-tuple-element.285), channel_id=1, source_target_pairs={{0,2},{1,7},{2,0},{3,5},{4,6},{5,3},{6,4},{7,1},{8,10},{9,15},{10,... | collective-permute-start | bytes 491528 | tf_op jit(solution)/shard_map/ppermute | solution.py:461
  50.7 7.0 %collective-permute-start.6 = (bf16[512,128]{1,0:T(8,128)(2,1)S(1)}, bf16[512,128]{1,0:T(8,128)(2,1)S(1)}, u32[]{:S(2)}, u32[]{:S(2)}) collective-permute-start(bf16[512,128]{1,0:T(8,128)(2,1)S(1)} %add_convert_fusion.4), channel_id=1, source_target_pairs={{0,4},{1,5},{2,6},{3,7},{4,0},{5,1},{6,2},{7,3},{8,12},{9,13},{10,... | collective-permute-start | bytes 393224 | tf_op jit(solution)/shard_map/ppermute | solution.py:464
  57.8 1.4 collective-permute-start.7
  58.4 14.4 %copy-start.2 = (bf16[128,8192]{1,0:T(8,128)(2,1)S(1)}, bf16[128,8192]{1,0:T(8,128)(2,1)}, u32[]{:S(2)}) copy-start(bf16[128,8192]{1,0:T(8,128)(2,1)} %factor.2) | copy-start | bytes 6291460
  58.4 14.3 %copy-start.4 = (bf16[128,4096]{1,0:T(8,128)(2,1)S(1)}, bf16[128,4096]{1,0:T(8,128)(2,1)}, u32[]{:S(2)}) copy-start(bf16[128,4096]{1,0:T(8,128)(2,1)} %factor.3) | copy-start | bytes 3145732
  58.4 14.3 %copy-start.8 = (s32[4,32]{1,0:T(4,128)S(1)}, s32[4,32]{1,0:T(4,128)}, u32[]{:S(2)}) copy-start(s32[4,32]{1,0:T(4,128)} %pattern.4) | copy-start | bytes 1540
  58.4 14.3 %copy-start.10 = (s32[2,64]{1,0:T(2,128)S(1)}, s32[2,64]{1,0:T(2,128)}, u32[]{:S(2)}) copy-start(s32[2,64]{1,0:T(2,128)} %pattern.3) | copy-start | bytes 1540
  75.2 3.4 %collective-permute-start.8 = (bf16[64,64,128]{2,1,0:T(8,128)(2,1)S(1)}, bf16[64,64,128]{2,1,0:T(8,128)(2,1)S(1)}, u32[]{:S(2)}, u32[]{:S(2)}) collective-permute-start(bf16[64,64,128]{2,1,0:T(8,128)(2,1)S(1)} %get-tuple-element.309), channel_id=1, source_target_pairs={{0,1},{1,0},{2,3},{3,2},{4,5},{5,4},{6,7},{7,6},{8,9},{9,8},{10,11... | collective-permute-start | bytes 3145736 | tf_op jit(solution)/shard_map/ppermute | solution.py:458
  76.3 27.0 %collective-permute-start.9 = (bf16[128,4096]{1,0:T(8,128)(2,1)S(1)}, bf16[128,4096]{1,0:T(8,128)(2,1)S(1)}, u32[]{:S(2)}, u32[]{:S(2)}) collective-permute-start(bf16[128,4096]{1,0:T(8,128)(2,1)S(1)} %copy-done.3), channel_id=1, source_target_pairs={{0,2},{1,7},{2,0},{3,5},{4,6},{5,3},{6,4},{7,1},{8,10},{9,15},{10,... | collective-permute-start | bytes 3145736 | tf_op jit(solution)/shard_map/ppermute | solution.py:461
  79.0 34.8 %copy-start = (bf16[1,1,2048,1024]{3,2,1,0:T(8,128)(2,1)S(1)}, bf16[1,1,2048,1024]{3,2,1,0:T(8,128)(2,1)}, u32[]{:S(2)}) copy-start(bf16[1,1,2048,1024]{3,2,1,0:T(8,128)(2,1)} %param.12) | copy-start | bytes 12582916
  113.1 34.0 %collective-permute-start.12 = (bf16[1024,1024]{1,0:T(8,128)(2,1)S(1)}, bf16[1024,1024]{1,0:T(8,128)(2,1)S(1)}, u32[]{:S(2)}, u32[]{:S(2)}) collective-permute-start(bf16[1024,1024]{1,0:T(8,128)(2,1)S(1)} %bitcast.23), channel_id=1, source_target_pairs={{0,2},{1,7},{2,0},{3,5},{4,6},{5,3},{6,4},{7,1},{8,10},{9,15},{10,... | collective-permute-start | bytes 6291464 | tf_op jit(solution)/shard_map/ppermute | solution.py:461
  113.7 1.4 collective-permute-start.10
  145.7 1.4 collective-permute-start.11
  176.6 2.7 %collective-permute-start.13 = (bf16[64,64,128]{2,1,0:T(8,128)(2,1)S(1)}, bf16[64,64,128]{2,1,0:T(8,128)(2,1)S(1)}, u32[]{:S(2)}, u32[]{:S(2)}) collective-permute-start(bf16[64,64,128]{2,1,0:T(8,128)(2,1)S(1)} %bitcast.25), channel_id=1, source_target_pairs={{0,1},{1,0},{2,3},{3,2},{4,5},{5,4},{6,7},{7,6},{8,9},{9,8},{10,11... | collective-permute-start | bytes 3145736 | tf_op jit(solution)/shard_map/ppermute | solution.py:458
  192.8 1.3 collective-permute-start.14
  194.1 5.8 %collective-permute-start.15 = (bf16[4,64,128]{2,1,0:T(8,128)(2,1)S(1)}, bf16[4,64,128]{2,1,0:T(8,128)(2,1)S(1)}, u32[]{:S(2)}, u32[]{:S(2)}) collective-permute-start(bf16[4,64,128]{2,1,0:T(8,128)(2,1)S(1)} %add_convert_fusion.5.mine), channel_id=1, source_target_pairs={{0,4},{1,5},{2,6},{3,7},{4,0},{5,1},{6,2},{7,3},{8,12},{9,13},{10,... | collective-permute-start | bytes 196616 | tf_op jit(solution)/shard_map/ppermute | solution.py:464
  212.0 13.3 %copy-start.6 = (bf16[1,1,512,1024]{3,2,1,0:T(8,128)(2,1)S(1)}, bf16[1,1,512,1024]{3,2,1,0:T(8,128)(2,1)}, u32[]{:S(2)}) copy-start(bf16[1,1,512,1024]{3,2,1,0:T(8,128)(2,1)} %param.14) | copy-start | bytes 3145732
  212.0 1.9 collective-permute-start.16
  212.0 4.2 %collective-permute-start.17 = (bf16[3,64,128]{2,1,0:T(8,128)(2,1)S(1)}, bf16[3,64,128]{2,1,0:T(8,128)(2,1)S(1)}, u32[]{:S(2)}, u32[]{:S(2)}) collective-permute-start(bf16[3,64,128]{2,1,0:T(8,128)(2,1)S(1)} %pad_maximum_fusion), channel_id=1, source_target_pairs={{0,2},{1,7},{2,0},{3,5},{4,6},{5,3},{6,4},{7,1},{8,10},{9,15},{10,... | collective-permute-start | bytes 147464 | tf_op jit(solution)/shard_map/ppermute | solution.py:461
  225.6 1.8 collective-permute-start.18

commit v8 on v7

--- a/solution.py
+++ b/solution.py
@@ -47,7 +47,7 @@
     return lambda *refs: kernel(refs[:count], *refs[count:])
 
 
-def call(kernel, name, out_shape, smem, vmem, scratch=(), limit=24, cost=None, smem_spec=SMEM):
+def call(kernel, name, out_shape, smem, vmem, scratch=(), limit=14, cost=None, smem_spec=SMEM):
     return pl.pallas_call(
         kernel,
         out_shape=out_shape,

time: 237 us -> 238 us (level)
  no operation moved by 1% of the time
where the time goes in v8:
time: 238 us; the launch traced here: 237 us
  blocking collectives  171 us (72%)
  waiting for transfers between devices  28.3 us (12%)
  Pallas kernels  16.7 us (7%)
  starting transfers between devices  16.5 us (7%)
  local copies, waits for them, and re-layouts  2.79 us (1%)
    all_to_all x13, blocking collectives, exchange(): lax.all_to_all(value, axis, 0, 0, tiled=True, axis_index_groups=groups)  171 us
    pallas_call x22, Pallas kernels, call(): pl.pallas_call(kernel, out_shape=out_shape, in_specs=[smem_spec] * len(sm...  16.7 us
    ppermute x10, waiting for transfers between devices, swap_core(): return lax.ppermute(value, 'blk', [(i, i ^ 1) for i in range(block_count)])  12.8 us
    ppermute x2, waiting for transfers between devices, swap_far(): return lax.ppermute(value, 'blk', [(i, i ^ 4) for i in range(block_count)])  7.6 us
    ppermute x6, waiting for transfers between devices, swap_near(): lax.ppermute(value, 'blk', [(i, near_of(i)) for i in range(block_count)])  5.37 us
  transfers between devices with their start and end apart: 20, of which 15 were waited for; matrix products, arithmetic and copies ran while one was open for 0% of the time, Pallas kernels for 4%

profile of v8, /device:TPU:0, one launch (start us, length us, event | category | flops | bytes accessed | tf_op | source)
XLA Modules:
  0.0 236.8 jit_solution(133541785395999641)
XLA Ops:
  2.1 4.4 %all-to-all-start = ((bf16[4,128,128]{2,1,0:T(8,128)(2,1)}), bf16[4,128,128]{2,1,0:T(8,128)(2,1)S(1)}, u32[]{:S(2)}, u32[]{:S(2)}) async-start(bf16[4,128,128]{2,1,0:T(8,128)(2,1)} %broadcast_in_dim.9), calls=%async_computation | async-start | bytes 262144 | tf_op jit(solution)/shard_map/all_to_all | solution.py:494
  6.5 2.0 collective-permute-start.1
  8.5 1.6 collective-permute-start.2
  10.1 2.5 %all-to-all-done.own = bf16[4,128,128]{2,1,0:T(8,128)(2,1)S(1)} async-done(((bf16[4,128,128]{2,1,0:T(8,128)(2,1)}), bf16[4,128,128]{2,1,0:T(8,128)(2,1)S(1)}, u32[]{:S(2)}, u32[]{:S(2)}) %all-to-all-start) | async-done | bytes 131104 | tf_op jit(solution)/shard_map/all_to_all | solution.py:494
  13.9 1.2 copy-done.5
  15.7 12.4 %all_to_all.70.refs_2_ = bf16[4,192,128]{2,1,0:T(8,128)(2,1)S(1)} all-to-all(bf16[4,192,128]{2,1,0:T(8,128)(2,1)S(1)} %multiply.1), channel_id=1, replica_groups={{0,8,16,24},{32,40,48,56},{64,72,80,88},{96,104,112,120},{1,9,17,25},{3..., dimensions={0} | all-to-all | bytes 393216 | tf_op jit(solution)/shard_map/all_to_all | solution.py:494
  29.5 1.9 collective-permute-done.3
  31.6 13.6 %all_to_all.71.parts = bf16[8,4,64,128]{3,2,1,0:T(8,128)(2,1)S(1)} all-to-all(bf16[8,4,64,128]{3,2,1,0:T(8,128)(2,1)S(1)} %bitcast.43), channel_id=1, replica_groups={{0,8,16,24,32,40,48,56},{64,72,80,88,96,104,112,120},{1,9,17,25,33,41,4..., dimensions={0} | all-to-all | bytes 1048576 | tf_op jit(solution)/shard_map/all_to_all | solution.py:494
  46.0 4.7 %collective-permute-done.5 = bf16[640,128]{1,0:T(8,128)(2,1)S(1)} collective-permute-done((bf16[640,128]{1,0:T(8,128)(2,1)S(1)}, bf16[640,128]{1,0:T(8,128)(2,1)S(1)}, u32[]{:S(2)}, u32[]{:S(2)}) %collective-permute-start.5) | collective-permute-done | bytes 163872 | tf_op jit(solution)/shard_map/ppermute | solution.py:461
  50.8 2.7 %collective-permute-start.6 = (bf16[512,128]{1,0:T(8,128)(2,1)S(1)}, bf16[512,128]{1,0:T(8,128)(2,1)S(1)}, u32[]{:S(2)}, u32[]{:S(2)}) collective-permute-start(bf16[512,128]{1,0:T(8,128)(2,1)S(1)} %add_convert_fusion.4), channel_id=1, source_target_pairs={{0,4},{1,5},{2,6},{3,7},{4,0},{5,1},{6,2},{7,3},{8,12},{9,13},{10,... | collective-permute-start | bytes 393224 | tf_op jit(solution)/shard_map/ppermute | solution.py:464
  53.4 4.3 %collective-permute-done.6 = bf16[512,128]{1,0:T(8,128)(2,1)S(1)} collective-permute-done((bf16[512,128]{1,0:T(8,128)(2,1)S(1)}, bf16[512,128]{1,0:T(8,128)(2,1)S(1)}, u32[]{:S(2)}, u32[]{:S(2)}) %collective-permute-start.6) | collective-permute-done | bytes 131104 | tf_op jit(solution)/shard_map/ppermute | solution.py:464
  59.8 13.0 %all_to_all.72 = bf16[16,64,128]{2,1,0:T(8,128)(2,1)S(1)} all-to-all(bf16[16,64,128]{2,1,0:T(8,128)(2,1)S(1)} %bitcast.30), channel_id=1, replica_groups={{0,2,8,10,16,18,24,26,32,34,40,42,48,50,56,58},{1,7,9,15,17,23,25,31,33..., dimensions={0} | all-to-all | bytes 524288 | tf_op jit(solution)/shard_map/all_to_all | solution.py:494
  72.8 2.5 %lift_pair.1 = (bf16[2,64,128]{2,1,0:T(8,128)(2,1)S(1)}, bf16[64,64,128]{2,1,0:T(8,128)(2,1)S(1)}, bf16[64,64,128]{2,1,0:T(8,128)(2,1)S(1)}) custom-call(s32[7]{0:T(128)S(1)} %copy-done.11, s32[2,64]{1,0:T(2,128)S(1)} %copy-done.10, s32[4,32]{1,0:T(4,128)S(1)} %copy-done.8, bf16[8,2,64,128]{3,2,1,0:T(8,128)(2,1)S(1)} %bitcast.33, ...), custom_call_target="tpu_custom_call" | custom-call | tf_op jit(solution)/shard_map/lift_pair/pallas_call | solution.py:51
  76.5 2.2 collective-permute-done.8
  79.1 24.1 %all_to_all.73.parts = bf16[16,4,64,128]{3,2,1,0:T(8,128)(2,1)S(1)} all-to-all(bf16[16,4,64,128]{3,2,1,0:T(8,128)(2,1)S(1)} %bitcast.42), channel_id=1, replica_groups=mesh['leaf'=16,'blk'=8] {'leaf'}, dimensions={0} | all-to-all | bytes 2097152 | tf_op jit(solution)/shard_map/all_to_all | solution.py:494
  103.3 9.8 %all_to_all.74.parts = bf16[4,4,64,128]{3,2,1,0:T(8,128)(2,1)S(1)} all-to-all(bf16[4,4,64,128]{3,2,1,0:T(8,128)(2,1)S(1)} %rest.3), channel_id=1, replica_groups={{0,2,4,6},{1,3,5,7},{8,10,12,14},{9,11,13,15},{16,18,20,22},{17,19,21,2..., dimensions={0} | all-to-all | bytes 524288 | tf_op jit(solution)/shard_map/all_to_all | solution.py:494
  116.1 14.8 %all_to_all.75.parts = bf16[16,128,128]{2,1,0:T(8,128)(2,1)S(1)} all-to-all(bf16[16,128,128]{2,1,0:T(8,128)(2,1)S(1)} %multiply_rest.3), channel_id=1, replica_groups=mesh['leaf'=16,'blk'=8] {'leaf'}, dimensions={0} | all-to-all | bytes 1048576 | tf_op jit(solution)/shard_map/all_to_all | solution.py:494
  131.0 14.0 %all_to_all.76.gathered = bf16[16,128,128]{2,1,0:T(8,128)(2,1)S(1)} all-to-all(bf16[16,128,128]{2,1,0:T(8,128)(2,1)S(1)} %get-tuple-element.363), channel_id=1, replica_groups=mesh['leaf'=16,'blk'=8] {'leaf'}, dimensions={0} | all-to-all | bytes 1048576 | tf_op jit(solution)/shard_map/all_to_all | solution.py:494
  145.8 1.3 collective-permute-done.11.theirs
  147.2 10.1 %all_to_all.77.parts = bf16[4,4,64,128]{3,2,1,0:T(8,128)(2,1)S(1)} all-to-all(bf16[4,4,64,128]{3,2,1,0:T(8,128)(2,1)S(1)} %split.1), channel_id=1, replica_groups={{0,2,4,6},{1,3,5,7},{8,10,12,14},{9,11,13,15},{16,18,20,22},{17,19,21,2..., dimensions={0} | all-to-all | bytes 524288 | tf_op jit(solution)/shard_map/all_to_all | solution.py:494
  157.4 19.2 %all_to_all.78 = bf16[16,4,64,128]{3,2,1,0:T(8,128)(2,1)S(1)} all-to-all(bf16[16,4,64,128]{3,2,1,0:T(8,128)(2,1)S(1)} %get-tuple-element.403), channel_id=1, replica_groups=mesh['leaf'=16,'blk'=8] {'leaf'}, dimensions={0} | all-to-all | bytes 2097152 | tf_op jit(solution)/shard_map/all_to_all | solution.py:494
  176.6 2.7 %collective-permute-done.13.other = bf16[64,64,128]{2,1,0:T(8,128)(2,1)S(1)} collective-permute-done((bf16[64,64,128]{2,1,0:T(8,128)(2,1)S(1)}, bf16[64,64,128]{2,1,0:T(8,128)(2,1)S(1)}, u32[]{:S(2)}, u32[]{:S(2)}) %collective-permute-start.13) | collective-permute-done | bytes 1048608 | tf_op jit(solution)/shard_map/ppermute | solution.py:458
  179.3 2.4 %reduced.2 = bf16[8,2,64,128]{3,2,1,0:T(8,128)(2,1)S(1)} custom-call(s32[2,64]{1,0:T(2,128)S(1)} %copy-done.10, bf16[64,64,128]{2,1,0:T(8,128)(2,1)S(1)} %bitcast.26, bf16[64,64,128]{2,1,0:T(8,128)(2,1)S(1)} %collective-permute-done.13.other, bf16[128,8192]{1,0:T(8,128)(2,1)S(1)} %copy-done.2, bf16[128,8192]{1,0:T(8,128)(2,1)S(1)} %collective-permute-done.4.refs_7_.near, ...), custom_call_target="tpu_custom_call" | custom-call | tf_op jit(solution)/shard_map/reduced/pallas_call | solution.py:51
  181.7 10.3 %all_to_all.79.gathered = bf16[8,2,64,128]{3,2,1,0:T(8,128)(2,1)S(1)} all-to-all(bf16[8,2,64,128]{3,2,1,0:T(8,128)(2,1)S(1)} %reduced.2), channel_id=1, replica_groups={{0,8,16,24,32,40,48,56},{64,72,80,88,96,104,112,120},{1,9,17,25,33,41,4..., dimensions={0} | all-to-all | bytes 524288 | tf_op jit(solution)/shard_map/all_to_all | solution.py:494
  192.9 1.2 collective-permute-done.14
  195.1 1.6 pull.1.refs_0_
  196.7 3.3 %collective-permute-done.15.far = bf16[4,64,128]{2,1,0:T(8,128)(2,1)S(1)} collective-permute-done((bf16[4,64,128]{2,1,0:T(8,128)(2,1)S(1)}, bf16[4,64,128]{2,1,0:T(8,128)(2,1)S(1)}, u32[]{:S(2)}, u32[]{:S(2)}) %collective-permute-start.15) | collective-permute-done | bytes 65568 | tf_op jit(solution)/shard_map/ppermute | solution.py:464
  200.1 12.0 %all_to_all.80 = bf16[8,4,64,128]{3,2,1,0:T(8,128)(2,1)S(1)} all-to-all(bf16[8,4,64,128]{3,2,1,0:T(8,128)(2,1)S(1)} %get-tuple-element.460), channel_id=1, replica_groups={{0,8,16,24,32,40,48,56},{64,72,80,88,96,104,112,120},{1,9,17,25,33,41,4..., dimensions={0} | all-to-all | bytes 1048576 | tf_op jit(solution)/shard_map/all_to_all | solution.py:494
  212.7 1.2 collective-permute-done.16.other
  214.0 1.6 reduced.3
  216.3 9.1 %all_to_all.81 = bf16[8,64,128]{2,1,0:T(8,128)(2,1)S(1)} all-to-all(bf16[8,64,128]{2,1,0:T(8,128)(2,1)S(1)} %bitcast.34), channel_id=1, replica_groups={{0,2,8,10,16,18,24,26},{1,7,9,15,17,23,25,31},{4,6,12,14,20,22,28,30},{..., dimensions={0} | all-to-all | bytes 262144 | tf_op jit(solution)/shard_map/all_to_all | solution.py:494
  227.5 8.5 %all_to_all.82.parts = bf16[4,128,128]{2,1,0:T(8,128)(2,1)S(1)} all-to-all(bf16[4,128,128]{2,1,0:T(8,128)(2,1)S(1)} %add_convert_fusion.2), channel_id=1, replica_groups={{0,2,4,6},{1,3,5,7},{8,10,12,14},{9,11,13,15},{16,18,20,22},{17,19,21,2..., dimensions={0} | all-to-all | bytes 262144 | tf_op jit(solution)/shard_map/all_to_all | solution.py:494
  (79 shorter events, 19.6 us)
Async XLA Ops:
  2.1 10.5 %all-to-all-start = ((bf16[4,128,128]{2,1,0:T(8,128)(2,1)}), bf16[4,128,128]{2,1,0:T(8,128)(2,1)S(1)}, u32[]{:S(2)}, u32[]{:S(2)}) async-start(bf16[4,128,128]{2,1,0:T(8,128)(2,1)} %broadcast_in_dim.9), calls=%async_computation | async-start | bytes 262144 | tf_op jit(solution)/shard_map/all_to_all | solution.py:494
  6.5 21.6 %collective-permute-start.1 = (bf16[128,4096]{1,0:T(8,128)(2,1)}, bf16[128,4096]{1,0:T(8,128)(2,1)S(1)}, u32[]{:S(2)}, u32[]{:S(2)}) collective-permute-start(bf16[128,4096]{1,0:T(8,128)(2,1)} %factor.3), channel_id=1, source_target_pairs={{0,2},{1,7},{2,0},{3,5},{4,6},{5,3},{6,4},{7,1},{8,10},{9,15},{10,... | collective-permute-start | bytes 3145736 | tf_op jit(solution)/shard_map/ppermute | solution.py:461
  8.5 19.6 %collective-permute-start.2 = (bf16[128,4096]{1,0:T(8,128)(2,1)}, bf16[128,4096]{1,0:T(8,128)(2,1)S(1)}, u32[]{:S(2)}, u32[]{:S(2)}) collective-permute-start(bf16[128,4096]{1,0:T(8,128)(2,1)} %factor.4), channel_id=1, source_target_pairs={{0,8},{1,25},{2,10},{3,27},{4,12},{5,29},{6,14},{7,31},{8,0},{9,17... | collective-permute-start | bytes 3145736 | tf_op jit(solution)/shard_map/ppermute | solution.py:483
  12.6 1.3 collective-permute-start
  12.6 32.7 %collective-permute-start.4 = (bf16[128,8192]{1,0:T(8,128)(2,1)}, bf16[128,8192]{1,0:T(8,128)(2,1)S(1)}, u32[]{:S(2)}, u32[]{:S(2)}) collective-permute-start(bf16[128,8192]{1,0:T(8,128)(2,1)} %factor.2), channel_id=1, source_target_pairs={{0,2},{1,7},{2,0},{3,5},{4,6},{5,3},{6,4},{7,1},{8,10},{9,15},{10,... | collective-permute-start | bytes 6291464 | tf_op jit(solution)/shard_map/ppermute | solution.py:461
  13.9 1.2 copy-start.5
  15.2 12.9 %copy-start.3 = (bf16[128,4096]{1,0:T(8,128)(2,1)S(1)}, bf16[128,4096]{1,0:T(8,128)(2,1)}, u32[]{:S(2)}) copy-start(bf16[128,4096]{1,0:T(8,128)(2,1)} %factor.4) | copy-start | bytes 3145732
  15.2 13.0 %copy-start.9 = (s32[4,32]{1,0:T(4,128)S(1)}, s32[4,32]{1,0:T(4,128)}, u32[]{:S(2)}) copy-start(s32[4,32]{1,0:T(4,128)} %pattern.5) | copy-start | bytes 1540
  15.2 13.0 %copy-start.11 = (s32[7]{0:T(128)S(1)}, s32[7]{0:T(128)}, u32[]{:S(2)}) copy-start(s32[7]{0:T(128)} %refs_0_.3) | copy-start | bytes 88
  28.1 17.1 %copy-start.7 = (f32[3,128,128]{2,1,0:T(8,128)S(1)}, f32[3,128,128]{2,1,0:T(8,128)}, u32[]{:S(2)}) copy-start(f32[3,128,128]{2,1,0:T(8,128)} %loads.1) | copy-start | bytes 589828
  29.4 2.0 collective-permute-start.3
  31.4 26.5 %copy-start.1 = (bf16[1,1,1024,1024]{3,2,1,0:T(8,128)(2,1)S(1)}, bf16[1,1,1024,1024]{3,2,1,0:T(8,128)(2,1)}, u32[]{:S(2)}) copy-start(bf16[1,1,1024,1024]{3,2,1,0:T(8,128)(2,1)} %param.13) | copy-start | bytes 6291460
  45.3 5.4 %collective-permute-start.5 = (bf16[640,128]{1,0:T(8,128)(2,1)S(1)}, bf16[640,128]{1,0:T(8,128)(2,1)S(1)}, u32[]{:S(2)}, u32[]{:S(2)}) collective-permute-start(bf16[640,128]{1,0:T(8,128)(2,1)S(1)} %get-tuple-element.285), channel_id=1, source_target_pairs={{0,2},{1,7},{2,0},{3,5},{4,6},{5,3},{6,4},{7,1},{8,10},{9,15},{10,... | collective-permute-start | bytes 491528 | tf_op jit(solution)/shard_map/ppermute | solution.py:461
  50.8 7.0 %collective-permute-start.6 = (bf16[512,128]{1,0:T(8,128)(2,1)S(1)}, bf16[512,128]{1,0:T(8,128)(2,1)S(1)}, u32[]{:S(2)}, u32[]{:S(2)}) collective-permute-start(bf16[512,128]{1,0:T(8,128)(2,1)S(1)} %add_convert_fusion.4), channel_id=1, source_target_pairs={{0,4},{1,5},{2,6},{3,7},{4,0},{5,1},{6,2},{7,3},{8,12},{9,13},{10,... | collective-permute-start | bytes 393224 | tf_op jit(solution)/shard_map/ppermute | solution.py:464
  57.8 1.4 collective-permute-start.7
  58.4 14.4 %copy-start.2 = (bf16[128,8192]{1,0:T(8,128)(2,1)S(1)}, bf16[128,8192]{1,0:T(8,128)(2,1)}, u32[]{:S(2)}) copy-start(bf16[128,8192]{1,0:T(8,128)(2,1)} %factor.2) | copy-start | bytes 6291460
  58.4 14.3 %copy-start.4 = (bf16[128,4096]{1,0:T(8,128)(2,1)S(1)}, bf16[128,4096]{1,0:T(8,128)(2,1)}, u32[]{:S(2)}) copy-start(bf16[128,4096]{1,0:T(8,128)(2,1)} %factor.3) | copy-start | bytes 3145732
  58.4 14.3 %copy-start.8 = (s32[4,32]{1,0:T(4,128)S(1)}, s32[4,32]{1,0:T(4,128)}, u32[]{:S(2)}) copy-start(s32[4,32]{1,0:T(4,128)} %pattern.4) | copy-start | bytes 1540
  58.4 14.3 %copy-start.10 = (s32[2,64]{1,0:T(2,128)S(1)}, s32[2,64]{1,0:T(2,128)}, u32[]{:S(2)}) copy-start(s32[2,64]{1,0:T(2,128)} %pattern.3) | copy-start | bytes 1540
  75.2 3.4 %collective-permute-start.8 = (bf16[64,64,128]{2,1,0:T(8,128)(2,1)S(1)}, bf16[64,64,128]{2,1,0:T(8,128)(2,1)S(1)}, u32[]{:S(2)}, u32[]{:S(2)}) collective-permute-start(bf16[64,64,128]{2,1,0:T(8,128)(2,1)S(1)} %get-tuple-element.309), channel_id=1, source_target_pairs={{0,1},{1,0},{2,3},{3,2},{4,5},{5,4},{6,7},{7,6},{8,9},{9,8},{10,11... | collective-permute-start | bytes 3145736 | tf_op jit(solution)/shard_map/ppermute | solution.py:458
  76.4 26.9 %collective-permute-start.9 = (bf16[128,4096]{1,0:T(8,128)(2,1)S(1)}, bf16[128,4096]{1,0:T(8,128)(2,1)S(1)}, u32[]{:S(2)}, u32[]{:S(2)}) collective-permute-start(bf16[128,4096]{1,0:T(8,128)(2,1)S(1)} %copy-done.3), channel_id=1, source_target_pairs={{0,2},{1,7},{2,0},{3,5},{4,6},{5,3},{6,4},{7,1},{8,10},{9,15},{10,... | collective-permute-start | bytes 3145736 | tf_op jit(solution)/shard_map/ppermute | solution.py:461
  79.1 34.8 %copy-start = (bf16[1,1,2048,1024]{3,2,1,0:T(8,128)(2,1)S(1)}, bf16[1,1,2048,1024]{3,2,1,0:T(8,128)(2,1)}, u32[]{:S(2)}) copy-start(bf16[1,1,2048,1024]{3,2,1,0:T(8,128)(2,1)} %param.12) | copy-start | bytes 12582916
  113.1 34.0 %collective-permute-start.12 = (bf16[1024,1024]{1,0:T(8,128)(2,1)S(1)}, bf16[1024,1024]{1,0:T(8,128)(2,1)S(1)}, u32[]{:S(2)}, u32[]{:S(2)}) collective-permute-start(bf16[1024,1024]{1,0:T(8,128)(2,1)S(1)} %bitcast.23), channel_id=1, source_target_pairs={{0,2},{1,7},{2,0},{3,5},{4,6},{5,3},{6,4},{7,1},{8,10},{9,15},{10,... | collective-permute-start | bytes 6291464 | tf_op jit(solution)/shard_map/ppermute | solution.py:461
  113.7 1.4 collective-permute-start.10
  145.7 1.4 collective-permute-start.11
  176.6 2.7 %collective-permute-start.13 = (bf16[64,64,128]{2,1,0:T(8,128)(2,1)S(1)}, bf16[64,64,128]{2,1,0:T(8,128)(2,1)S(1)}, u32[]{:S(2)}, u32[]{:S(2)}) collective-permute-start(bf16[64,64,128]{2,1,0:T(8,128)(2,1)S(1)} %bitcast.25), channel_id=1, source_target_pairs={{0,1},{1,0},{2,3},{3,2},{4,5},{5,4},{6,7},{7,6},{8,9},{9,8},{10,11... | collective-permute-start | bytes 3145736 | tf_op jit(solution)/shard_map/ppermute | solution.py:458
  192.9 1.3 collective-permute-start.14
  194.2 5.8 %collective-permute-start.15 = (bf16[4,64,128]{2,1,0:T(8,128)(2,1)S(1)}, bf16[4,64,128]{2,1,0:T(8,128)(2,1)S(1)}, u32[]{:S(2)}, u32[]{:S(2)}) collective-permute-start(bf16[4,64,128]{2,1,0:T(8,128)(2,1)S(1)} %add_convert_fusion.5.mine), channel_id=1, source_target_pairs={{0,4},{1,5},{2,6},{3,7},{4,0},{5,1},{6,2},{7,3},{8,12},{9,13},{10,... | collective-permute-start | bytes 196616 | tf_op jit(solution)/shard_map/ppermute | solution.py:464
  212.1 13.3 %copy-start.6 = (bf16[1,1,512,1024]{3,2,1,0:T(8,128)(2,1)S(1)}, bf16[1,1,512,1024]{3,2,1,0:T(8,128)(2,1)}, u32[]{:S(2)}) copy-start(bf16[1,1,512,1024]{3,2,1,0:T(8,128)(2,1)} %param.14) | copy-start | bytes 3145732
  212.1 1.9 collective-permute-start.16
  212.1 4.2 %collective-permute-start.17 = (bf16[3,64,128]{2,1,0:T(8,128)(2,1)S(1)}, bf16[3,64,128]{2,1,0:T(8,128)(2,1)S(1)}, u32[]{:S(2)}, u32[]{:S(2)}) collective-permute-start(bf16[3,64,128]{2,1,0:T(8,128)(2,1)S(1)} %pad_maximum_fusion), channel_id=1, source_target_pairs={{0,2},{1,7},{2,0},{3,5},{4,6},{5,3},{6,4},{7,1},{8,10},{9,15},{10,... | collective-permute-start | bytes 147464 | tf_op jit(solution)/shard_map/ppermute | solution.py:461
  225.7 1.8 collective-permute-start.18
